TPU v7x, 32 devices: a whole 2x2x4 slice. The times are simulated.
32 devices in a mesh: dp: 4 (over x, core), ctx: 8 (over z, y).
Axes of the slice: x: 2, y: 2, z: 4, core: 2. Of those that a mesh axis runs over, the one named last changes fastest.
Arguments:
- tokens: bfloat16 [8, 1024, 2048], P('dp', 'ctx'), may hold values from -6 to 6
- cotangent: bfloat16 [8, 1024, 2048], P('dp', 'ctx'), may hold values from -6 to 6
- counts: int32 [4], P('dp'), may hold values from 1 to 2, as said below
- query_weight: bfloat16 [2048, 2048], P('dp', 'ctx'), may hold values from -0.125 to 0.125
- key_weight: bfloat16 [2048, 2048], P('dp', 'ctx'), may hold values from -0.125 to 0.125
- value_weight: bfloat16 [2048, 2048], P('dp', 'ctx'), may hold values from -0.125 to 0.125
- output_weight: bfloat16 [2048, 2048], P('dp', 'ctx'), may hold values from -1.5 to 1.5
- gate_weight: bfloat16 [2048, 8192], P('dp', 'ctx'), may hold values from -0.125 to 0.125
- up_weight: bfloat16 [2048, 8192], P('dp', 'ctx'), may hold values from -0.125 to 0.125
- down_weight: bfloat16 [8192, 2048], P('dp', 'ctx'), may hold values from -0.0625 to 0.0625
Outputs:
- mixed: bfloat16 [8, 1024, 2048], P('dp', 'ctx')
- token_grad: float32 [8, 1024, 2048], P('dp', 'ctx')
- grad_query_weight: float32 [2048, 2048], P('dp', 'ctx')
- grad_key_weight: float32 [2048, 2048], P('dp', 'ctx')
- grad_value_weight: float32 [2048, 2048], P('dp', 'ctx')
- grad_output_weight: float32 [2048, 2048], P('dp', 'ctx')
- grad_gate_weight: float32 [2048, 8192], P('dp', 'ctx')
- grad_up_weight: float32 [2048, 8192], P('dp', 'ctx')
- grad_down_weight: float32 [8192, 2048], P('dp', 'ctx')
Inputs may be any that keep to these rules, and one draw needn't show every extreme that they name: Group g holds sequences in its slots 0 to counts[g] - 1; some group holds 2 and some group holds 1.
All inputs are finite; a program needn't handle non-finite values.
Results may differ from a plain program's by a relative error of at most 0.02.
Values may be sent and summed in bfloat16 or wider, within the bound.
No kernel may reach another device: no remote copies, remote signals or barrier semaphores. Data moves between devices by JAX's collectives and lax.ppermute only.
A program may use at most 704 MiB of HBM per device.

v0:
```python
import jax
import jax.numpy as jnp
from jax import lax
from jax.sharding import PartitionSpec as P

HEADS = 16
HEAD_DIM = 128
FF = 8192


epsilon = 1e-05
rope_base = 10000.0


def layer_norm(values):
    centred = values - jnp.mean(values, axis=-1, keepdims=True)
    variance = jnp.mean(centred * centred, axis=-1, keepdims=True)
    return centred * lax.rsqrt(variance + epsilon)


def paired_positions(row_index, tok_rows, blocks):
    half_block = tok_rows // 2
    device = row_index // tok_rows
    offset = row_index % tok_rows
    return jnp.where(
        offset < half_block,
        device * half_block + offset,
        (2 * blocks - 1 - device) * half_block + offset - half_block,
    )


def rope_tables(positions):
    half_dim = HEAD_DIM // 2
    frequency = rope_base ** (-jnp.arange(half_dim, dtype=jnp.float32) / half_dim)
    angles = positions.astype(jnp.float32)[:, None] * frequency[None, :]
    return (jnp.cos(angles)[:, None, :], jnp.sin(angles)[:, None, :])


def rotate(values, cosine_table, sine_table):
    half_dim = values.shape[-1] // 2
    first_half = values[..., :half_dim]
    second_half = values[..., half_dim:]
    return jnp.concatenate(
        [
            first_half * cosine_table - second_half * sine_table,
            second_half * cosine_table + first_half * sine_table,
        ],
        axis=-1,
    )


def outer_sum(left, right):
    return lax.dot_general(
        left, right, (((0,), (0,)), ((), ())), preferred_element_type=jnp.float32
    )


def back_product(grad_rows, weight):
    return lax.dot_general(
        grad_rows, weight, (((1,), (1,)), ((), ())), preferred_element_type=jnp.float32
    )


def block_start(block, tile_span, blocks):
    upper_side = (block >= blocks // tile_span).astype(jnp.int32)
    lead_tile = jnp.where(
        upper_side == 0, block * tile_span, 2 * blocks - (block + 1) * tile_span
    ).astype(jnp.int32)
    return (lead_tile, upper_side)


def tile_starts(tiles, lead_tile, upper_side):
    zero_index = jnp.zeros((), jnp.int32)
    return (lead_tile, upper_side) + (zero_index,) * (tiles.ndim - 2)


def take_block(tiles, lead_tile, upper_side, tile_span):
    piece = lax.dynamic_slice(
        tiles, tile_starts(tiles, lead_tile, upper_side), (tile_span, 1) + tiles.shape[2:]
    )
    return piece.reshape((tile_span * tiles.shape[2],) + tiles.shape[3:])


def add_block(tiles, part, lead_tile, upper_side, tile_span):
    starts = tile_starts(tiles, lead_tile, upper_side)
    piece_shape = (tile_span, 1) + tiles.shape[2:]
    before = lax.dynamic_slice(tiles, starts, piece_shape)
    return lax.dynamic_update_slice(tiles, before + part.reshape(piece_shape), starts)


def block_scores(query_half, query_pos, key_block, key_pos):
    scores = jnp.einsum(
        "qhd,khd->hqk", query_half, key_block, preferred_element_type=jnp.float32
    ) * HEAD_DIM ** (-0.5)
    allowed = query_pos[:, None] >= key_pos[None, :]
    return jnp.where(allowed[None, :, :], scores, -1e30)


def attend_half(query_half, query_pos, tables, needed, tile_span, blocks):
    key_tiles, value_tiles, pos_tiles = tables
    row_count = query_half.shape[0]

    def scores_at(block):
        lead_tile, upper_side = block_start(block, tile_span, blocks)
        key_block = take_block(key_tiles, lead_tile, upper_side, tile_span)
        key_pos = take_block(pos_tiles, lead_tile, upper_side, tile_span)
        return (block_scores(query_half, query_pos, key_block, key_pos), lead_tile, upper_side)

    def total_step(block, carried):
        highest, total_mass = carried
        scores = scores_at(block)[0]
        new_highest = jnp.maximum(highest, jnp.max(scores, axis=-1))
        total_mass = total_mass * jnp.exp(highest - new_highest) + jnp.sum(
            jnp.exp(scores - new_highest[..., None]), axis=-1
        )
        return (new_highest, total_mass)

    start_high = jnp.full((HEADS, row_count), -1e30, jnp.float32)
    highest, total_mass = lax.fori_loop(
        0, needed, total_step, (start_high, jnp.zeros((HEADS, row_count), jnp.float32))
    )
    log_total = highest + jnp.log(total_mass)

    def value_step(block, output_rows):
        scores, lead_tile, upper_side = scores_at(block)
        soft_low = jnp.exp(scores - log_total[..., None]).astype(jnp.bfloat16)
        value_block = take_block(value_tiles, lead_tile, upper_side, tile_span)
        return output_rows + jnp.einsum(
            "hqk,khd->qhd", soft_low, value_block, preferred_element_type=jnp.float32
        )

    output_rows = lax.fori_loop(
        0, needed, value_step, jnp.zeros((row_count, HEADS, HEAD_DIM), jnp.float32)
    )
    return (output_rows, log_total)


def attend_half_back(
    query_half,
    query_pos,
    grad_half,
    log_total,
    centre,
    tables,
    needed,
    tile_span,
    blocks,
    key_grad,
    value_grad,
):
    key_tiles, value_tiles, pos_tiles = tables
    score_scale = HEAD_DIM ** (-0.5)

    def back_step(block, state):
        query_grad, key_acc, value_acc = state
        lead_tile, upper_side = block_start(block, tile_span, blocks)
        key_block = take_block(key_tiles, lead_tile, upper_side, tile_span)
        value_block = take_block(value_tiles, lead_tile, upper_side, tile_span)
        key_pos = take_block(pos_tiles, lead_tile, upper_side, tile_span)
        soft = jnp.exp(
            block_scores(query_half, query_pos, key_block, key_pos) - log_total[..., None]
        )
        value_part = jnp.einsum(
            "hqk,qhd->khd", soft.astype(jnp.bfloat16), grad_half, preferred_element_type=jnp.float32
        )
        grad_soft = jnp.einsum(
            "qhd,khd->hqk", grad_half, value_block, preferred_element_type=jnp.float32
        )
        grad_scores = (soft * (grad_soft - centre[..., None]) * score_scale).astype(jnp.bfloat16)
        query_grad = query_grad + jnp.einsum(
            "hqk,khd->qhd", grad_scores, key_block, preferred_element_type=jnp.float32
        )
        key_part = jnp.einsum(
            "hqk,qhd->khd", grad_scores, query_half, preferred_element_type=jnp.float32
        )
        key_acc = add_block(key_acc, key_part, lead_tile, upper_side, tile_span)
        value_acc = add_block(value_acc, value_part, lead_tile, upper_side, tile_span)
        return (query_grad, key_acc, value_acc)

    initial = (jnp.zeros(query_half.shape, jnp.float32), key_grad, value_grad)
    return lax.fori_loop(0, needed, back_step, initial)


def gather_weights(
    query_weight, key_weight, value_weight, output_weight, gate_weight, up_weight, down_weight
):
    row_parts = (
        lax.all_gather(query_weight, "dp", axis=0, tiled=True),
        lax.all_gather(key_weight, "dp", axis=0, tiled=True),
        lax.all_gather(value_weight, "dp", axis=0, tiled=True),
        lax.all_gather(output_weight, "dp", axis=0, tiled=True),
        lax.all_gather(gate_weight, "dp", axis=0, tiled=True),
        lax.all_gather(up_weight, "dp", axis=0, tiled=True),
        lax.all_gather(down_weight, "dp", axis=0, tiled=True),
    )
    return (
        lax.all_gather(row_parts[0], "ctx", axis=1, tiled=True),
        lax.all_gather(row_parts[1], "ctx", axis=1, tiled=True),
        lax.all_gather(row_parts[2], "ctx", axis=1, tiled=True),
        lax.all_gather(row_parts[3], "ctx", axis=1, tiled=True),
        lax.all_gather(row_parts[4], "ctx", axis=1, tiled=True),
        lax.all_gather(row_parts[5], "ctx", axis=1, tiled=True),
        lax.all_gather(row_parts[6], "ctx", axis=1, tiled=True),
    )


def fold_columns(running, operands, grads):
    norm_in_low, attended_low, norm_mid_low, hidden_low = operands
    columns = (
        lax.all_to_all(grads[0], "ctx", split_axis=1, concat_axis=0, tiled=True),
        lax.all_to_all(grads[1], "ctx", split_axis=1, concat_axis=0, tiled=True),
        lax.all_to_all(grads[2], "ctx", split_axis=1, concat_axis=0, tiled=True),
        lax.all_to_all(grads[3], "ctx", split_axis=1, concat_axis=0, tiled=True),
        lax.all_to_all(grads[4], "ctx", split_axis=1, concat_axis=0, tiled=True),
        lax.all_to_all(grads[5], "ctx", split_axis=1, concat_axis=0, tiled=True),
        lax.all_to_all(grads[6], "ctx", split_axis=1, concat_axis=0, tiled=True),
    )
    totals = tuple(running)
    norm_in_piece = lax.all_gather(norm_in_low, "ctx", axis=0, tiled=True)
    attended_piece = lax.all_gather(attended_low, "ctx", axis=0, tiled=True)
    norm_mid_piece = lax.all_gather(norm_mid_low, "ctx", axis=0, tiled=True)
    hidden_piece = lax.all_gather(hidden_low, "ctx", axis=0, tiled=True)
    lefts = (
        norm_in_piece,
        norm_in_piece,
        norm_in_piece,
        attended_piece,
        norm_mid_piece,
        norm_mid_piece,
        hidden_piece,
    )
    return list(
        tuple(
            (total + outer_sum(left, column) for total, left, column in zip(totals, lefts, columns))
        )
    )


def body(
    tokens,
    cotangent,
    counts,
    query_weight,
    key_weight,
    value_weight,
    output_weight,
    gate_weight,
    up_weight,
    down_weight,
):
    slot_count, tok_rows, model_width = tokens.shape
    blocks = lax.axis_size("ctx")
    ctx_index = lax.axis_index("ctx")
    seq_rows = tok_rows * blocks
    half_rows = tok_rows // 2
    proj_width = HEADS * HEAD_DIM
    tile_span = min(512, seq_rows // 2) // half_rows
    first_needed = ctx_index // tile_span + 1
    second_needed = (2 * blocks - 1 - ctx_index) // tile_span + 1
    own_positions = paired_positions(
        ctx_index * tok_rows + jnp.arange(tok_rows, dtype=jnp.int32), tok_rows, blocks
    )
    pos_tiles = paired_positions(jnp.arange(seq_rows, dtype=jnp.int32), tok_rows, blocks).reshape(
        blocks, 2, half_rows
    )
    cosine_table, sine_table = rope_tables(own_positions)

    def rotate_heads(projected):
        return rotate(
            projected.reshape(tok_rows, HEADS, HEAD_DIM), cosine_table, sine_table
        ).reshape(tok_rows, proj_width)

    running = [
        jnp.zeros((model_width, proj_width // blocks), jnp.float32),
        jnp.zeros((model_width, proj_width // blocks), jnp.float32),
        jnp.zeros((model_width, proj_width // blocks), jnp.float32),
        jnp.zeros((proj_width, model_width // blocks), jnp.float32),
        jnp.zeros((model_width, FF // blocks), jnp.float32),
        jnp.zeros((model_width, FF // blocks), jnp.float32),
        jnp.zeros((FF, model_width // blocks), jnp.float32),
    ]
    outputs = []
    token_grads = []
    for slot_index in range(slot_count):
        gathered = gather_weights(
            query_weight,
            key_weight,
            value_weight,
            output_weight,
            gate_weight,
            up_weight,
            down_weight,
        )
        full_query, full_key, full_value, full_output, full_gate, full_up, full_down = gathered
        live_mask = (slot_index < counts[0]).astype(jnp.float32)
        inputs = tokens[slot_index].astype(jnp.float32)
        normed_in, norm_in_back = jax.vjp(layer_norm, inputs)
        norm_in_low = normed_in.astype(jnp.bfloat16)
        query_proj = jnp.dot(norm_in_low, full_query, preferred_element_type=jnp.float32)
        key_proj = jnp.dot(norm_in_low, full_key, preferred_element_type=jnp.float32)
        value_proj = jnp.dot(norm_in_low, full_value, preferred_element_type=jnp.float32)
        query_rot, query_turn_back = jax.vjp(rotate_heads, query_proj)
        key_rot, key_turn_back = jax.vjp(rotate_heads, key_proj)
        query_heads = query_rot.astype(jnp.bfloat16).reshape(tok_rows, HEADS, HEAD_DIM)
        key_rows, value_rows = (
            lax.all_gather(key_rot.astype(jnp.bfloat16), "ctx", axis=0, tiled=True),
            lax.all_gather(value_proj.astype(jnp.bfloat16), "ctx", axis=0, tiled=True),
        )
        tables = (
            key_rows.reshape(blocks, 2, half_rows, HEADS, HEAD_DIM),
            value_rows.reshape(blocks, 2, half_rows, HEADS, HEAD_DIM),
            pos_tiles,
        )
        first_out, first_total = attend_half(
            query_heads[:half_rows],
            own_positions[:half_rows],
            tables,
            first_needed,
            tile_span,
            blocks,
        )
        second_out, second_total = attend_half(
            query_heads[half_rows:],
            own_positions[half_rows:],
            tables,
            second_needed,
            tile_span,
            blocks,
        )
        attended_wide = jnp.concatenate([first_out, second_out], axis=0)
        attended_low = attended_wide.reshape(tok_rows, proj_width).astype(jnp.bfloat16)
        after_attn = inputs + jnp.dot(attended_low, full_output, preferred_element_type=jnp.float32)
        normed_mid, norm_mid_back = jax.vjp(layer_norm, after_attn)
        norm_mid_low = normed_mid.astype(jnp.bfloat16)
        gate_proj = jnp.dot(norm_mid_low, full_gate, preferred_element_type=jnp.float32)
        up_proj = jnp.dot(norm_mid_low, full_up, preferred_element_type=jnp.float32)
        hidden, hidden_back = jax.vjp(
            lambda gate_in, up_in: jax.nn.silu(gate_in) * up_in, gate_proj, up_proj
        )
        hidden_low = hidden.astype(jnp.bfloat16)
        layer_out = after_attn + jnp.dot(hidden_low, full_down, preferred_element_type=jnp.float32)
        outputs.append((layer_out * live_mask).astype(jnp.bfloat16))
        grad_out = cotangent[slot_index].astype(jnp.float32) * live_mask
        grad_out_low = grad_out.astype(jnp.bfloat16)
        grad_gate_in, grad_up_in = hidden_back(back_product(grad_out_low, full_down))
        grad_gate_low = grad_gate_in.astype(jnp.bfloat16)
        grad_up_low = grad_up_in.astype(jnp.bfloat16)
        grad_norm_mid = back_product(grad_gate_low, full_gate) + back_product(grad_up_low, full_up)
        grad_after = grad_out + norm_mid_back(grad_norm_mid)[0]
        grad_after_low = grad_after.astype(jnp.bfloat16)
        grad_attended_low = back_product(grad_after_low, full_output).astype(jnp.bfloat16)
        grad_heads = grad_attended_low.reshape(tok_rows, HEADS, HEAD_DIM)
        centre = jnp.einsum("qhd,qhd->hq", grad_heads.astype(jnp.float32), attended_wide)
        empty_tiles = jnp.zeros((blocks, 2, half_rows, HEADS, HEAD_DIM), jnp.float32)
        first_query, key_acc, value_acc = attend_half_back(
            query_heads[:half_rows],
            own_positions[:half_rows],
            grad_heads[:half_rows],
            first_total,
            centre[:, :half_rows],
            tables,
            first_needed,
            tile_span,
            blocks,
            empty_tiles,
            empty_tiles,
        )
        second_query, key_acc, value_acc = attend_half_back(
            query_heads[half_rows:],
            own_positions[half_rows:],
            grad_heads[half_rows:],
            second_total,
            centre[:, half_rows:],
            tables,
            second_needed,
            tile_span,
            blocks,
            key_acc,
            value_acc,
        )
        grad_query_rot = jnp.concatenate([first_query, second_query], axis=0).reshape(
            tok_rows, proj_width
        )
        key_share, value_share = (
            lax.psum_scatter(
                key_acc.reshape(seq_rows, proj_width).astype(jnp.bfloat16),
                "ctx",
                scatter_dimension=0,
                tiled=True,
            ).astype(jnp.float32),
            lax.psum_scatter(
                value_acc.reshape(seq_rows, proj_width).astype(jnp.bfloat16),
                "ctx",
                scatter_dimension=0,
                tiled=True,
            ).astype(jnp.float32),
        )
        grad_query_low = query_turn_back(grad_query_rot)[0].astype(jnp.bfloat16)
        grad_key_low = key_turn_back(key_share)[0].astype(jnp.bfloat16)
        grad_value_low = value_share.astype(jnp.bfloat16)
        grad_norm_in = (
            back_product(grad_query_low, full_query)
            + back_product(grad_key_low, full_key)
            + back_product(grad_value_low, full_value)
        )
        token_grads.append(grad_after + norm_in_back(grad_norm_in)[0])
        grads = (
            grad_query_low,
            grad_key_low,
            grad_value_low,
            grad_after_low,
            grad_gate_low,
            grad_up_low,
            grad_out_low,
        )
        running = fold_columns(
            running, (norm_in_low, attended_low, norm_mid_low, hidden_low), grads
        )
    row_sums = (
        lax.psum_scatter(
            running[0].astype(jnp.bfloat16), "dp", scatter_dimension=0, tiled=True
        ).astype(jnp.float32),
        lax.psum_scatter(
            running[1].astype(jnp.bfloat16), "dp", scatter_dimension=0, tiled=True
        ).astype(jnp.float32),
        lax.psum_scatter(
            running[2].astype(jnp.bfloat16), "dp", scatter_dimension=0, tiled=True
        ).astype(jnp.float32),
        lax.psum_scatter(
            running[3].astype(jnp.bfloat16), "dp", scatter_dimension=0, tiled=True
        ).astype(jnp.float32),
        lax.psum_scatter(
            running[4].astype(jnp.bfloat16), "dp", scatter_dimension=0, tiled=True
        ).astype(jnp.float32),
        lax.psum_scatter(
            running[5].astype(jnp.bfloat16), "dp", scatter_dimension=0, tiled=True
        ).astype(jnp.float32),
        lax.psum_scatter(
            running[6].astype(jnp.bfloat16), "dp", scatter_dimension=0, tiled=True
        ).astype(jnp.float32),
    )
    return (
        jnp.stack(outputs),
        jnp.stack(token_grads),
        row_sums[0],
        row_sums[1],
        row_sums[2],
        row_sums[3],
        row_sums[4],
        row_sums[5],
        row_sums[6],
    )


def solution(mesh):
    in_specs = (
        P("dp", "ctx", None),
        P("dp", "ctx", None),
        P("dp"),
        P("dp", "ctx"),
        P("dp", "ctx"),
        P("dp", "ctx"),
        P("dp", "ctx"),
        P("dp", "ctx"),
        P("dp", "ctx"),
        P("dp", "ctx"),
    )
    out_specs = (
        P("dp", "ctx", None),
        P("dp", "ctx", None),
        P("dp", "ctx"),
        P("dp", "ctx"),
        P("dp", "ctx"),
        P("dp", "ctx"),
        P("dp", "ctx"),
        P("dp", "ctx"),
        P("dp", "ctx"),
    )
    return jax.shard_map(body, mesh=mesh, in_specs=in_specs, out_specs=out_specs, check_vma=False)
```

profile of v0, /device:TPU:0, one launch (start us, length us, event | category | flops | bytes accessed | tf_op | source)
XLA Modules:
  0.0 4924.4 jit_solution(12710881169533162679)
XLA Ops:
  70.2 122.8 %all-gather.29.cloned.1.call-done = bf16[2048,2048]{1,0:T(8,128)(2,1)} async-done(((bf16[2048,256]{1,0:T(8,128)(2,1)}), bf16[2048,2048]{1,0:T(8,128)(2,1)}) %all-gather.29.cloned.1.call-update) | async-done | bytes 8388624 | tf_op jit(solution)/shard_map/all_gather | solution.py:199
  199.3 119.2 %all-gather.41.cloned.1.call-done = bf16[2048,2048]{1,0:T(8,128)(2,1)} async-done(((bf16[2048,256]{1,0:T(8,128)(2,1)}), bf16[2048,2048]{1,0:T(8,128)(2,1)}) %all-gather.41.cloned.1.call-update) | async-done | bytes 8388624 | tf_op jit(solution)/shard_map/all_gather | solution.py:197
  331.0 113.1 %all-gather.35.cloned.1.call-done = bf16[2048,2048]{1,0:T(8,128)(2,1)} async-done(((bf16[2048,256]{1,0:T(8,128)(2,1)}), bf16[2048,2048]{1,0:T(8,128)(2,1)}) %all-gather.35.cloned.1.call-update) | async-done | bytes 8388624 | tf_op jit(solution)/shard_map/all_gather | solution.py:198
  574.8 70.0 %all-gather.59.cloned.1.call-done = bf16[1024,2048]{1,0:T(8,128)(2,1)} async-done(((bf16[128,2048]{1,0:T(8,128)(2,1)}), bf16[1024,2048]{1,0:T(8,128)(2,1)}) %all-gather.59.cloned.1.call-update) | async-done | bytes 4194320 | tf_op jit(solution)/shard_map/all_gather | solution.py:307
  651.6 67.5 %all-gather.61.cloned.1.call-done = bf16[1024,2048]{1,0:T(8,128)(2,1)} async-done(((bf16[128,2048]{1,0:T(8,128)(2,1)}), bf16[1024,2048]{1,0:T(8,128)(2,1)}) %all-gather.61.cloned.1.call-update) | async-done | bytes 4194320 | tf_op jit(solution)/shard_map/all_gather | solution.py:306
  800.2 67.5 %all-gather.37.cloned.1.call-done = bf16[1024,2048]{1,0:T(8,128)(2,1)} async-done(((bf16[128,2048]{1,0:T(8,128)(2,1)}), bf16[1024,2048]{1,0:T(8,128)(2,1)}) %all-gather.37.cloned.1.call-update) | async-done | bytes 4194320 | tf_op jit(solution)/shard_map/all_gather | solution.py:306
  922.1 71.4 %all-gather.45.cloned.1.call-done = bf16[2048,2048]{1,0:T(8,128)(2,1)} async-done(((bf16[2048,256]{1,0:T(8,128)(2,1)}), bf16[2048,2048]{1,0:T(8,128)(2,1)}) %all-gather.45.cloned.1.call-update) | async-done | bytes 8388624 | tf_op jit(solution)/shard_map/all_gather | solution.py:200
  1006.0 624.8 %all-gather.49.cloned.1.call-done = bf16[2048,8192]{1,0:T(8,128)(2,1)} async-done(((bf16[2048,1024]{1,0:T(8,128)(2,1)}), bf16[2048,8192]{1,0:T(8,128)(2,1)}) %all-gather.49.cloned.1.call-update) | async-done | bytes 33554448 | tf_op jit(solution)/shard_map/all_gather | solution.py:201
  1648.9 621.0 %all-gather.53.cloned.1.call-done = bf16[2048,8192]{1,0:T(8,128)(2,1)} async-done(((bf16[2048,1024]{1,0:T(8,128)(2,1)}), bf16[2048,8192]{1,0:T(8,128)(2,1)}) %all-gather.53.cloned.1.call-update) | async-done | bytes 33554448 | tf_op jit(solution)/shard_map/all_gather | solution.py:202
  2287.7 622.6 %all-gather.57.cloned.1.call-done = bf16[8192,2048]{1,0:T(8,128)(2,1)} async-done(((bf16[8192,256]{1,0:T(8,128)(2,1)}), bf16[8192,2048]{1,0:T(8,128)(2,1)}) %all-gather.57.cloned.1.call-update) | async-done | bytes 33554448 | tf_op jit(solution)/shard_map/all_gather | solution.py:203
  3203.8 42.8 while.153
  3500.2 71.7 %all-gather.69.cloned.1.call-done = bf16[1024,2048]{0,1:T(8,128)(2,1)} async-done(((bf16[128,2048]{0,1:T(8,128)(2,1)}), bf16[1024,2048]{0,1:T(8,128)(2,1)}) %all-gather.69.cloned.1.call-update) | async-done | bytes 4194320 | tf_op jit(solution)/shard_map/all_gather | solution.py:220
  3581.8 90.4 %reduce-scatter.14.cloned.1.call-done = bf16[128,2048]{1,0:T(8,128)(2,1)} async-done(((bf16[1024,2048]{1,0:T(8,128)(2,1)}), bf16[128,2048]{1,0:T(8,128)(2,1)}) %reduce-scatter.14.cloned.1.call-update) | async-done | bytes 524304 | tf_op jit(solution)/shard_map/reduce_scatter | solution.py:391
  3678.5 75.8 %all-gather.63.cloned.1.call-done = bf16[1024,2048]{1,0:T(8,128)(2,1)} async-done(((bf16[128,2048]{1,0:T(8,128)(2,1)}), bf16[1024,2048]{1,0:T(8,128)(2,1)}) %all-gather.63.cloned.1.call-update) | async-done | bytes 4194320 | tf_op jit(solution)/shard_map/all_gather | solution.py:219
  3759.3 69.0 %all-gather.65.cloned.1.call-done = bf16[1024,2048]{1,0:T(8,128)(2,1)} async-done(((bf16[128,2048]{1,0:T(8,128)(2,1)}), bf16[1024,2048]{1,0:T(8,128)(2,1)}) %all-gather.65.cloned.1.call-update) | async-done | bytes 4194320 | tf_op jit(solution)/shard_map/all_gather | solution.py:219
  3833.6 84.8 %reduce-scatter.18.cloned.1.call-done = bf16[128,2048]{1,0:T(8,128)(2,1)} async-done(((bf16[1024,2048]{1,0:T(8,128)(2,1)}), bf16[128,2048]{1,0:T(8,128)(2,1)}) %reduce-scatter.18.cloned.1.call-update) | async-done | bytes 524304 | tf_op jit(solution)/shard_map/reduce_scatter | solution.py:391
  3968.8 66.3 %all-gather.71.cloned.1.call-done = bf16[1024,2048]{1,0:T(8,128)(2,1)} async-done(((bf16[128,2048]{1,0:T(8,128)(2,1)}), bf16[1024,2048]{1,0:T(8,128)(2,1)}) %all-gather.71.cloned.1.call-update) | async-done | bytes 4194320 | tf_op jit(solution)/shard_map/all_gather | solution.py:221
  4050.4 92.9 %all-gather.73.cloned.1.call-done = bf16[1024,2048]{1,0:T(8,128)(2,1)} async-done(((bf16[128,2048]{1,0:T(8,128)(2,1)}), bf16[1024,2048]{1,0:T(8,128)(2,1)}) %all-gather.73.cloned.1.call-update) | async-done | bytes 4194320 | tf_op jit(solution)/shard_map/all_gather | solution.py:221
  4173.2 89.7 %all-to-all-done.11 = bf16[128,8,1024]{2,0,1:T(8,128)(2,1)S(1)} async-done(((bf16[128,8,1024]{2,0,1:T(8,128)(2,1)}), bf16[128,8,1024]{2,0,1:T(8,128)(2,1)S(1)}, u32[]{:S(2)}, u32[]{:S(2)}) %all-to-all-start.11) | async-done | bytes 2097184 | tf_op jit(solution)/shard_map/all_to_all | solution.py:215
  4310.8 125.4 %all-gather.75.cloned.1.call-done = bf16[1024,8192]{1,0:T(8,128)(2,1)} async-done(((bf16[128,8192]{1,0:T(8,128)(2,1)}), bf16[1024,8192]{1,0:T(8,128)(2,1)}) %all-gather.75.cloned.1.call-update) | async-done | bytes 16777232 | tf_op jit(solution)/shard_map/all_gather | solution.py:222
  4450.5 214.9 %all-gather.77.cloned.1.call-done = bf16[1024,8192]{1,0:T(8,128)(2,1)} async-done(((bf16[128,8192]{1,0:T(8,128)(2,1)}), bf16[1024,8192]{1,0:T(8,128)(2,1)}) %all-gather.77.cloned.1.call-update) | async-done | bytes 16777232 | tf_op jit(solution)/shard_map/all_gather | solution.py:222
  4775.3 45.3 reduce-scatter.28.cloned.1.call-done
  4823.4 44.3 reduce-scatter.30.cloned.1.call-done
  4870.4 44.2 reduce-scatter.32.cloned.1.call-done
  (788 shorter events, 1445.9 us)
Async XLA Ops:
  66.4 430.2 %all-gather.47.cloned.1.call-start = ((), (), s32[]{:S(2)}) async-start(), calls=%async_computation.35 | async-start | bytes 5242880 | tf_op jit(solution)/shard_map/all_gather | solution.py:192
  67.2 465.5 %all-gather.51.cloned.1.call-start = ((), (), s32[]{:S(2)}) async-start(), calls=%async_computation.37 | async-start | bytes 5242880 | tf_op jit(solution)/shard_map/all_gather | solution.py:193
  67.9 500.7 %all-gather.55.cloned.1.call-start = ((), (), s32[]{:S(2)}) async-start(), calls=%async_computation.39 | async-start | bytes 5242880 | tf_op jit(solution)/shard_map/all_gather | solution.py:194
  68.5 576.3 %all-gather.59.cloned.1.call-start = ((), (), s32[]{:S(2)}) async-start(), calls=%async_computation.41 | async-start | bytes 4718592 | tf_op jit(solution)/shard_map/all_gather | solution.py:307
  198.5 520.5 %all-gather.61.cloned.1.call-start = ((), (), s32[]{:S(2)}) async-start(), calls=%async_computation.42 | async-start | bytes 4718592 | tf_op jit(solution)/shard_map/all_gather | solution.py:306
  478.6 514.8 %all-gather.45.cloned.1.call-start = ((), (), s32[]{:S(2)}) async-start(), calls=%async_computation.34 | async-start | bytes 9437184 | tf_op jit(solution)/shard_map/all_gather | solution.py:200
  479.2 1151.6 %all-gather.49.cloned.1.call-start = ((), (), s32[]{:S(2)}) async-start(), calls=%async_computation.36 | async-start | bytes 37748736 | tf_op jit(solution)/shard_map/all_gather | solution.py:201
  496.7 1773.2 %all-gather.53.cloned.1.call-start = ((), (), s32[]{:S(2)}) async-start(), calls=%async_computation.38 | async-start | bytes 37748736 | tf_op jit(solution)/shard_map/all_gather | solution.py:202
  532.8 2377.5 %all-gather.57.cloned.1.call-start = ((), (), s32[]{:S(2)}) async-start(), calls=%async_computation.40 | async-start | bytes 37748736 | tf_op jit(solution)/shard_map/all_gather | solution.py:203
  568.7 2773.4 %reduce-scatter.16.cloned.1.call-start = ((), (), s32[]{:S(2)}) async-start(), calls=%async_computation.45 | async-start | bytes 4718592 | tf_op jit(solution)/shard_map/reduce_scatter | solution.py:385
  3272.6 481.6 %all-gather.63.cloned.1.call-start = ((), (), s32[]{:S(2)}) async-start(), calls=%async_computation.47 | async-start | bytes 4718592 | tf_op jit(solution)/shard_map/all_gather | solution.py:219
  3273.2 555.1 %all-gather.65.cloned.1.call-start = ((), (), s32[]{:S(2)}) async-start(), calls=%async_computation.48 | async-start | bytes 4718592 | tf_op jit(solution)/shard_map/all_gather | solution.py:219
  3273.9 644.5 %reduce-scatter.18.cloned.1.call-start = ((), (), s32[]{:S(2)}) async-start(), calls=%async_computation.46 | async-start | bytes 4718592 | tf_op jit(solution)/shard_map/reduce_scatter | solution.py:391
  3286.4 748.7 %all-gather.71.cloned.1.call-start = ((), (), s32[]{:S(2)}) async-start(), calls=%async_computation.55 | async-start | bytes 4718592 | tf_op jit(solution)/shard_map/all_gather | solution.py:221
  3287.0 856.3 %all-gather.73.cloned.1.call-start = ((), (), s32[]{:S(2)}) async-start(), calls=%async_computation.56 | async-start | bytes 4718592 | tf_op jit(solution)/shard_map/all_gather | solution.py:221
  3287.7 1148.5 %all-gather.75.cloned.1.call-start = ((), (), s32[]{:S(2)}) async-start(), calls=%async_computation.59 | async-start | bytes 18874368 | tf_op jit(solution)/shard_map/all_gather | solution.py:222
  3288.5 1376.9 %all-gather.77.cloned.1.call-start = ((), (), s32[]{:S(2)}) async-start(), calls=%async_computation.60 | async-start | bytes 18874368 | tf_op jit(solution)/shard_map/all_gather | solution.py:222
  3470.1 1241.4 %reduce-scatter.26.cloned.1.call-start = ((), (), s32[]{:S(2)}) async-start(), calls=%async_computation.54 | async-start | bytes 1310720 | tf_op jit(solution)/shard_map/reduce_scatter | solution.py:429
  3678.4 1068.6 %reduce-scatter.20.cloned.1.call-start = ((), (), s32[]{:S(2)}) async-start(), calls=%async_computation.49 | async-start | bytes 1310720 | tf_op jit(solution)/shard_map/reduce_scatter | solution.py:420
  3953.1 795.8 %reduce-scatter.22.cloned.1.call-start = ((), (), s32[]{:S(2)}) async-start(), calls=%async_computation.50 | async-start | bytes 1310720 | tf_op jit(solution)/shard_map/reduce_scatter | solution.py:423
  3959.3 814.2 %reduce-scatter.24.cloned.1.call-start = ((), (), s32[]{:S(2)}) async-start(), calls=%async_computation.51 | async-start | bytes 1310720 | tf_op jit(solution)/shard_map/reduce_scatter | solution.py:426
  4050.2 770.4 %reduce-scatter.28.cloned.1.call-start = ((), (), s32[]{:S(2)}) async-start(), calls=%async_computation.57 | async-start | bytes 5242880 | tf_op jit(solution)/shard_map/reduce_scatter | solution.py:432
  4162.4 705.3 %reduce-scatter.30.cloned.1.call-start = ((), (), s32[]{:S(2)}) async-start(), calls=%async_computation.58 | async-start | bytes 5242880 | tf_op jit(solution)/shard_map/reduce_scatter | solution.py:435
  4310.7 603.9 %reduce-scatter.32.cloned.1.call-start = ((), (), s32[]{:S(2)}) async-start(), calls=%async_computation.61 | async-start | bytes 5242880 | tf_op jit(solution)/shard_map/reduce_scatter | solution.py:438
  (180 other events, 14574.1 us)
Sparse Core Ops, SparseCore 0:
  67.6 125.3 all-gather.28
  194.9 123.6 all-gather.40
  320.5 123.5 all-gather.34
  571.4 73.3 all-gather.58
  647.3 71.6 all-gather.60
  721.7 71.7 all-gather.30
  796.0 71.6 all-gather.36
  869.6 123.7 all-gather.44
  994.8 635.9 all-gather.48
  1632.2 637.6 all-gather.52
  2271.2 639.0 all-gather.56
  3157.7 87.9 reduce-scatter.15
  3258.9 116.2 reduce-scatter.11
  3377.8 117.5 all-gather.66
  3498.0 73.8 all-gather.68
  3575.5 96.5 reduce-scatter.13
  3674.4 79.8 all-gather.62
  3756.6 71.6 all-gather.64
  3832.2 86.1 reduce-scatter.17
  3921.0 114.0 all-gather.70
  4037.8 105.5 all-gather.72
  4145.4 290.6 all-gather.74
  4438.7 226.5 all-gather.76
  4776.0 44.5 reduce-scatter.27
  (13 shorter events, 357.1 us)
where the time goes:
time: 4930 us; the launch traced here: 4920 us
  waiting for transfers between devices  4030 us (82%)
  matrix products  453 us (9%)
  local copies, waits for them, and re-layouts  233 us (5%)
  other arithmetic  129 us (3%)
  starting transfers between devices  61.9 us (1%)
    all_gather x1, waiting for transfers between devices, gather_weights(): lax.all_gather(row_parts[4], 'ctx', axis=1, tiled=True)  625 us
    all_gather x1, waiting for transfers between devices, gather_weights(): lax.all_gather(row_parts[6], 'ctx', axis=1, tiled=True)  623 us
    all_gather x1, waiting for transfers between devices, gather_weights(): lax.all_gather(row_parts[5], 'ctx', axis=1, tiled=True)  621 us
    all_gather x2, waiting for transfers between devices, fold_columns(): hidden_piece = lax.all_gather(hidden_low, 'ctx', axis=0, tiled=True)  340 us
    reduce_scatter x2, waiting for transfers between devices, body(): lax.psum_scatter(value_acc.reshape(seq_rows, proj_width).astype(jnp.bfloa...  175 us
    all_gather x2, waiting for transfers between devices, fold_columns(): norm_mid_piece = lax.all_gather(norm_mid_low, 'ctx', axis=0, tiled=True)  159 us
    dot_general x14, matrix products, back_product(): lax.dot_general(grad_rows, weight, (((1,), (1,)), ((), ())), preferred_el...  152 us
    all_gather x2, waiting for transfers between devices, fold_columns(): norm_in_piece = lax.all_gather(norm_in_low, 'ctx', axis=0, tiled=True)  145 us
  transfers between devices with their start and end apart: 51, of which 40 were waited for; matrix products, arithmetic and copies ran while one was open for 11% of the time, Pallas kernels for 0%

commit v1 on v0

--- a/solution.py
+++ b/solution.py
@@ -1,6 +1,11 @@
+import functools
+
 import jax
 import jax.numpy as jnp
 from jax import lax
+from jax.experimental import pallas as pl
+from jax.experimental.pallas import tpu as pltpu
+from jax.sharding import Mesh
 from jax.sharding import PartitionSpec as P
 
 HEADS = 16
@@ -452,7 +457,547 @@
     )
 
 
+PAIRS = ("x", "c", "w", "u", "v")
+SWAP = ((0, 1), (1, 0))
+
+
+def swap(value, axis):
+    return lax.ppermute(value, axis, SWAP)
+
+
+def join(own, other, bit, axis):
+    low = jnp.where(bit == 0, own, other)
+    high = jnp.where(bit == 0, other, own)
+    return jnp.concatenate([low, high], axis=axis)
+
+
+def low_bits(value):
+    return value.astype(jnp.bfloat16)
+
+
+def wide_bits(value):
+    return value.astype(jnp.float32)
+
+
+def half(value, bit, axis):
+    size = value.shape[axis] // 2
+    return lax.dynamic_slice_in_dim(value, bit * size, size, axis)
+
+
+def split_column_weights(weights, c):
+    kept = jnp.concatenate([half(weight, c, 1) for weight in weights], axis=1)
+    sent = jnp.concatenate([half(weight, 1 - c, 1) for weight in weights], axis=1)
+    return join(kept, swap(sent, "c"), c, 0)
+
+
+def join_column_grads(total, c, counts):
+    other = swap(low_bits(half(total, 1 - c, 0)), "c")
+    kept = half(total, c, 0)
+    grads, at = [], 0
+    for count in counts:
+        grads.append(join(wide_bits(kept[:, at : at + count]), wide_bits(other[:, at : at + count]), c, 1))
+        at += count
+    return grads
+
+
+def split_row_weights(parts, spots):
+    _, _, span, columns = parts.shape
+    kept, other = half(parts, spots["c"], 1), half(parts, 1 - spots["c"], 1)
+    parts = join(kept[:, 0], swap(other, "c")[:, 0], spots["c"], 0).reshape(2, 2, span, columns)
+    kept, other = half(parts, spots["u"], 0), half(parts, 1 - spots["u"], 0)
+    parts = join(kept[0], swap(other, "u")[0], spots["u"], 2)
+    kept, other = half(parts, spots["v"], 0)[0], swap(half(parts, 1 - spots["v"], 0), "v")[0]
+    low = jnp.where(spots["v"] == 0, kept, other)
+    high = jnp.where(spots["v"] == 0, other, kept)
+    return jnp.concatenate(
+        [low[:, :columns], high[:, :columns], low[:, columns:], high[:, columns:]], axis=1
+    )
+
+
+def join_row_grads(total, spots):
+    total = low_bits(total)
+    span, columns = total.shape[0], total.shape[1] // 4
+    even = jnp.concatenate([total[:, :columns], total[:, 2 * columns : 3 * columns]], axis=1)
+    odd = jnp.concatenate([total[:, columns : 2 * columns], total[:, 3 * columns :]], axis=1)
+    kept = jnp.where(spots["v"] == 0, even, odd)
+    other = swap(jnp.where(spots["v"] == 0, odd, even), "v")
+    parts = join(kept[None], other[None], spots["v"], 0)
+    kept, other = half(parts, spots["u"], 2), half(parts, 1 - spots["u"], 2)
+    parts = join(kept[None], swap(other, "u")[None], spots["u"], 0)
+    kept, other = half(parts, spots["c"], 0), half(parts, 1 - spots["c"], 0)
+    return join(kept[0][:, None], swap(other, "c")[0][:, None], spots["c"], 1)
+
+
+def spread(piece):
+    rows, columns = piece.shape
+    return lax.all_gather(piece, ("w", "x"), axis=0, tiled=True).reshape(2, 2 * rows, columns)
+
+
+def spread_by_pairs(piece, spots):
+    beside = swap(piece, "w")
+    across = swap(piece, "x")
+    both = swap(beside, "x")
+    own = join(piece, across, spots["x"], 0)
+    other = join(beside, both, spots["x"], 0)
+    return lax.optimization_barrier(join(own[None], other[None], spots["w"], 0))
+
+
+def collect(grad):
+    _, rows, columns = grad.shape
+    return lax.psum_scatter(
+        grad.reshape(2 * rows, columns), ("w", "x"), scatter_dimension=0, tiled=True
+    )
+
+
+def collect_by_pairs(grad, spots):
+    kept, other = half(grad, spots["x"], 1), half(grad, 1 - spots["x"], 1)
+    total = wide_bits(kept) + wide_bits(swap(other, "x"))
+    kept, other = half(total, spots["w"], 0)[0], half(total, 1 - spots["w"], 0)[0]
+    return kept + wide_bits(swap(low_bits(other), "w"))
+
+
+def gather_rows(value):
+    size = value.shape[0] // 2
+    first, second = value[:size], value[size:]
+    first_u = swap(first, "u")
+    second_v = swap(second, "v")
+    first_v = swap(first, "v")
+    second_u = swap(second, "u")
+    first_uv = swap(first_u, "v")
+    second_uv = swap(second_v, "u")
+    own = jnp.concatenate(
+        [first, first_u, first_v, first_uv, second, second_v, second_u, second_uv], axis=0
+    )
+    return own, swap(own, "c")
+
+
+def scatter_rows(total):
+    size = total.shape[0] // 8
+    first = total[: 4 * size]
+    second = total[4 * size :]
+    first = low_bits(wide_bits(first[: 2 * size]) + wide_bits(swap(first[2 * size :], "v")))
+    second = low_bits(wide_bits(second[: 2 * size]) + wide_bits(swap(second[2 * size :], "u")))
+    first = wide_bits(first[:size]) + wide_bits(swap(first[size:], "u"))
+    second = wide_bits(second[:size]) + wide_bits(swap(second[size:], "v"))
+    return jnp.concatenate([first, second], axis=0)
+
+
+ACROSS = (((1,), (1,)), ((), ()))
+DOWN = (((0,), (0,)), ((), ()))
+CHUNK = 256
+
+
+def dot(left, right, dims=(((1,), (0,)), ((), ()))):
+    return lax.dot_general(left, right, dims, preferred_element_type=jnp.float32)
+
+
+def whole(shape):
+    return pl.BlockSpec(shape, lambda *_: (0,) * len(shape))
+
+
+def kernel_call(kernel, grid, in_specs, out_specs, out_shape, flops, size, scratch=()):
+    return pl.pallas_call(
+        kernel,
+        grid=grid,
+        in_specs=in_specs,
+        out_specs=out_specs,
+        out_shape=out_shape,
+        scratch_shapes=scratch,
+        compiler_params=pltpu.CompilerParams(vmem_limit_bytes=48 * 2**20),
+        cost_estimate=pl.CostEstimate(flops=flops, bytes_accessed=size, transcendentals=0),
+    )
+
+
+def turn(values, cosine, sine):
+    return values * cosine + pltpu.roll(values, HEAD_DIM // 2, 1) * sine
+
+
+def attend_kernel(rows_ref, weight_ref, cos_ref, sin_ref, pos_col_ref, pos_row_ref, turned_ref, out_ref):
+    key_pos = pos_row_ref[...]
+    rows = rows_ref.shape[0]
+
+    @pl.loop(0, rows // CHUNK)
+    def _(i):
+        at = pl.ds(pl.multiple_of(i * CHUNK, CHUNK), CHUNK)
+        proj = dot(rows_ref[at, :], weight_ref[0])
+        cosine, sine = cos_ref[at, :], sin_ref[at, :]
+        turned_ref[at, :HEAD_DIM] = low_bits(turn(proj[:, :HEAD_DIM], cosine, sine))
+        turned_ref[at, HEAD_DIM : 2 * HEAD_DIM] = low_bits(
+            turn(proj[:, HEAD_DIM : 2 * HEAD_DIM], cosine, sine)
+        )
+        turned_ref[at, 2 * HEAD_DIM :] = low_bits(proj[:, 2 * HEAD_DIM :])
+
+    @pl.loop(0, rows // CHUNK)
+    def _(i):
+        at = pl.ds(pl.multiple_of(i * CHUNK, CHUNK), CHUNK)
+        scores = dot(turned_ref[at, :HEAD_DIM], turned_ref[:, HEAD_DIM : 2 * HEAD_DIM], ACROSS)
+        scores = scores * HEAD_DIM ** (-0.5)
+        scores = jnp.where(pos_col_ref[at, :] >= key_pos, scores, -1e30)
+        shifted = jnp.exp(scores - jnp.max(scores, axis=1, keepdims=True))
+        soft = shifted / jnp.sum(shifted, axis=1, keepdims=True)
+        out_ref[at, :] = low_bits(dot(low_bits(soft), turned_ref[:, 2 * HEAD_DIM :]))
+
+
+def attend(rows, weight, tables):
+    count, width = rows.shape
+    span = weight.shape[2]
+    return kernel_call(
+        attend_kernel,
+        (2,),
+        [
+            whole(rows.shape),
+            pl.BlockSpec((1, width, span), lambda h: (h, 0, 0)),
+            *[whole(table.shape) for table in tables],
+        ],
+        (
+            pl.BlockSpec((count, span), lambda h: (0, h)),
+            pl.BlockSpec((count, HEAD_DIM), lambda h: (0, h)),
+        ),
+        (
+            jax.ShapeDtypeStruct((count, 2 * span), jnp.bfloat16),
+            jax.ShapeDtypeStruct((count, 2 * HEAD_DIM), jnp.bfloat16),
+        ),
+        2 * count * width * 2 * span + 8 * count * count * HEAD_DIM * 3,
+        count * width * 2 + weight.size * 2,
+    )(rows, weight, *tables)
+
+
+def attend_back_kernel(
+    grad_ref, weight_ref, turned_ref, cos_ref, sin_ref, pos_col_ref, pos_row_ref, out_ref, key_acc, value_acc
+):
+    key_pos = pos_col_ref[...]
+    rows, width = grad_ref.shape
+    scale = HEAD_DIM ** (-0.5)
+    keys = turned_ref[:, HEAD_DIM : 2 * HEAD_DIM]
+    values = turned_ref[:, 2 * HEAD_DIM :]
+    key_acc[...] = jnp.zeros_like(key_acc)
+    value_acc[...] = jnp.zeros_like(value_acc)
+    for start in range(0, rows, CHUNK):
+        at = slice(start, start + CHUNK)
+        queries = turned_ref[at, :HEAD_DIM]
+        grads = low_bits(
+            dot(grad_ref[at, : width // 2], weight_ref[0], ACROSS)
+            + dot(grad_ref[at, width // 2 :], weight_ref[1], ACROSS)
+        )
+        scores = dot(keys, queries, ACROSS) * scale
+        scores = jnp.where(pos_row_ref[:, at] >= key_pos, scores, -1e30)
+        shifted = jnp.exp(scores - jnp.max(scores, axis=0, keepdims=True))
+        soft = shifted / jnp.sum(shifted, axis=0, keepdims=True)
+        grad_soft = dot(values, grads, ACROSS)
+        centre = jnp.sum(soft * grad_soft, axis=0, keepdims=True)
+        grad_scores = low_bits(soft * (grad_soft - centre) * scale)
+        value_acc[...] += dot(low_bits(soft), grads)
+        key_acc[...] += dot(grad_scores, queries)
+        query_grad = dot(grad_scores, keys, DOWN)
+        out_ref[at, :HEAD_DIM] = low_bits(turn(query_grad, cos_ref[at, :], -sin_ref[at, :]))
+    out_ref[:, HEAD_DIM : 2 * HEAD_DIM] = low_bits(turn(key_acc[...], cos_ref[...], -sin_ref[...]))
+    out_ref[:, 2 * HEAD_DIM :] = low_bits(value_acc[...])
+
+
+def attend_back(grads, weight, turned, tables):
+    count, width = grads.shape
+    span = turned.shape[1] // 2
+    return kernel_call(
+        attend_back_kernel,
+        (2,),
+        [
+            whole(grads.shape),
+            pl.BlockSpec((2, HEAD_DIM, width // 2), lambda h: (0, h, 0)),
+            pl.BlockSpec((count, span), lambda h: (0, h)),
+            *[whole(table.shape) for table in tables],
+        ],
+        pl.BlockSpec((count, span), lambda h: (0, h)),
+        jax.ShapeDtypeStruct(turned.shape, jnp.bfloat16),
+        2 * count * width * 2 * HEAD_DIM + 20 * count * count * HEAD_DIM * 2,
+        count * width * 2 + turned.size * 4,
+        [pltpu.VMEM((count, HEAD_DIM), jnp.float32)] * 2,
+    )(grads, weight, turned, *tables)
+
+
+def hidden_kernel(rows_ref, grad_ref, wide_ref, down_ref, hidden_ref, out_ref):
+    rows, width = rows_ref.shape
+    span = hidden_ref.shape[1]
+
+    @pl.loop(0, rows // CHUNK)
+    def _(i):
+        at = pl.ds(pl.multiple_of(i * CHUNK, CHUNK), CHUNK)
+        both = dot(rows_ref[at, :], wide_ref[0])
+        gate, up = both[:, :span], both[:, span:]
+        grad_hidden = dot(grad_ref[at, : width // 2], down_ref[0], ACROSS) + dot(
+            grad_ref[at, width // 2 :], down_ref[1], ACROSS
+        )
+        sigma = jax.nn.sigmoid(gate)
+        silu = gate * sigma
+        hidden_ref[at, :] = low_bits(silu * up)
+        out_ref[at, :span] = low_bits(grad_hidden * up * (sigma * (1.0 + gate * (1.0 - sigma))))
+        out_ref[at, span:] = low_bits(grad_hidden * silu)
+
+
+def hidden_pass(rows, grads, wide, down, tile):
+    count, width = rows.shape
+    span = wide.shape[2] // 2
+    tiles = span // tile
+    return kernel_call(
+        hidden_kernel,
+        (2, tiles),
+        [
+            whole(rows.shape),
+            whole(grads.shape),
+            pl.BlockSpec((1, width, 2 * tile), lambda w, t: (w, 0, t)),
+            pl.BlockSpec((2, tile, width // 2), lambda w, t: (0, tiles * w + t, 0)),
+        ],
+        (
+            pl.BlockSpec((count, tile), lambda w, t: (0, tiles * w + t)),
+            pl.BlockSpec((count, 2 * tile), lambda w, t: (0, tiles * w + t)),
+        ),
+        (
+            jax.ShapeDtypeStruct((count, 2 * span), jnp.bfloat16),
+            jax.ShapeDtypeStruct((count, 4 * span), jnp.bfloat16),
+        ),
+        2 * count * width * 6 * span,
+        count * width * 8 + wide.size * 3,
+    )(rows, grads, wide, down)
+
+
+def back_kernel(added, left_ref, weight_ref, *refs):
+    out_ref = refs[-1]
+    rows, depth = left_ref.shape
+
+    @pl.loop(0, rows // CHUNK)
+    def _(i):
+        at = pl.ds(pl.multiple_of(i * CHUNK, CHUNK), CHUNK)
+        total = dot(left_ref[at, : depth // 2], weight_ref[0], ACROSS) + dot(
+            left_ref[at, depth // 2 :], weight_ref[1], ACROSS
+        )
+        if added:
+            total += wide_bits(refs[0][at, :])
+        out_ref[at, :] = low_bits(total)
+
+
+def back_rows(left, weight, added=None):
+    count, depth = left.shape
+    width = weight.shape[1]
+    tile = 256
+    more = [] if added is None else [added]
+    return kernel_call(
+        functools.partial(back_kernel, len(more)),
+        (width // tile,),
+        [
+            whole(left.shape),
+            pl.BlockSpec((2, tile, depth // 2), lambda i: (0, i, 0)),
+            *[pl.BlockSpec((count, tile), lambda i: (0, i)) for _ in more],
+        ],
+        pl.BlockSpec((count, tile), lambda i: (0, i)),
+        jax.ShapeDtypeStruct((count, width), jnp.bfloat16),
+        2 * count * width * depth,
+        count * (width + depth) * 2 + weight.size * 2,
+    )(left, weight, *more)
+
+
+def ahead_kernel(added, left_ref, weight_ref, *refs):
+    out_ref = refs[-1]
+    rows = left_ref.shape[0]
+
+    @pl.loop(0, rows // CHUNK)
+    def _(i):
+        at = pl.ds(pl.multiple_of(i * CHUNK, CHUNK), CHUNK)
+        total = dot(left_ref[at, :], weight_ref[0])
+        if added:
+            total += wide_bits(refs[0][at, :])
+        out_ref[at, :] = low_bits(total)
+
+
+def ahead_rows(left, weight, added=None):
+    count, depth = left.shape
+    span = weight.shape[2]
+    tile = 512
+    tiles = span // tile
+    more = [] if added is None else [added]
+    return kernel_call(
+        functools.partial(ahead_kernel, len(more)),
+        (2, tiles),
+        [
+            whole(left.shape),
+            pl.BlockSpec((1, depth, tile), lambda w, t: (w, 0, t)),
+            *[pl.BlockSpec((count, tile), lambda w, t: (0, w * tiles + t)) for _ in more],
+        ],
+        pl.BlockSpec((count, tile), lambda w, t: (0, w * tiles + t)),
+        jax.ShapeDtypeStruct((count, 2 * span), jnp.bfloat16),
+        2 * count * depth * 2 * span,
+        count * (2 * span + depth) * 2 + weight.size * 2,
+    )(left, weight, *more)
+
+
+def outer_kernel(left_ref, left_other_ref, right_ref, right_other_ref, out_ref):
+    out_ref[0] = low_bits(
+        dot(left_ref[...], right_ref[...], DOWN) + dot(left_other_ref[...], right_other_ref[...], DOWN)
+    )
+
+
+def outer_rows(lefts, rights):
+    count, depth = lefts[0].shape
+    span = rights[0].shape[1] // 2
+    tile = 256
+    left_spec = pl.BlockSpec((count, tile), lambda w, i: (0, i))
+    right_spec = pl.BlockSpec((count, span), lambda w, i: (0, w))
+    return kernel_call(
+        outer_kernel,
+        (2, depth // tile),
+        [left_spec, left_spec, right_spec, right_spec],
+        pl.BlockSpec((1, tile, span), lambda w, i: (w, i, 0)),
+        jax.ShapeDtypeStruct((2, depth, span), jnp.bfloat16),
+        2 * 2 * count * depth * 2 * span,
+        4 * count * (depth + 2 * span) + depth * span * 4,
+    )(*lefts, *rights)
+
+
+def row_tables(half_block, blocks, spots):
+    block_at = jnp.arange(2 * half_block, dtype=jnp.int32)
+    pieces = []
+    for side, order in (("own", ((0, 0), (1, 0), (0, 1), (1, 1))), ("other", ((0, 0), (0, 1), (1, 0), (1, 1)))):
+        far = spots["w"] if side == "own" else 1 - spots["w"]
+        for flip_u, flip_v in order:
+            block = far * 4 + (spots["u"] ^ flip_u) * 2 + (spots["v"] ^ flip_v)
+            pieces.append(paired_positions(block * 2 * half_block + block_at, 2 * half_block, blocks))
+    positions = jnp.concatenate(pieces)
+    cosine, sine = rope_tables(positions)
+    cosine, sine = cosine[:, 0], sine[:, 0]
+    return (
+        jnp.concatenate([cosine, cosine], axis=1),
+        jnp.concatenate([-sine, sine], axis=1),
+        positions[:, None],
+        positions[None, :],
+    )
+
+
+def paired_body(
+    tokens,
+    cotangent,
+    counts,
+    query_weight,
+    key_weight,
+    value_weight,
+    output_weight,
+    gate_weight,
+    up_weight,
+    down_weight,
+):
+    tok_rows = tokens.shape[1]
+    spots = {name: lax.axis_index(name) for name in PAIRS}
+    tables = row_tables(tok_rows // 2, 8, spots)
+
+    def own_sequence(stored):
+        other = swap(half(stored, 1 - spots["w"], 0), "w")
+        return jnp.concatenate([half(stored, spots["w"], 0)[0], other[0]], axis=0)
+
+    def stored_slots(rows):
+        other = swap(low_bits(rows[tok_rows:]), "w").astype(rows.dtype)
+        return join(rows[None, :tok_rows], other[None], spots["w"], 0)
+
+    live = (spots["w"] < counts[0]).astype(jnp.float32)
+    token_rows = own_sequence(tokens)
+    grad_rows = own_sequence(cotangent)
+
+    columns = split_column_weights(
+        [query_weight, key_weight, value_weight, gate_weight, up_weight], spots["c"]
+    )
+    tile = 256
+    head_columns = 3 * HEAD_DIM
+    full_qkv = spread_by_pairs(columns[:, :head_columns], spots)
+    gate_at, up_at = head_columns, head_columns + gate_weight.shape[1] // 2
+    wide = jnp.concatenate(
+        [
+            columns[:, at + start : at + start + tile]
+            for start in range(0, up_at - gate_at, tile)
+            for at in (gate_at, up_at)
+        ],
+        axis=1,
+    )
+    full_wide = spread(wide)
+    output_span, down_span = output_weight.shape[0] // 4, down_weight.shape[0] // 4
+    rows = split_row_weights(
+        jnp.concatenate(
+            [
+                output_weight.reshape(2, 2, output_span, -1),
+                down_weight.reshape(2, 2, down_span, -1),
+            ],
+            axis=2,
+        ),
+        spots,
+    )
+    full_output = spread_by_pairs(rows[:output_span], spots)
+    full_down = spread_by_pairs(rows[output_span:], spots)
+
+    inputs = token_rows.astype(jnp.float32)
+    normed_in, norm_in_back = jax.vjp(layer_norm, inputs)
+    norm_in = gather_rows(low_bits(normed_in))
+    turned, attended = zip(*[attend(part, full_qkv, tables) for part in norm_in])
+    other = swap(ahead_rows(attended[1], full_output), "c")
+    after_attn = inputs + scatter_rows(ahead_rows(attended[0], full_output, other))
+    normed_mid, norm_mid_back = jax.vjp(layer_norm, after_attn)
+
+    norm_mid = gather_rows(low_bits(normed_mid))
+    grad_out = grad_rows.astype(jnp.float32) * live
+    grad_all = gather_rows(low_bits(grad_out))
+    hidden, grad_wide = zip(
+        *[hidden_pass(part, grads, full_wide, full_down, tile) for part, grads in zip(norm_mid, grad_all)]
+    )
+    other = swap(back_rows(grad_wide[1], full_wide), "c")
+    down_total = collect(outer_rows(hidden, grad_all))
+    grad_norm_mid = scatter_rows(back_rows(grad_wide[0], full_wide, other))
+    wide_total = collect(outer_rows(norm_mid, grad_wide))
+    other = swap(ahead_rows(hidden[1], full_down), "c")
+    layer_out = after_attn + scatter_rows(ahead_rows(hidden[0], full_down, other))
+    mixed = low_bits(layer_out * live)
+    grad_after = grad_out + norm_mid_back(grad_norm_mid)[0]
+
+    after_all = gather_rows(low_bits(grad_after))
+    grad_qkv = [
+        attend_back(part, full_output, kept, tables) for kept, part in zip(turned, after_all)
+    ]
+    other = swap(back_rows(grad_qkv[1], full_qkv), "c")
+    grad_norm_in = scatter_rows(back_rows(grad_qkv[0], full_qkv, other))
+    token_grad = grad_after + norm_in_back(grad_norm_in)[0]
+    output_total = collect_by_pairs(outer_rows(attended, after_all), spots)
+    qkv_total = collect_by_pairs(outer_rows(norm_in, grad_qkv), spots)
+
+    wide_parts = [wide_total[:, at : at + tile] for at in range(0, wide_total.shape[1], tile)]
+    wide_total = jnp.concatenate(wide_parts[0::2] + wide_parts[1::2], axis=1)
+    span = wide_total.shape[1] // 2
+    gate_grad, up_grad = join_column_grads(wide_total, spots["c"], (span, span))
+    query_grad, key_grad, value_grad = join_column_grads(qkv_total, spots["c"], (HEAD_DIM,) * 3)
+    output_grad = join_row_grads(output_total, spots)
+    down_grad = join_row_grads(down_total, spots)
+    return (
+        stored_slots(mixed),
+        stored_slots(token_grad),
+        query_grad,
+        key_grad,
+        value_grad,
+        wide_bits(output_grad.reshape(output_weight.shape)),
+        gate_grad,
+        up_grad,
+        wide_bits(down_grad.reshape(down_weight.shape)),
+    )
+
+
+def paired_solution(mesh):
+    pairs = Mesh(mesh.devices.reshape((2,) * 5), PAIRS)
+    rows, columns = ("x", "c"), ("w", "u", "v")
+    slots = P(rows, columns, None)
+    weight = P(rows, columns)
+    return jax.shard_map(
+        paired_body,
+        mesh=pairs,
+        in_specs=(slots, slots, P(rows)) + (weight,) * 7,
+        out_specs=(slots, slots) + (weight,) * 7,
+        check_vma=False,
+    )
+
+
 def solution(mesh):
+    if mesh.shape["ctx"] == 8 and mesh.shape["dp"] == 4:
+        return paired_solution(mesh)
     in_specs = (
         P("dp", "ctx", None),
         P("dp", "ctx", None),

time: 4930 us -> 1100 us (0.22)
  waiting for transfers between devices: 4030 us -> 617 us
  matrix products: 453 us -> 0 us
  Pallas kernels: 0 us -> 263 us
  local copies, waits for them, and re-layouts: 233 us -> 54.8 us
  other arithmetic: 129 us -> 57.8 us
    all_gather x26 -> x1, waiting for transfers between devices: 3410 us -> 0.01 us  [spread(): lax.all_gather(piece, ('w', 'x'), axis=0, tiled=True)]
    ppermute x0 -> x77, waiting for transfers between devices: none -> 617 us  [swap(): return lax.ppermute(value, axis, SWAP)]
    dot_general x84 -> x0, matrix products: 453 us -> none  [the longest x14 152 us: back_product(): lax.dot_general(grad_rows, weight, (((1,), (1,)), ((), ())), preferred_el...]
    reduce_scatter x11 -> x2, waiting for transfers between devices: 363 us -> 0.01 us  [collect(): lax.psum_scatter(grad.reshape(2 * rows, columns), ('w', 'x'), scatter_dim...]
    pallas_call x0 -> x18, Pallas kernels: none -> 263 us  [the longest x4 65.6 us: outer_rows(): kernel_call(outer_kernel, (2, depth // tile), [left_spec, left_spec, righ...]
    all_to_all x14 -> x0, waiting for transfers between devices: 240 us -> none  [the longest x2 89.7 us: fold_columns(): lax.all_to_all(grads[5], 'ctx', split_axis=1, concat_axis=0, tiled=True)]
    ppermute x0 -> x77, starting transfers between devices: none -> 67.6 us  [swap(): return lax.ppermute(value, axis, SWAP)]
    dynamic_update_slice x6 -> x0, other arithmetic: 63.3 us -> none  [add_block(): lax.dynamic_update_slice(tiles, before + part.reshape(piece_shape), starts)]
  transfers between devices with their start and end apart: 51 -> 80, of which waited for: 40 -> 34; matrix products, arithmetic and copies ran while one was open for 11% -> 9% of each run, Pallas kernels for 0% -> 19%
where the time goes in v1:
time: 1100 us; the launch traced here: 1090 us
  waiting for transfers between devices  617 us (56%)
  Pallas kernels  263 us (24%)
  starting transfers between devices  78.4 us (7%)
  other arithmetic  57.8 us (5%)
  local copies, waits for them, and re-layouts  54.8 us (5%)
  between operations  16.3 us (1%)
    ppermute x77, waiting for transfers between devices, swap(): return lax.ppermute(value, axis, SWAP)  617 us
    ppermute x77, starting transfers between devices, swap(): return lax.ppermute(value, axis, SWAP)  67.6 us
    pallas_call x4, Pallas kernels, outer_rows(): kernel_call(outer_kernel, (2, depth // tile), [left_spec, left_spec, righ...  65.6 us
    pallas_call x4, Pallas kernels, back_rows(): kernel_call(functools.partial(back_kernel, len(more)), (width // tile,),...  60.6 us
    pallas_call x2, Pallas kernels, hidden_pass(): kernel_call(hidden_kernel, (2, tiles), [whole(rows.shape), whole(grads.sh...  43.8 us
    unnamed x134, local copies, waits for them, and re-layouts  31.9 us
    pallas_call x2, Pallas kernels, attend(): kernel_call(attend_kernel, (2,), [whole(rows.shape), pl.BlockSpec((1, wid...  31.5 us
    pallas_call x2, Pallas kernels, attend_back(): kernel_call(attend_back_kernel, (2,), [whole(grads.shape), pl.BlockSpec((...  31 us
  transfers between devices with their start and end apart: 80, of which 34 were waited for; matrix products, arithmetic and copies ran while one was open for 9% of the time, Pallas kernels for 19%

profile of v1, /device:TPU:0, one launch (start us, length us, event | category | flops | bytes accessed | tf_op | source)
XLA Modules:
  0.0 1087.7 jit_solution(16096595825256432447)
XLA Ops:
  22.1 23.2 %collective-permute-done = bf16[1,128,2048]{2,1,0:T(8,128)(2,1)S(1)} collective-permute-done((bf16[1,128,2048]{2,1,0:T(8,128)(2,1)S(1)}, bf16[1,128,2048]{2,1,0:T(8,128)(2,1)S(1)}, u32[]{:S(2)}, u32[]{:S(2)}) %collective-permute-start) | collective-permute-done | bytes 524320 | tf_op jit(solution)/shard_map/ppermute | solution.py:465
  126.5 20.5 %collective-permute-done.9 = bf16[1024,384]{1,0:T(8,128)(2,1)} collective-permute-done((bf16[1024,384]{1,0:T(8,128)(2,1)S(1)}, bf16[1024,384]{1,0:T(8,128)(2,1)}, u32[]{:S(2)}, u32[]{:S(2)}) %collective-permute-start.9) | collective-permute-done | bytes 786464 | tf_op jit(solution)/shard_map/ppermute | solution.py:465
  154.7 16.2 %collective-permute-done.16 = bf16[128,1024]{1,0:T(8,128)(2,1)S(1)} collective-permute-done((bf16[128,1024]{1,0:T(8,128)(2,1)}, bf16[128,1024]{1,0:T(8,128)(2,1)S(1)}, u32[]{:S(2)}, u32[]{:S(2)}) %collective-permute-start.16) | collective-permute-done | bytes 262176 | tf_op jit(solution)/shard_map/ppermute | solution.py:465
  203.8 15.8 %shard_map.169 = (bf16[1024,768]{1,0:T(8,128)(2,1)S(1)}, bf16[1024,256]{1,0:T(8,128)(2,1)S(1)}) custom-call(bf16[1024,2048]{1,0:T(8,128)(2,1)} %constant_dynamic-update-slice_fusion.rows_ref.left_ref, bf16[2,2048,384]{2,1,0:T(8,128)(2,1)} %pad_maximum_fusion.1.weight_ref, f32[1024,128]{1,0:T(8,128)S(1)} %get-tuple-element.148.cos_ref, ...), custom_call_target="tpu_custom_call" | custom-call | flops 6442450944 | bytes 7340032 | tf_op jit(solution)/shard_map/pallas_call | solution.py:644
  231.3 23.8 %collective-permute-done.29 = bf16[1,128,2048]{2,1,0:T(8,128)(2,1)} collective-permute-done((bf16[1,128,2048]{2,1,0:T(8,128)(2,1)}, bf16[1,128,2048]{2,1,0:T(8,128)(2,1)}, u32[]{:S(2)}, u32[]{:S(2)}) %collective-permute-start.29) | collective-permute-done | bytes 524320 | tf_op jit(solution)/shard_map/ppermute | solution.py:465
  258.7 36.9 %collective-permute-done.30 = bf16[128,2048]{1,0:T(8,128)(2,1)S(1)} collective-permute-done((bf16[128,2048]{1,0:T(8,128)(2,1)S(1)}, bf16[128,2048]{1,0:T(8,128)(2,1)S(1)}, u32[]{:S(2)}, u32[]{:S(2)}) %collective-permute-start.30) | collective-permute-done | bytes 524320 | tf_op jit(solution)/shard_map/ppermute | solution.py:465
  310.6 33.7 %collective-permute-done.20 = bf16[128,2048]{1,0:T(8,128)(2,1)S(1)} collective-permute-done((bf16[128,2048]{1,0:T(8,128)(2,1)S(1)}, bf16[128,2048]{1,0:T(8,128)(2,1)S(1)}, u32[]{:S(2)}, u32[]{:S(2)}) %collective-permute-start.20) | collective-permute-done | bytes 524320 | tf_op jit(solution)/shard_map/ppermute | solution.py:465
  349.4 37.4 %collective-permute-done.23 = bf16[128,2048]{1,0:T(8,128)(2,1)S(1)} collective-permute-done((bf16[128,2048]{1,0:T(8,128)(2,1)S(1)}, bf16[128,2048]{1,0:T(8,128)(2,1)S(1)}, u32[]{:S(2)}, u32[]{:S(2)}) %collective-permute-start.23) | collective-permute-done | bytes 524320 | tf_op jit(solution)/shard_map/ppermute | solution.py:465
  414.9 47.8 %collective-permute-done.37 = bf16[512,1024]{1,0:T(8,128)(2,1)S(1)} collective-permute-done((bf16[512,1024]{1,0:T(8,128)(2,1)S(1)}, bf16[512,1024]{1,0:T(8,128)(2,1)S(1)}, u32[]{:S(2)}, u32[]{:S(2)}) %collective-permute-start.37) | collective-permute-done | bytes 1048608 | tf_op jit(solution)/shard_map/ppermute | solution.py:465
  462.8 25.0 %collective-permute-done.38 = bf16[512,1024]{1,0:T(8,128)(2,1)S(1)} collective-permute-done((bf16[512,1024]{1,0:T(8,128)(2,1)S(1)}, bf16[512,1024]{1,0:T(8,128)(2,1)S(1)}, u32[]{:S(2)}, u32[]{:S(2)}) %collective-permute-start.38) | collective-permute-done | bytes 1048608 | tf_op jit(solution)/shard_map/ppermute | solution.py:465
  491.7 21.9 %shard_map.174 = (bf16[1024,1024]{1,0:T(8,128)(2,1)S(1)}, bf16[1024,2048]{1,0:T(8,128)(2,1)}) custom-call(bf16[1024,2048]{1,0:T(8,128)(2,1)} %collective-permute-done.39.rows_ref.left_other_ref, bf16[1024,2048]{1,0:T(8,128)(2,1)} %collective-permute-done.40.grad_ref.right_other_ref, bf16[2,2048,1024]{2,1,0:T(8,128)(2,1)} %bitcast.125, ...), custom_call_target="tpu_custom_call" | custom-call | flops 12884901888 | bytes 29360128 | tf_op jit(solution)/shard_map/pallas_call | solution.py:740
  513.6 18.6 %shard_map.177 = bf16[1024,2048]{1,0:T(8,128)(2,1)} custom-call(bf16[1024,2048]{1,0:T(8,128)(2,1)} %get-tuple-element.22.left_ref.right_other_ref, bf16[2,2048,1024]{2,1,0:T(8,128)(2,1)} %bitcast.126), custom_call_target="tpu_custom_call" | custom-call | flops 8589934592 | bytes 16777216 | tf_op jit(solution)/shard_map/pallas_call | solution.py:782
  542.0 21.9 %shard_map.173 = (bf16[1024,1024]{1,0:T(8,128)(2,1)S(1)}, bf16[1024,2048]{1,0:T(8,128)(2,1)}) custom-call(bf16[1024,2048]{1,0:T(8,128)(2,1)} %constant_dynamic-update-slice_fusion.9.rows_ref.left_ref, bf16[1024,2048]{1,0:T(8,128)(2,1)} %copy-done.46, bf16[2,2048,1024]{2,1,0:T(8,128)(2,1)} %bitcast.127, bf16[2,1024,1024]{2,1,0:T(8,128)(2,1)} %pad_maximum_fusion.down_ref.weight_ref), custom_call_target="tpu_custom_call" | custom-call | flops 12884901888 | bytes 29360128 | tf_op jit(solution)/shard_map/pallas_call | solution.py:740
  563.9 15.9 %shard_map.186 = bf16[2,1024,1024]{2,1,0:T(8,128)(2,1)} custom-call(bf16[1024,1024]{1,0:T(8,128)(2,1)S(1)} %get-tuple-element.19.left_ref, bf16[1024,1024]{1,0:T(8,128)(2,1)S(1)} %get-tuple-element.20.left_ref.left_other_ref, bf16[1024,2048]{1,0:T(8,128)(2,1)} %copy-done.46, bf16[1024,2048]{1,0:T(8,128)(2,1)} %collective-permute-done.40.grad_ref.right_other_ref), custom_call_target="tpu_custom_call" | custom-call | flops 8589934592 | bytes 16777216 | tf_op jit(solution)/shard_map/pallas_call | solution.py:843
  590.4 18.5 %shard_map.178 = bf16[1024,2048]{1,0:T(8,128)(2,1)S(1)} custom-call(bf16[1024,2048]{1,0:T(8,128)(2,1)} %get-tuple-element.21.left_ref.right_ref, bf16[2,2048,1024]{2,1,0:T(8,128)(2,1)} %bitcast.128, bf16[1024,2048]{1,0:T(8,128)(2,1)} %collective-permute-done.47.refs_0_), custom_call_target="tpu_custom_call" | custom-call | flops 8589934592 | bytes 16777216 | tf_op jit(solution)/shard_map/pallas_call | solution.py:782
  636.2 23.3 %collective-permute-done.50 = bf16[256,2048]{1,0:T(8,128)(2,1)} collective-permute-done((bf16[256,2048]{1,0:T(8,128)(2,1)S(1)}, bf16[256,2048]{1,0:T(8,128)(2,1)}, u32[]{:S(2)}, u32[]{:S(2)}) %collective-permute-start.50) | collective-permute-done | bytes 1048608 | tf_op jit(solution)/shard_map/ppermute | solution.py:465
  663.9 20.2 %collective-permute-done.44 = bf16[256,2048]{1,0:T(8,128)(2,1)S(1)} collective-permute-done((bf16[256,2048]{1,0:T(8,128)(2,1)S(1)}, bf16[256,2048]{1,0:T(8,128)(2,1)S(1)}, u32[]{:S(2)}, u32[]{:S(2)}) %collective-permute-start.44) | collective-permute-done | bytes 1048608 | tf_op jit(solution)/shard_map/ppermute | solution.py:465
  727.3 26.5 %shard_map.185 = bf16[2,2048,1024]{2,1,0:T(8,128)(2,1)} custom-call(bf16[1024,2048]{1,0:T(8,128)(2,1)} %constant_dynamic-update-slice_fusion.9.rows_ref.left_ref, bf16[1024,2048]{1,0:T(8,128)(2,1)} %collective-permute-done.39.rows_ref.left_other_ref, bf16[1024,2048]{1,0:T(8,128)(2,1)} %get-tuple-element.21.left_ref.right_ref, ...), custom_call_target="tpu_custom_call" | custom-call | flops 17179869184 | bytes 25165824 | tf_op jit(solution)/shard_map/pallas_call | solution.py:843
  778.1 17.6 %collective-permute-done.57 = bf16[128,2048]{1,0:T(8,128)(2,1)S(1)} collective-permute-done((bf16[128,2048]{1,0:T(8,128)(2,1)}, bf16[128,2048]{1,0:T(8,128)(2,1)S(1)}, u32[]{:S(2)}, u32[]{:S(2)}) %collective-permute-start.57) | collective-permute-done | bytes 524320 | tf_op jit(solution)/shard_map/ppermute | solution.py:465
  797.6 50.7 %collective-permute-done.46 = bf16[128,2048]{1,0:T(8,128)(2,1)} collective-permute-done((bf16[128,2048]{1,0:T(8,128)(2,1)}, bf16[128,2048]{1,0:T(8,128)(2,1)}, u32[]{:S(2)}, u32[]{:S(2)}) %collective-permute-start.46) | collective-permute-done | bytes 524320 | tf_op jit(solution)/shard_map/ppermute | solution.py:465
  912.6 18.4 %shard_map.183 = bf16[2,2048,384]{2,1,0:T(8,128)(2,1)} custom-call(bf16[1024,2048]{1,0:T(8,128)(2,1)} %constant_dynamic-update-slice_fusion.rows_ref.left_ref, bf16[1024,2048]{1,0:T(8,128)(2,1)} %collective-permute-done.17.rows_ref.left_other_ref, bf16[1024,768]{1,0:T(8,128)(2,1)S(1)} %shard_map.179.left_ref.right_ref, ...), custom_call_target="tpu_custom_call" | custom-call | flops 6442450944 | bytes 14680064 | tf_op jit(solution)/shard_map/pallas_call | solution.py:843
  950.3 18.6 %collective-permute-done.65 = bf16[2,1024,384]{2,1,0:T(8,128)(2,1)S(1)} collective-permute-done((bf16[2,1024,384]{2,1,0:T(8,128)(2,1)S(1)}, bf16[2,1024,384]{2,1,0:T(8,128)(2,1)S(1)}, u32[]{:S(2)}, u32[]{:S(2)}) %collective-permute-start.65) | collective-permute-done | bytes 1572896 | tf_op jit(solution)/shard_map/ppermute | solution.py:465
  987.7 39.7 %collective-permute-done.71 = bf16[2,128,256]{2,1,0:T(8,128)(2,1)S(1)} collective-permute-done((bf16[2,128,256]{2,1,0:T(8,128)(2,1)S(1)}, bf16[2,128,256]{2,1,0:T(8,128)(2,1)S(1)}, u32[]{:S(2)}, u32[]{:S(2)}) %collective-permute-start.71) | collective-permute-done | bytes 131104 | tf_op jit(solution)/shard_map/ppermute | solution.py:465
  1056.5 18.0 %collective-permute-done.64 = bf16[128,2048]{1,0:T(8,128)(2,1)} collective-permute-done((bf16[128,2048]{1,0:T(8,128)(2,1)}, bf16[128,2048]{1,0:T(8,128)(2,1)}, u32[]{:S(2)}, u32[]{:S(2)}) %collective-permute-start.64) | collective-permute-done | bytes 524320 | tf_op jit(solution)/shard_map/ppermute | solution.py:465
  (430 shorter events, 461.4 us)
Async XLA Ops:
  7.2 484.5 %all-gather.2.cloned.1.call-start = ((), (), s32[]{:S(2)}) async-start(), calls=%async_computation.2 | async-start | bytes 10485760 | tf_op jit(solution)/shard_map/all_gather | solution.py:533
  16.4 83.2 %collective-permute-start.7 = (bf16[512,1408]{1,0:T(8,128)(2,1)}, bf16[512,1408]{1,0:T(8,128)(2,1)}, u32[]{:S(2)}, u32[]{:S(2)}) collective-permute-start(bf16[512,1408]{1,0:T(8,128)(2,1)} %get-tuple-element.112), channel_id=1, source_target_pairs={{0,8},{8,0},{1,9},{9,1},{2,10},{10,2},{3,11},{11,3},{4,12},{12,4},... | collective-permute-start | bytes 4325384 | tf_op jit(solution)/shard_map/ppermute | solution.py:465
  98.2 78.1 %collective-permute-start.17 = (bf16[1024,2048]{1,0:T(8,128)(2,1)}, bf16[1024,2048]{1,0:T(8,128)(2,1)}, u32[]{:S(2)}, u32[]{:S(2)}) collective-permute-start(bf16[1024,2048]{1,0:T(8,128)(2,1)} %constant_dynamic-update-slice_fusion.rows_ref.left_ref), channel_id=1, source_target_pairs={{0,8},{8,0},{1,9},{9,1},{2,10},{10,2},{3,11},{11,3},{4,12},{12,4},... | collective-permute-start | bytes 12582920 | tf_op jit(solution)/shard_map/ppermute | solution.py:465
  101.4 51.0 %collective-permute-start.8 = (bf16[1024,384]{1,0:T(8,128)(2,1)S(1)}, bf16[1024,384]{1,0:T(8,128)(2,1)}, u32[]{:S(2)}, u32[]{:S(2)}) collective-permute-start(bf16[1024,384]{1,0:T(8,128)(2,1)S(1)} %fusion.18), channel_id=1, source_target_pairs={{0,16},{16,0},{1,17},{17,1},{2,18},{18,2},{3,19},{19,3},{4,20},{20... | collective-permute-start | bytes 2359304 | tf_op jit(solution)/shard_map/ppermute | solution.py:465
  198.1 57.0 %collective-permute-start.29 = (bf16[1,128,2048]{2,1,0:T(8,128)(2,1)}, bf16[1,128,2048]{2,1,0:T(8,128)(2,1)}, u32[]{:S(2)}, u32[]{:S(2)}) collective-permute-start(bf16[1,128,2048]{2,1,0:T(8,128)(2,1)} %get-tuple-element.106), channel_id=1, source_target_pairs={{0,4},{4,0},{1,5},{5,1},{2,6},{6,2},{3,7},{7,3},{8,12},{12,8},{9,1... | collective-permute-start | bytes 1572872 | tf_op jit(solution)/shard_map/ppermute | solution.py:465
  203.5 647.1 %reduce-scatter.5.cloned.1.call-start = ((), (), s32[]{:S(2)}) async-start(), calls=%async_computation.4 | async-start | bytes 5242880 | tf_op jit(solution)/shard_map/reduce_scatter | solution.py:547
  225.9 69.7 %collective-permute-start.19 = (bf16[256,2048]{1,0:T(8,128)(2,1)S(1)}, bf16[256,2048]{1,0:T(8,128)(2,1)S(1)}, u32[]{:S(2)}, u32[]{:S(2)}) collective-permute-start(bf16[256,2048]{1,0:T(8,128)(2,1)S(1)} %get-tuple-element.47), channel_id=1, source_target_pairs={{0,1},{1,0},{2,3},{3,2},{4,5},{5,4},{6,7},{7,6},{8,9},{9,8},{10,11... | collective-permute-start | bytes 3145736 | tf_op jit(solution)/shard_map/ppermute | solution.py:465
  226.6 69.6 %collective-permute-start.21 = (bf16[256,2048]{1,0:T(8,128)(2,1)S(1)}, bf16[256,2048]{1,0:T(8,128)(2,1)S(1)}, u32[]{:S(2)}, u32[]{:S(2)}) collective-permute-start(bf16[256,2048]{1,0:T(8,128)(2,1)S(1)} %get-tuple-element.48), channel_id=1, source_target_pairs={{0,2},{2,0},{1,3},{3,1},{4,6},{6,4},{5,7},{7,5},{8,10},{10,8},{9,1... | collective-permute-start | bytes 3145736 | tf_op jit(solution)/shard_map/ppermute | solution.py:465
  295.7 53.7 %collective-permute-start.34 = (bf16[128,2048]{1,0:T(8,128)(2,1)S(1)}, bf16[128,2048]{1,0:T(8,128)(2,1)S(1)}, u32[]{:S(2)}, u32[]{:S(2)}) collective-permute-start(bf16[128,2048]{1,0:T(8,128)(2,1)S(1)} %get-tuple-element.102), channel_id=1, source_target_pairs={{0,2},{2,0},{1,3},{3,1},{4,6},{6,4},{5,7},{7,5},{8,10},{10,8},{9,1... | collective-permute-start | bytes 1572872 | tf_op jit(solution)/shard_map/ppermute | solution.py:465
  297.2 47.0 %collective-permute-start.20 = (bf16[128,2048]{1,0:T(8,128)(2,1)S(1)}, bf16[128,2048]{1,0:T(8,128)(2,1)S(1)}, u32[]{:S(2)}, u32[]{:S(2)}) collective-permute-start(bf16[128,2048]{1,0:T(8,128)(2,1)S(1)} %slice.344), channel_id=1, source_target_pairs={{0,2},{2,0},{1,3},{3,1},{4,6},{6,4},{5,7},{7,5},{8,10},{10,8},{9,1... | collective-permute-start | bytes 1572872 | tf_op jit(solution)/shard_map/ppermute | solution.py:465
  299.4 87.9 %collective-permute-start.35 = (bf16[128,2048]{1,0:T(8,128)(2,1)S(1)}, bf16[128,2048]{1,0:T(8,128)(2,1)S(1)}, u32[]{:S(2)}, u32[]{:S(2)}) collective-permute-start(bf16[128,2048]{1,0:T(8,128)(2,1)S(1)} %collective-permute-done.33), channel_id=1, source_target_pairs={{0,2},{2,0},{1,3},{3,1},{4,6},{6,4},{5,7},{7,5},{8,10},{10,8},{9,1... | collective-permute-start | bytes 1572872 | tf_op jit(solution)/shard_map/ppermute | solution.py:465
  387.3 104.4 %collective-permute-start.40 = (bf16[1024,2048]{1,0:T(8,128)(2,1)S(1)}, bf16[1024,2048]{1,0:T(8,128)(2,1)}, u32[]{:S(2)}, u32[]{:S(2)}) collective-permute-start(bf16[1024,2048]{1,0:T(8,128)(2,1)S(1)} %constant_dynamic-update-slice_fusion.17.grad_ref.right_ref), channel_id=1, source_target_pairs={{0,8},{8,0},{1,9},{9,1},{2,10},{10,2},{3,11},{11,3},{4,12},{12,4},... | collective-permute-start | bytes 12582920 | tf_op jit(solution)/shard_map/ppermute | solution.py:465
  413.8 77.9 %collective-permute-start.39 = (bf16[1024,2048]{1,0:T(8,128)(2,1)}, bf16[1024,2048]{1,0:T(8,128)(2,1)}, u32[]{:S(2)}, u32[]{:S(2)}) collective-permute-start(bf16[1024,2048]{1,0:T(8,128)(2,1)} %constant_dynamic-update-slice_fusion.9.rows_ref.left_ref), channel_id=1, source_target_pairs={{0,8},{8,0},{1,9},{9,1},{2,10},{10,2},{3,11},{11,3},{4,12},{12,4},... | collective-permute-start | bytes 12582920 | tf_op jit(solution)/shard_map/ppermute | solution.py:465
  414.0 48.7 %collective-permute-start.37 = (bf16[512,1024]{1,0:T(8,128)(2,1)S(1)}, bf16[512,1024]{1,0:T(8,128)(2,1)S(1)}, u32[]{:S(2)}, u32[]{:S(2)}) collective-permute-start(bf16[512,1024]{1,0:T(8,128)(2,1)S(1)} %pad_maximum_fusion.13), channel_id=1, source_target_pairs={{0,4},{4,0},{1,5},{5,1},{2,6},{6,2},{3,7},{7,3},{8,12},{12,8},{9,1... | collective-permute-start | bytes 3145736 | tf_op jit(solution)/shard_map/ppermute | solution.py:465
  414.9 47.8 %collective-permute-start.36 = (bf16[512,1024]{1,0:T(8,128)(2,1)S(1)}, bf16[512,1024]{1,0:T(8,128)(2,1)S(1)}, u32[]{:S(2)}, u32[]{:S(2)}) collective-permute-start(bf16[512,1024]{1,0:T(8,128)(2,1)S(1)} %pad_maximum_fusion.13), channel_id=1, source_target_pairs={{0,16},{16,0},{1,17},{17,1},{2,18},{18,2},{3,19},{19,3},{4,20},{20... | collective-permute-start | bytes 3145736 | tf_op jit(solution)/shard_map/ppermute | solution.py:465
  532.2 58.2 %collective-permute-start.47 = (bf16[1024,2048]{1,0:T(8,128)(2,1)}, bf16[1024,2048]{1,0:T(8,128)(2,1)}, u32[]{:S(2)}, u32[]{:S(2)}) collective-permute-start(bf16[1024,2048]{1,0:T(8,128)(2,1)} %shard_map.177), channel_id=1, source_target_pairs={{0,8},{8,0},{1,9},{9,1},{2,10},{10,2},{3,11},{11,3},{4,12},{12,4},... | collective-permute-start | bytes 12582920 | tf_op jit(solution)/shard_map/ppermute | solution.py:465
  541.5 69.3 %collective-permute-start.41 = (bf16[1024,2048]{1,0:T(8,128)(2,1)}, bf16[1024,2048]{1,0:T(8,128)(2,1)}, u32[]{:S(2)}, u32[]{:S(2)}) collective-permute-start(bf16[1024,2048]{1,0:T(8,128)(2,1)} %shard_map.175), channel_id=1, source_target_pairs={{0,8},{8,0},{1,9},{9,1},{2,10},{10,2},{3,11},{11,3},{4,12},{12,4},... | collective-permute-start | bytes 12582920 | tf_op jit(solution)/shard_map/ppermute | solution.py:465
  579.8 472.9 %reduce-scatter.3.cloned.1.call-start = ((), (), s32[]{:S(2)}) async-start(), calls=%async_computation.3 | async-start | bytes 10485760 | tf_op jit(solution)/shard_map/reduce_scatter | solution.py:547
  610.8 48.8 %collective-permute-start.50 = (bf16[256,2048]{1,0:T(8,128)(2,1)S(1)}, bf16[256,2048]{1,0:T(8,128)(2,1)}, u32[]{:S(2)}, u32[]{:S(2)}) collective-permute-start(bf16[256,2048]{1,0:T(8,128)(2,1)S(1)} %get-tuple-element.38), channel_id=1, source_target_pairs={{0,2},{2,0},{1,3},{3,1},{4,6},{6,4},{5,7},{7,5},{8,10},{10,8},{9,1... | collective-permute-start | bytes 3145736 | tf_op jit(solution)/shard_map/ppermute | solution.py:465
  623.7 60.3 %collective-permute-start.44 = (bf16[256,2048]{1,0:T(8,128)(2,1)S(1)}, bf16[256,2048]{1,0:T(8,128)(2,1)S(1)}, u32[]{:S(2)}, u32[]{:S(2)}) collective-permute-start(bf16[256,2048]{1,0:T(8,128)(2,1)S(1)} %get-tuple-element.42), channel_id=1, source_target_pairs={{0,2},{2,0},{1,3},{3,1},{4,6},{6,4},{5,7},{7,5},{8,10},{10,8},{9,1... | collective-permute-start | bytes 3145736 | tf_op jit(solution)/shard_map/ppermute | solution.py:465
  796.6 56.0 %collective-permute-start.58 = (bf16[1024,2048]{1,0:T(8,128)(2,1)}, bf16[1024,2048]{1,0:T(8,128)(2,1)}, u32[]{:S(2)}, u32[]{:S(2)}) collective-permute-start(bf16[1024,2048]{1,0:T(8,128)(2,1)} %constant_dynamic-update-slice_fusion.25.grad_ref.right_ref), channel_id=1, source_target_pairs={{0,8},{8,0},{1,9},{9,1},{2,10},{10,2},{3,11},{11,3},{4,12},{12,4},... | collective-permute-start | bytes 12582920 | tf_op jit(solution)/shard_map/ppermute | solution.py:465
  797.4 50.9 %collective-permute-start.46 = (bf16[128,2048]{1,0:T(8,128)(2,1)}, bf16[128,2048]{1,0:T(8,128)(2,1)}, u32[]{:S(2)}, u32[]{:S(2)}) collective-permute-start(bf16[128,2048]{1,0:T(8,128)(2,1)} %slice.368), channel_id=1, source_target_pairs={{0,4},{4,0},{1,5},{5,1},{2,6},{6,2},{3,7},{7,3},{8,12},{12,8},{9,1... | collective-permute-start | bytes 1572872 | tf_op jit(solution)/shard_map/ppermute | solution.py:465
  879.2 90.2 %collective-permute-start.59 = (bf16[1024,2048]{1,0:T(8,128)(2,1)}, bf16[1024,2048]{1,0:T(8,128)(2,1)}, u32[]{:S(2)}, u32[]{:S(2)}) collective-permute-start(bf16[1024,2048]{1,0:T(8,128)(2,1)} %shard_map.181), channel_id=1, source_target_pairs={{0,8},{8,0},{1,9},{9,1},{2,10},{10,2},{3,11},{11,3},{4,12},{12,4},... | collective-permute-start | bytes 12582920 | tf_op jit(solution)/shard_map/ppermute | solution.py:465
  969.3 58.4 %collective-permute-start.66 = (bf16[1024,384]{1,0:T(8,128)(2,1)S(1)}, bf16[1024,384]{1,0:T(8,128)(2,1)S(1)}, u32[]{:S(2)}, u32[]{:S(2)}) collective-permute-start(bf16[1024,384]{1,0:T(8,128)(2,1)S(1)} %fusion.17), channel_id=1, source_target_pairs={{0,4},{4,0},{1,5},{5,1},{2,6},{6,2},{3,7},{7,3},{8,12},{12,8},{9,1... | collective-permute-start | bytes 2359304 | tf_op jit(solution)/shard_map/ppermute | solution.py:465
  (109 other events, 2069.5 us)
Sparse Core Ops, SparseCore 0:
  203.6 161.9 all-gather.1
  579.9 85.2 reduce-scatter.4
  753.9 175.0 reduce-scatter.2

commit v2 on v1

--- a/solution.py
+++ b/solution.py
@@ -484,15 +484,22 @@
     return lax.dynamic_slice_in_dim(value, bit * size, size, axis)
 
 
-def split_column_weights(weights, c):
-    kept = jnp.concatenate([half(weight, c, 1) for weight in weights], axis=1)
-    sent = jnp.concatenate([half(weight, 1 - c, 1) for weight in weights], axis=1)
-    return join(kept, swap(sent, "c"), c, 0)
-
-
-def join_column_grads(total, c, counts):
-    other = swap(low_bits(half(total, 1 - c, 0)), "c")
-    kept = half(total, c, 0)
+def stage(sends, waits=()):
+    values, _ = lax.optimization_barrier((tuple(value for value, _ in sends), tuple(waits)))
+    return [swap(value, axis) for value, (_, axis) in zip(values, sends)]
+
+
+def both_halves(value, bit, axis):
+    return half(value, bit, axis), half(value, 1 - bit, axis)
+
+
+def column_halves(weights, c):
+    return tuple(
+        jnp.concatenate([half(weight, bit, 1) for weight in weights], axis=1) for bit in (c, 1 - c)
+    )
+
+
+def join_columns(kept, other, c, counts):
     grads, at = [], 0
     for count in counts:
         grads.append(join(wide_bits(kept[:, at : at + count]), wide_bits(other[:, at : at + count]), c, 1))
@@ -500,46 +507,15 @@
     return grads
 
 
-def split_row_weights(parts, spots):
-    _, _, span, columns = parts.shape
-    kept, other = half(parts, spots["c"], 1), half(parts, 1 - spots["c"], 1)
-    parts = join(kept[:, 0], swap(other, "c")[:, 0], spots["c"], 0).reshape(2, 2, span, columns)
-    kept, other = half(parts, spots["u"], 0), half(parts, 1 - spots["u"], 0)
-    parts = join(kept[0], swap(other, "u")[0], spots["u"], 2)
-    kept, other = half(parts, spots["v"], 0)[0], swap(half(parts, 1 - spots["v"], 0), "v")[0]
-    low = jnp.where(spots["v"] == 0, kept, other)
-    high = jnp.where(spots["v"] == 0, other, kept)
-    return jnp.concatenate(
-        [low[:, :columns], high[:, :columns], low[:, columns:], high[:, columns:]], axis=1
-    )
-
-
-def join_row_grads(total, spots):
-    total = low_bits(total)
-    span, columns = total.shape[0], total.shape[1] // 4
-    even = jnp.concatenate([total[:, :columns], total[:, 2 * columns : 3 * columns]], axis=1)
-    odd = jnp.concatenate([total[:, columns : 2 * columns], total[:, 3 * columns :]], axis=1)
-    kept = jnp.where(spots["v"] == 0, even, odd)
-    other = swap(jnp.where(spots["v"] == 0, odd, even), "v")
-    parts = join(kept[None], other[None], spots["v"], 0)
-    kept, other = half(parts, spots["u"], 2), half(parts, 1 - spots["u"], 2)
-    parts = join(kept[None], swap(other, "u")[None], spots["u"], 0)
-    kept, other = half(parts, spots["c"], 0), half(parts, 1 - spots["c"], 0)
-    return join(kept[0][:, None], swap(other, "c")[0][:, None], spots["c"], 1)
+def square(own, beside, across, both, spots):
+    first = join(own, across, spots["x"], 0)
+    second = join(beside, both, spots["x"], 0)
+    return join(first[None], second[None], spots["w"], 0)
 
 
 def spread(piece):
     rows, columns = piece.shape
     return lax.all_gather(piece, ("w", "x"), axis=0, tiled=True).reshape(2, 2 * rows, columns)
-
-
-def spread_by_pairs(piece, spots):
-    beside = swap(piece, "w")
-    across = swap(piece, "x")
-    both = swap(beside, "x")
-    own = join(piece, across, spots["x"], 0)
-    other = join(beside, both, spots["x"], 0)
-    return lax.optimization_barrier(join(own[None], other[None], spots["w"], 0))
 
 
 def collect(grad):
@@ -549,42 +525,49 @@
     )
 
 
-def collect_by_pairs(grad, spots):
-    kept, other = half(grad, spots["x"], 1), half(grad, 1 - spots["x"], 1)
-    total = wide_bits(kept) + wide_bits(swap(other, "x"))
-    kept, other = half(total, spots["w"], 0)[0], half(total, 1 - spots["w"], 0)[0]
-    return kept + wide_bits(swap(low_bits(other), "w"))
-
-
-def gather_rows(value):
-    size = value.shape[0] // 2
-    first, second = value[:size], value[size:]
-    first_u = swap(first, "u")
-    second_v = swap(second, "v")
-    first_v = swap(first, "v")
-    second_u = swap(second, "u")
-    first_uv = swap(first_u, "v")
-    second_uv = swap(second_v, "u")
-    own = jnp.concatenate(
-        [first, first_u, first_v, first_uv, second, second_v, second_u, second_uv], axis=0
-    )
-    return own, swap(own, "c")
-
-
-def scatter_rows(total):
+def weave(own, from_u, from_v, first_uv, second_uv):
+    size = own.shape[0] // 2
+    return jnp.concatenate(
+        [
+            own[:size],
+            from_u[:size],
+            from_v[:size],
+            first_uv,
+            own[size:],
+            from_v[size:],
+            from_u[size:],
+            second_uv,
+        ],
+        axis=0,
+    )
+
+
+def corners(from_u, from_v):
+    size = from_u.shape[0] // 2
+    return [(from_u[:size], "v"), (from_v[size:], "u")]
+
+
+def fold_sends(total):
     size = total.shape[0] // 8
-    first = total[: 4 * size]
-    second = total[4 * size :]
-    first = low_bits(wide_bits(first[: 2 * size]) + wide_bits(swap(first[2 * size :], "v")))
-    second = low_bits(wide_bits(second[: 2 * size]) + wide_bits(swap(second[2 * size :], "u")))
-    first = wide_bits(first[:size]) + wide_bits(swap(first[size:], "u"))
-    second = wide_bits(second[:size]) + wide_bits(swap(second[size:], "v"))
-    return jnp.concatenate([first, second], axis=0)
+    return [(total[2 * size : 4 * size], "v"), (total[6 * size :], "u")]
+
+
+def fold(total, from_v, from_u):
+    size = total.shape[0] // 8
+    first = wide_bits(total[: 2 * size]) + wide_bits(from_v)
+    second = wide_bits(total[4 * size : 6 * size]) + wide_bits(from_u)
+    kept = jnp.concatenate([first[:size], second[:size]], axis=0)
+    return kept, [(low_bits(first[size:]), "u"), (low_bits(second[size:]), "v")]
+
+
+def fold_end(kept, from_u, from_v):
+    return kept + jnp.concatenate([wide_bits(from_u), wide_bits(from_v)], axis=0)
 
 
 ACROSS = (((1,), (1,)), ((), ()))
 DOWN = (((0,), (0,)), ((), ()))
 CHUNK = 256
+TALL = 1024
 
 
 def dot(left, right, dims=(((1,), (0,)), ((), ()))):
@@ -593,6 +576,20 @@
 
 def whole(shape):
     return pl.BlockSpec(shape, lambda *_: (0,) * len(shape))
+
+
+def tie_kernel(value_ref, *refs):
+    refs[-1][...] = value_ref[...]
+
+
+def tie(value, *held):
+    return pl.pallas_call(
+        tie_kernel,
+        in_specs=[whole(value.shape), *[pl.BlockSpec(memory_space=pl.ANY) for _ in held]],
+        out_specs=whole(value.shape),
+        out_shape=jax.ShapeDtypeStruct(value.shape, value.dtype),
+        compiler_params=pltpu.CompilerParams(vmem_limit_bytes=48 * 2**20),
+    )(value, *held)
 
 
 def kernel_call(kernel, grid, in_specs, out_specs, out_shape, flops, size, scratch=()):
@@ -612,7 +609,8 @@
     return values * cosine + pltpu.roll(values, HEAD_DIM // 2, 1) * sine
 
 
-def attend_kernel(rows_ref, weight_ref, cos_ref, sin_ref, pos_col_ref, pos_row_ref, turned_ref, out_ref):
+def attend_kernel(rows_ref, weight_ref, cos_ref, sin_ref, pos_col_ref, pos_row_ref, *refs):
+    turned_ref, out_ref = refs[-2:]
     key_pos = pos_row_ref[...]
     rows = rows_ref.shape[0]
 
@@ -638,7 +636,7 @@
         out_ref[at, :] = low_bits(dot(low_bits(soft), turned_ref[:, 2 * HEAD_DIM :]))
 
 
-def attend(rows, weight, tables):
+def attend(rows, weight, tables, *held):
     count, width = rows.shape
     span = weight.shape[2]
     return kernel_call(
@@ -648,6 +646,7 @@
             whole(rows.shape),
             pl.BlockSpec((1, width, span), lambda h: (h, 0, 0)),
             *[whole(table.shape) for table in tables],
+            *[pl.BlockSpec(memory_space=pl.ANY) for _ in held],
         ],
         (
             pl.BlockSpec((count, span), lambda h: (0, h)),
@@ -659,12 +658,13 @@
         ),
         2 * count * width * 2 * span + 8 * count * count * HEAD_DIM * 3,
         count * width * 2 + weight.size * 2,
-    )(rows, weight, *tables)
+    )(rows, weight, *tables, *held)
 
 
 def attend_back_kernel(
-    grad_ref, weight_ref, turned_ref, cos_ref, sin_ref, pos_col_ref, pos_row_ref, out_ref, key_acc, value_acc
+    grad_ref, weight_ref, turned_ref, cos_ref, sin_ref, pos_col_ref, pos_row_ref, *refs
 ):
+    out_ref, key_acc, value_acc = refs[-3:]
     key_pos = pos_col_ref[...]
     rows, width = grad_ref.shape
     scale = HEAD_DIM ** (-0.5)
@@ -694,7 +694,7 @@
     out_ref[:, 2 * HEAD_DIM :] = low_bits(value_acc[...])
 
 
-def attend_back(grads, weight, turned, tables):
+def attend_back(grads, weight, turned, tables, *held):
     count, width = grads.shape
     span = turned.shape[1] // 2
     return kernel_call(
@@ -705,13 +705,14 @@
             pl.BlockSpec((2, HEAD_DIM, width // 2), lambda h: (0, h, 0)),
             pl.BlockSpec((count, span), lambda h: (0, h)),
             *[whole(table.shape) for table in tables],
+            *[pl.BlockSpec(memory_space=pl.ANY) for _ in held],
         ],
         pl.BlockSpec((count, span), lambda h: (0, h)),
         jax.ShapeDtypeStruct(turned.shape, jnp.bfloat16),
         2 * count * width * 2 * HEAD_DIM + 20 * count * count * HEAD_DIM * 2,
         count * width * 2 + turned.size * 4,
         [pltpu.VMEM((count, HEAD_DIM), jnp.float32)] * 2,
-    )(grads, weight, turned, *tables)
+    )(grads, weight, turned, *tables, *held)
 
 
 def hidden_kernel(rows_ref, grad_ref, wide_ref, down_ref, hidden_ref, out_ref):
@@ -759,48 +760,53 @@
     )(rows, grads, wide, down)
 
 
-def back_kernel(added, left_ref, weight_ref, *refs):
+def back_kernel(counts, *refs):
     out_ref = refs[-1]
-    rows, depth = left_ref.shape
-
-    @pl.loop(0, rows // CHUNK)
+    pairs, more = counts
+    lefts, weights = refs[:pairs], refs[pairs : 2 * pairs]
+    added = refs[2 * pairs : 2 * pairs + more]
+    rows, depth = lefts[0].shape
+
+    @pl.loop(0, rows // TALL)
     def _(i):
-        at = pl.ds(pl.multiple_of(i * CHUNK, CHUNK), CHUNK)
-        total = dot(left_ref[at, : depth // 2], weight_ref[0], ACROSS) + dot(
-            left_ref[at, depth // 2 :], weight_ref[1], ACROSS
-        )
-        if added:
-            total += wide_bits(refs[0][at, :])
+        at = pl.ds(pl.multiple_of(i * TALL, TALL), TALL)
+        total = sum(
+            dot(left_ref[at, : depth // 2], weight_ref[0], ACROSS)
+            + dot(left_ref[at, depth // 2 :], weight_ref[1], ACROSS)
+            for left_ref, weight_ref in zip(lefts, weights)
+        )
+        for added_ref in added:
+            total += wide_bits(added_ref[at, :])
         out_ref[at, :] = low_bits(total)
 
 
-def back_rows(left, weight, added=None):
-    count, depth = left.shape
-    width = weight.shape[1]
+def back_rows(lefts, weights, added=(), held=()):
+    count, depth = lefts[0].shape
+    width = weights[0].shape[1]
     tile = 256
-    more = [] if added is None else [added]
     return kernel_call(
-        functools.partial(back_kernel, len(more)),
+        functools.partial(back_kernel, (len(lefts), len(added))),
         (width // tile,),
         [
-            whole(left.shape),
-            pl.BlockSpec((2, tile, depth // 2), lambda i: (0, i, 0)),
-            *[pl.BlockSpec((count, tile), lambda i: (0, i)) for _ in more],
+            *[whole(left.shape) for left in lefts],
+            *[pl.BlockSpec((2, tile, depth // 2), lambda i: (0, i, 0)) for _ in weights],
+            *[pl.BlockSpec((count, tile), lambda i: (0, i)) for _ in added],
+            *[pl.BlockSpec(memory_space=pl.ANY) for _ in held],
         ],
         pl.BlockSpec((count, tile), lambda i: (0, i)),
         jax.ShapeDtypeStruct((count, width), jnp.bfloat16),
-        2 * count * width * depth,
-        count * (width + depth) * 2 + weight.size * 2,
-    )(left, weight, *more)
+        2 * count * width * depth * len(lefts),
+        len(lefts) * (count * (width + depth) * 2 + weights[0].size * 2),
+    )(*lefts, *weights, *added, *held)
 
 
 def ahead_kernel(added, left_ref, weight_ref, *refs):
     out_ref = refs[-1]
     rows = left_ref.shape[0]
 
-    @pl.loop(0, rows // CHUNK)
+    @pl.loop(0, rows // TALL)
     def _(i):
-        at = pl.ds(pl.multiple_of(i * CHUNK, CHUNK), CHUNK)
+        at = pl.ds(pl.multiple_of(i * TALL, TALL), TALL)
         total = dot(left_ref[at, :], weight_ref[0])
         if added:
             total += wide_bits(refs[0][at, :])
@@ -884,100 +890,185 @@
 ):
     tok_rows = tokens.shape[1]
     spots = {name: lax.axis_index(name) for name in PAIRS}
+    c, w, x, u, v = (spots[name] for name in ("c", "w", "x", "u", "v"))
     tables = row_tables(tok_rows // 2, 8, spots)
-
-    def own_sequence(stored):
-        other = swap(half(stored, 1 - spots["w"], 0), "w")
-        return jnp.concatenate([half(stored, spots["w"], 0)[0], other[0]], axis=0)
-
-    def stored_slots(rows):
-        other = swap(low_bits(rows[tok_rows:]), "w").astype(rows.dtype)
-        return join(rows[None, :tok_rows], other[None], spots["w"], 0)
-
-    live = (spots["w"] < counts[0]).astype(jnp.float32)
-    token_rows = own_sequence(tokens)
-    grad_rows = own_sequence(cotangent)
-
-    columns = split_column_weights(
-        [query_weight, key_weight, value_weight, gate_weight, up_weight], spots["c"]
-    )
+    live = (w < counts[0]).astype(jnp.float32)
     tile = 256
     head_columns = 3 * HEAD_DIM
-    full_qkv = spread_by_pairs(columns[:, :head_columns], spots)
-    gate_at, up_at = head_columns, head_columns + gate_weight.shape[1] // 2
-    wide = jnp.concatenate(
+    wide_columns = gate_weight.shape[1] // 2
+    output_span, down_span = output_weight.shape[0] // 4, down_weight.shape[0] // 4
+
+    token_kept, token_sent = both_halves(tokens, w, 0)
+    cotangent_kept, cotangent_sent = both_halves(cotangent, w, 0)
+    columns_kept, columns_sent = column_halves(
+        [query_weight, key_weight, value_weight, gate_weight, up_weight], c
+    )
+    parts = jnp.concatenate(
+        [output_weight.reshape(2, 2, output_span, -1), down_weight.reshape(2, 2, down_span, -1)],
+        axis=2,
+    )
+    parts_kept, parts_sent = both_halves(parts, v, 0)
+    token_got, columns_got, parts_got = (
+        swap(token_sent[0], "w"),
+        swap(columns_sent, "c"),
+        swap(parts_sent[0], "v"),
+    )
+    inputs = wide_bits(jnp.concatenate([token_kept[0], token_got], axis=0))
+    normed_in, norm_in_back = jax.vjp(layer_norm, inputs)
+    norm_own = low_bits(normed_in)
+    columns = join(columns_kept, columns_got, c, 0)
+    qkv_piece = columns[:, :head_columns]
+    wide_piece = jnp.concatenate(
         [
             columns[:, at + start : at + start + tile]
-            for start in range(0, up_at - gate_at, tile)
-            for at in (gate_at, up_at)
+            for start in range(0, wide_columns, tile)
+            for at in (head_columns, head_columns + wide_columns)
         ],
         axis=1,
     )
-    full_wide = spread(wide)
-    output_span, down_span = output_weight.shape[0] // 4, down_weight.shape[0] // 4
-    rows = split_row_weights(
-        jnp.concatenate(
-            [
-                output_weight.reshape(2, 2, output_span, -1),
-                down_weight.reshape(2, 2, down_span, -1),
-            ],
-            axis=2,
-        ),
-        spots,
-    )
-    full_output = spread_by_pairs(rows[:output_span], spots)
-    full_down = spread_by_pairs(rows[output_span:], spots)
-
-    inputs = token_rows.astype(jnp.float32)
-    normed_in, norm_in_back = jax.vjp(layer_norm, inputs)
-    norm_in = gather_rows(low_bits(normed_in))
-    turned, attended = zip(*[attend(part, full_qkv, tables) for part in norm_in])
-    other = swap(ahead_rows(attended[1], full_output), "c")
-    after_attn = inputs + scatter_rows(ahead_rows(attended[0], full_output, other))
+    full_wide = spread(wide_piece)
+    parts = join(parts_kept[0], parts_got, v, 2)
+    parts_kept, parts_sent = both_halves(parts, c, 0)
+    norm_u, norm_v, qkv_w, qkv_x, parts_got = stage(
+        [(norm_own, "u"), (norm_own, "v"), (qkv_piece, "w"), (qkv_piece, "x"), (parts_sent[0], "c")]
+    )
+    parts = join(parts_kept, parts_got[None], c, 0)
+    parts_kept, parts_sent = both_halves(parts, u, 0)
+    norm_uv, qkv_wx, parts_got, cotangent_got = stage(
+        [(norm_u, "v"), (qkv_w, "x"), (parts_sent[0], "u"), (cotangent_sent[0], "w")], [norm_v, qkv_x]
+    )
+    norm_in = weave(norm_own, norm_u, norm_v, norm_uv[:tok_rows], norm_uv[tok_rows:])
+    full_qkv = square(qkv_piece, qkv_w, qkv_x, qkv_wx, spots)
+    parts = join(parts_kept[0], parts_got, u, 1)
+    output_piece, down_piece = parts[:output_span], parts[output_span:]
+    grad_out = wide_bits(jnp.concatenate([cotangent_kept[0], cotangent_got], axis=0)) * live
+    grad_own = low_bits(grad_out)
+
+    norm_other, output_w, output_x = stage(
+        [(norm_in, "c"), (output_piece, "w"), (output_piece, "x")], [qkv_wx, cotangent_got]
+    )
+    grad_u, grad_v = stage([(grad_own, "u"), (grad_own, "v")], [qkv_wx])
+    first = attend(norm_in, full_qkv, tables)
+    second = attend(norm_other, full_qkv, tables)
+    output_wx, grad_uv, down_x, down_w = stage(
+        [(output_w, "x"), (grad_u, "v"), (down_piece, "x"), (down_piece, "w")],
+        [output_x, grad_v, first[0], second[0]],
+    )
+    norm_in = (norm_in, norm_other)
+    turned, attended = zip(first, second)
+    full_output = square(output_piece, output_w, output_x, output_wx, spots)
+    grad_all = weave(grad_own, grad_u, grad_v, grad_uv[:tok_rows], grad_uv[tok_rows:])
+    (other,) = stage([(ahead_rows(attended[1], full_output), "c")])
+    total = ahead_rows(attended[0], full_output, other)
+    from_v, from_u = stage(fold_sends(total))
+    (grad_other,) = stage([(grad_all, "c")], [other])
+    grad_all = (grad_all, grad_other)
+    kept, sends = fold(total, from_v, from_u)
+    from_u, from_v = stage(sends, [down_x])
+    (down_wx,) = stage([(down_w, "x")], [from_u])
+    full_down = square(down_piece, down_w, down_x, down_wx, spots)
+    after_attn = inputs + fold_end(kept, from_u, from_v)
     normed_mid, norm_mid_back = jax.vjp(layer_norm, after_attn)
-
-    norm_mid = gather_rows(low_bits(normed_mid))
-    grad_out = grad_rows.astype(jnp.float32) * live
-    grad_all = gather_rows(low_bits(grad_out))
+    mid_own = low_bits(normed_mid)
+    mid_u, mid_v = stage([(mid_own, "u"), (mid_own, "v")])
+    mid_uv, mid_vu = stage(corners(mid_u, mid_v), [grad_other, down_wx])
+    mid_uv = tie(mid_uv, full_wide)
+    norm_mid = weave(mid_own, mid_u, mid_v, mid_uv, mid_vu)
+    norm_mid = (norm_mid, swap(norm_mid, "c"))
+
     hidden, grad_wide = zip(
-        *[hidden_pass(part, grads, full_wide, full_down, tile) for part, grads in zip(norm_mid, grad_all)]
-    )
-    other = swap(back_rows(grad_wide[1], full_wide), "c")
-    down_total = collect(outer_rows(hidden, grad_all))
-    grad_norm_mid = scatter_rows(back_rows(grad_wide[0], full_wide, other))
-    wide_total = collect(outer_rows(norm_mid, grad_wide))
-    other = swap(ahead_rows(hidden[1], full_down), "c")
-    layer_out = after_attn + scatter_rows(ahead_rows(hidden[0], full_down, other))
-    mixed = low_bits(layer_out * live)
+        *[hidden_pass(rows, grads, full_wide, full_down, tile) for rows, grads in zip(norm_mid, grad_all)]
+    )
+    (other,) = stage([(back_rows([grad_wide[1]], [full_wide]), "c")], [grad_wide[0]])
+    wide_outer = outer_rows(norm_mid, grad_wide)
+    wide_total = collect(wide_outer)
+    other, _ = lax.optimization_barrier((other, wide_outer))
+    total = back_rows([grad_wide[0]], [full_wide], [other])
+    from_v, from_u = stage(fold_sends(total))
+    down_outer = outer_rows(hidden, grad_all)
+    down_kept, down_sent = both_halves(down_outer, x, 1)
+    kept, sends = fold(total, from_v, from_u)
+    from_u, from_v = stage(sends, [down_outer])
+    (down_got,) = stage([(down_sent, "x")], [from_u])
+    ahead = ahead_rows(hidden[1], full_down)
+    grad_norm_mid = fold_end(kept, from_u, from_v)
     grad_after = grad_out + norm_mid_back(grad_norm_mid)[0]
-
-    after_all = gather_rows(low_bits(grad_after))
-    grad_qkv = [
-        attend_back(part, full_output, kept, tables) for kept, part in zip(turned, after_all)
-    ]
-    other = swap(back_rows(grad_qkv[1], full_qkv), "c")
-    grad_norm_in = scatter_rows(back_rows(grad_qkv[0], full_qkv, other))
+    after_own = low_bits(grad_after)
+    after_u, after_v, other = stage([(after_own, "u"), (after_own, "v"), (ahead, "c")])
+    after_uv, after_vu = stage(corners(after_u, after_v), [other])
+    total = ahead_rows(hidden[0], full_down, other)
+    after_uv, after_vu, total = lax.optimization_barrier((after_uv, after_vu, total))
+    after_all = weave(after_own, after_u, after_v, after_uv, after_vu)
+
+    down_sum = wide_bits(down_kept) + wide_bits(down_got)
+    down_kept, down_sent = both_halves(down_sum, w, 0)
+    (after_other,) = stage([(after_all, "c")])
+    from_v, from_u = stage(fold_sends(total), [after_uv])
+    (down_got,) = stage([(low_bits(down_sent[0]), "w")], [after_other])
+    after_all = (after_all, after_other)
+    first = attend_back(after_all[0], full_output, turned[0], tables)
+    kept, sends = fold(total, from_v, from_u)
+    from_u, from_v = stage(sends, [first, after_other])
+    second = attend_back(after_other, full_output, turned[1], tables, wide_total)
+    grad_qkv = (first, second)
+    ahead = back_rows([second], [full_qkv])
+    qkv_outer = outer_rows(norm_in, grad_qkv)
+    mixed = low_bits((after_attn + fold_end(kept, from_u, from_v)) * live)
+    (other,) = stage([(ahead, "c")])
+    other, qkv_outer = lax.optimization_barrier((other, qkv_outer))
+    (mixed_got,) = stage([(mixed[tok_rows:], "w")], [other, down_got])
+    output_outer = outer_rows(attended, after_all)
+    total = back_rows([first], [full_qkv], [other])
+    qkv_kept, qkv_sent = both_halves(qkv_outer, x, 1)
+    output_kept, output_sent = both_halves(output_outer, x, 1)
+    from_v, from_u, qkv_got = stage(fold_sends(total) + [(qkv_sent, "x")], [mixed])
+    qkv_sum = wide_bits(qkv_kept) + wide_bits(qkv_got)
+    qkv_kept, qkv_sent = both_halves(qkv_sum, w, 0)
+    kept, sends = fold(total, from_v, from_u)
+    from_u, from_v, qkv_got, output_got = stage(
+        sends + [(low_bits(qkv_sent[0]), "w"), (output_sent, "x")], [mixed_got]
+    )
+    grad_norm_in = fold_end(kept, from_u, from_v)
     token_grad = grad_after + norm_in_back(grad_norm_in)[0]
-    output_total = collect_by_pairs(outer_rows(attended, after_all), spots)
-    qkv_total = collect_by_pairs(outer_rows(norm_in, grad_qkv), spots)
-
-    wide_parts = [wide_total[:, at : at + tile] for at in range(0, wide_total.shape[1], tile)]
+    output_sum = wide_bits(output_kept) + wide_bits(output_got)
+    output_kept, output_sent = both_halves(output_sum, w, 0)
+    token_got, output_got = stage(
+        [(low_bits(token_grad[tok_rows:]), "w"), (low_bits(output_sent[0]), "w")]
+    )
+    down_kept, down_got, wide_total, _ = lax.optimization_barrier(
+        (down_kept, down_got, wide_total, from_u)
+    )
+    down_total = low_bits(down_kept[0] + wide_bits(down_got))
+    qkv_total = qkv_kept[0] + wide_bits(qkv_got)
+    output_total = low_bits(output_kept[0] + wide_bits(output_got))
+
+    wide_parts = [wide_total[:, at : at + tile] for at in range(0, 2 * wide_columns, tile)]
     wide_total = jnp.concatenate(wide_parts[0::2] + wide_parts[1::2], axis=1)
-    span = wide_total.shape[1] // 2
-    gate_grad, up_grad = join_column_grads(wide_total, spots["c"], (span, span))
-    query_grad, key_grad, value_grad = join_column_grads(qkv_total, spots["c"], (HEAD_DIM,) * 3)
-    output_grad = join_row_grads(output_total, spots)
-    down_grad = join_row_grads(down_total, spots)
+
+    def columns_home(total, sizes):
+        kept, sent = both_halves(total, c, 0)
+        return join_columns(kept, swap(low_bits(sent), "c"), c, sizes)
+
+    def rows_home(total):
+        kept, sent = both_halves(total, u, 1)
+        parts = join(kept[None], swap(sent, "u")[None], u, 0)
+        kept, sent = both_halves(parts, c, 0)
+        parts = join(kept, swap(sent, "c"), c, 0)
+        kept, sent = both_halves(parts, v, 2)
+        return wide_bits(join(kept[None], swap(sent, "v")[None], v, 0))
+
+    gate_grad, up_grad = columns_home(wide_total, (wide_columns,) * 2)
+    query_grad, key_grad, value_grad = columns_home(qkv_total, (HEAD_DIM,) * 3)
     return (
-        stored_slots(mixed),
-        stored_slots(token_grad),
+        join(mixed[None, :tok_rows], mixed_got[None], w, 0),
+        join(token_grad[None, :tok_rows], wide_bits(token_got)[None], w, 0),
         query_grad,
         key_grad,
         value_grad,
-        wide_bits(output_grad.reshape(output_weight.shape)),
+        rows_home(output_total).reshape(output_weight.shape),
         gate_grad,
         up_grad,
-        wide_bits(down_grad.reshape(down_weight.shape)),
+        rows_home(down_total).reshape(down_weight.shape),
     )
 
 

time: 1100 us -> 935 us (0.85)
  waiting for transfers between devices: 617 us -> 471 us
  Pallas kernels: 263 us -> 240 us
  local copies, waits for them, and re-layouts: 54.8 us -> 66.9 us
    ppermute x77 -> x69, waiting for transfers between devices: 617 us -> 471 us  [swap(): return lax.ppermute(value, axis, SWAP)]
    pallas_call x4 -> x5, Pallas kernels: 60.6 us -> 45.4 us  [the longest x4 45.3 us: back_rows(): kernel_call(functools.partial(back_kernel, (len(lefts), len(added))), (wi...]
    unnamed x134 -> x228, local copies, waits for them, and re-layouts: 31.9 us -> 42.5 us
    ppermute x77 -> x69, starting transfers between devices: 67.6 us -> 72.7 us  [swap(): return lax.ppermute(value, axis, SWAP)]
  transfers between devices with their start and end apart: 80 -> 71, of which waited for: 34 -> 32; matrix products, arithmetic and copies ran while one was open for 9% -> 10% of each run, Pallas kernels for 19% -> 20%
where the time goes in v2:
time: 935 us; the launch traced here: 926 us
  waiting for transfers between devices  471 us (50%)
  Pallas kernels  240 us (26%)
  starting transfers between devices  72.8 us (8%)
  local copies, waits for them, and re-layouts  66.9 us (7%)
  other arithmetic  57.6 us (6%)
  between operations  17.1 us (2%)
    ppermute x69, waiting for transfers between devices, swap(): return lax.ppermute(value, axis, SWAP)  471 us
    ppermute x69, starting transfers between devices, swap(): return lax.ppermute(value, axis, SWAP)  72.7 us
    pallas_call x4, Pallas kernels, outer_rows(): kernel_call(outer_kernel, (2, depth // tile), [left_spec, left_spec, righ...  65.4 us
    pallas_call x4, Pallas kernels, back_rows(): kernel_call(functools.partial(back_kernel, (len(lefts), len(added))), (wi...  45.3 us
    pallas_call x2, Pallas kernels, hidden_pass(): kernel_call(hidden_kernel, (2, tiles), [whole(rows.shape), whole(grads.sh...  43.8 us
    unnamed x228, local copies, waits for them, and re-layouts  42.5 us
    pallas_call x2, Pallas kernels, attend(): kernel_call(attend_kernel, (2,), [whole(rows.shape), pl.BlockSpec((1, wid...  32.5 us
    pallas_call x2, Pallas kernels, attend_back(): kernel_call(attend_back_kernel, (2,), [whole(grads.shape), pl.BlockSpec((...  30.8 us
  transfers between devices with their start and end apart: 71, of which 32 were waited for; matrix products, arithmetic and copies ran while one was open for 10% of the time, Pallas kernels for 20%

profile of v2, /device:TPU:0, one launch (start us, length us, event | category | flops | bytes accessed | tf_op | source)
XLA Modules:
  0.0 925.6 jit_solution(4402865901560852346)
XLA Ops:
  21.8 15.0 %collective-permute-done = bf16[128,2048]{1,0:T(8,128)(2,1)S(1)} collective-permute-done((bf16[128,2048]{1,0:T(8,128)(2,1)}, bf16[128,2048]{1,0:T(8,128)(2,1)S(1)}, u32[]{:S(2)}, u32[]{:S(2)}) %collective-permute-start) | collective-permute-done | bytes 524320 | tf_op jit(solution)/shard_map/ppermute | solution.py:465
  49.2 32.1 %collective-permute-done.5 = bf16[1024,384]{1,0:T(8,128)(2,1)S(1)} collective-permute-done((bf16[1024,384]{1,0:T(8,128)(2,1)S(1)}, bf16[1024,384]{1,0:T(8,128)(2,1)S(1)}, u32[]{:S(2)}, u32[]{:S(2)}) %collective-permute-start.5) | collective-permute-done | bytes 786464 | tf_op jit(solution)/shard_map/ppermute | solution.py:465
  91.8 18.5 %collective-permute-done.10 = bf16[640,512]{1,0:T(8,128)(2,1)S(1)} collective-permute-done((bf16[640,512]{1,0:T(8,128)(2,1)S(1)}, bf16[640,512]{1,0:T(8,128)(2,1)S(1)}, u32[]{:S(2)}, u32[]{:S(2)}) %collective-permute-start.10) | collective-permute-done | bytes 655392 | tf_op jit(solution)/shard_map/ppermute | solution.py:465
  135.9 16.0 %shard_map.169 = (bf16[1024,768]{1,0:T(8,128)(2,1)S(1)}, bf16[1024,256]{1,0:T(8,128)(2,1)S(1)}) custom-call(bf16[1024,2048]{1,0:T(8,128)(2,1)} %slice_dynamic-update-slice_fusion.16.rows_ref.left_ref, bf16[2,2048,384]{2,1,0:T(8,128)(2,1)} %pad_maximum_fusion.1.weight_ref.refs_1_, f32[1024,128]{1,0:T(8,128)S(1)} %get-tuple-element.257.cos_ref, ...), custom_call_target="tpu_custom_call" | custom-call | flops 6442450944 | bytes 7340032 | tf_op jit(solution)/shard_map/pallas_call | solution.py:642
  151.9 16.5 %shard_map.170 = (bf16[1024,768]{1,0:T(8,128)(2,1)S(1)}, bf16[1024,256]{1,0:T(8,128)(2,1)S(1)}) custom-call(bf16[1024,2048]{1,0:T(8,128)(2,1)} %collective-permute-done.16.rows_ref.left_other_ref, bf16[2,2048,384]{2,1,0:T(8,128)(2,1)} %pad_maximum_fusion.1.weight_ref.refs_1_, f32[1024,128]{1,0:T(8,128)S(1)} %get-tuple-element.257.cos_ref, ...), custom_call_target="tpu_custom_call" | custom-call | flops 6442450944 | bytes 7340032 | tf_op jit(solution)/shard_map/pallas_call | solution.py:642
  192.2 21.1 %collective-permute-done.26 = bf16[256,2048]{1,0:T(8,128)(2,1)S(1)} collective-permute-done((bf16[256,2048]{1,0:T(8,128)(2,1)}, bf16[256,2048]{1,0:T(8,128)(2,1)S(1)}, u32[]{:S(2)}, u32[]{:S(2)}) %collective-permute-start.26) | collective-permute-done | bytes 1048608 | tf_op jit(solution)/shard_map/ppermute | solution.py:465
  230.4 16.5 %collective-permute-done.19 = bf16[256,2048]{1,0:T(8,128)(2,1)S(1)} collective-permute-done((bf16[256,2048]{1,0:T(8,128)(2,1)S(1)}, bf16[256,2048]{1,0:T(8,128)(2,1)S(1)}, u32[]{:S(2)}, u32[]{:S(2)}) %collective-permute-start.19) | collective-permute-done | bytes 1048608 | tf_op jit(solution)/shard_map/ppermute | solution.py:465
  246.9 46.6 %collective-permute-done.20 = bf16[256,2048]{1,0:T(8,128)(2,1)S(1)} collective-permute-done((bf16[256,2048]{1,0:T(8,128)(2,1)S(1)}, bf16[256,2048]{1,0:T(8,128)(2,1)S(1)}, u32[]{:S(2)}, u32[]{:S(2)}) %collective-permute-start.20) | collective-permute-done | bytes 1048608 | tf_op jit(solution)/shard_map/ppermute | solution.py:465
  298.5 19.5 %collective-permute-done.22 = bf16[128,2048]{1,0:T(8,128)(2,1)S(1)} collective-permute-done((bf16[128,2048]{1,0:T(8,128)(2,1)S(1)}, bf16[128,2048]{1,0:T(8,128)(2,1)S(1)}, u32[]{:S(2)}, u32[]{:S(2)}) %collective-permute-start.22) | collective-permute-done | bytes 524320 | tf_op jit(solution)/shard_map/ppermute | solution.py:465
  319.9 22.9 %collective-permute-done.28 = bf16[512,1024]{1,0:T(8,128)(2,1)S(1)} collective-permute-done((bf16[512,1024]{1,0:T(8,128)(2,1)S(1)}, bf16[512,1024]{1,0:T(8,128)(2,1)S(1)}, u32[]{:S(2)}, u32[]{:S(2)}) %collective-permute-start.28) | collective-permute-done | bytes 1048608 | tf_op jit(solution)/shard_map/ppermute | solution.py:465
  388.4 21.9 %shard_map.174 = (bf16[1024,1024]{1,0:T(8,128)(2,1)S(1)}, bf16[1024,2048]{1,0:T(8,128)(2,1)}) custom-call(bf16[1024,2048]{1,0:T(8,128)(2,1)} %copy-done.21, bf16[1024,2048]{1,0:T(8,128)(2,1)} %slice_dynamic-update-slice_fusion.6.grad_ref.right_ref, bf16[2,2048,1024]{2,1,0:T(8,128)(2,1)} %bitcast.113, bf16[2,1024,1024]{2,1,0:T(8,128)(2,1)} %pad_maximum_fusion.down_ref.weight_ref), custom_call_target="tpu_custom_call" | custom-call | flops 12884901888 | bytes 29360128 | tf_op jit(solution)/shard_map/pallas_call | solution.py:741
  410.3 22.0 %shard_map.175 = (bf16[1024,1024]{1,0:T(8,128)(2,1)S(1)}, bf16[1024,2048]{1,0:T(8,128)(2,1)}) custom-call(bf16[1024,2048]{1,0:T(8,128)(2,1)} %collective-permute-done.32.rows_ref.left_other_ref, bf16[1024,2048]{1,0:T(8,128)(2,1)} %copy-done.96, bf16[2,2048,1024]{2,1,0:T(8,128)(2,1)} %bitcast.114, bf16[2,1024,1024]{2,1,0:T(8,128)(2,1)} %pad_maximum_fusion.down_ref.weight_ref), custom_call_target="tpu_custom_call" | custom-call | flops 12884901888 | bytes 29360128 | tf_op jit(solution)/shard_map/pallas_call | solution.py:741
  433.5 14.7 %shard_map.176 = bf16[1024,2048]{1,0:T(8,128)(2,1)} custom-call(bf16[1024,2048]{1,0:T(8,128)(2,1)} %get-tuple-element.113.refs_0_.right_other_ref, bf16[2,2048,1024]{2,1,0:T(8,128)(2,1)} %bitcast.115), custom_call_target="tpu_custom_call" | custom-call | flops 8589934592 | bytes 16777216 | tf_op jit(solution)/shard_map/pallas_call | solution.py:787
  448.3 26.7 %shard_map.177 = bf16[2,2048,1024]{2,1,0:T(8,128)(2,1)} custom-call(bf16[1024,2048]{1,0:T(8,128)(2,1)S(1)} %copy-done.22, bf16[1024,2048]{1,0:T(8,128)(2,1)} %collective-permute-done.32.rows_ref.left_other_ref, bf16[1024,2048]{1,0:T(8,128)(2,1)} %get-tuple-element.112.right_ref.refs_0_, bf16[1024,2048]{1,0:T(8,128)(2,1)} %get-tuple-element.113.refs_0_.right_other_ref), custom_call_target="tpu_custom_call" | custom-call | flops 17179869184 | bytes 25165824 | tf_op jit(solution)/shard_map/pallas_call | solution.py:849
  490.5 15.3 %shard_map.179 = bf16[2,1024,1024]{2,1,0:T(8,128)(2,1)} custom-call(bf16[1024,1024]{1,0:T(8,128)(2,1)S(1)} %get-tuple-element.118.left_ref, bf16[1024,1024]{1,0:T(8,128)(2,1)S(1)} %copy-done.26, bf16[1024,2048]{1,0:T(8,128)(2,1)} %slice_dynamic-update-slice_fusion.6.grad_ref.right_ref, bf16[1024,2048]{1,0:T(8,128)(2,1)} %copy-done.96), custom_call_target="tpu_custom_call" | custom-call | flops 8589934592 | bytes 16777216 | tf_op jit(solution)/shard_map/pallas_call | solution.py:849
  514.9 23.0 %collective-permute-done.35 = bf16[256,2048]{1,0:T(8,128)(2,1)S(1)} collective-permute-done((bf16[256,2048]{1,0:T(8,128)(2,1)S(1)}, bf16[256,2048]{1,0:T(8,128)(2,1)S(1)}, u32[]{:S(2)}, u32[]{:S(2)}) %collective-permute-start.35) | collective-permute-done | bytes 1048608 | tf_op jit(solution)/shard_map/ppermute | solution.py:465
  548.1 16.4 %collective-permute-done.36 = bf16[128,2048]{1,0:T(8,128)(2,1)S(1)} collective-permute-done((bf16[128,2048]{1,0:T(8,128)(2,1)S(1)}, bf16[128,2048]{1,0:T(8,128)(2,1)S(1)}, u32[]{:S(2)}, u32[]{:S(2)}) %collective-permute-start.36) | collective-permute-done | bytes 524320 | tf_op jit(solution)/shard_map/ppermute | solution.py:465
  569.5 37.6 %collective-permute-done.38 = bf16[256,2048]{1,0:T(8,128)(2,1)S(1)} collective-permute-done((bf16[256,2048]{1,0:T(8,128)(2,1)S(1)}, bf16[256,2048]{1,0:T(8,128)(2,1)S(1)}, u32[]{:S(2)}, u32[]{:S(2)}) %collective-permute-start.38) | collective-permute-done | bytes 1048608 | tf_op jit(solution)/shard_map/ppermute | solution.py:465
  650.8 15.4 %shard_map.183.refs_0_.right_other_ref = bf16[1024,768]{1,0:T(8,128)(2,1)S(1)} custom-call(bf16[1024,2048]{1,0:T(8,128)(2,1)} %collective-permute-done.45.grad_ref.right_other_ref, bf16[2,256,1024]{2,1,0:T(8,128)(2,1)S(1)} %copy-done.2, bf16[1024,768]{1,0:T(8,128)(2,1)S(1)} %copy-done.28, f32[1024,128]{1,0:T(8,128)S(1)} %copy-done.11, ...), custom_call_target="tpu_custom_call" | custom-call | flops 6442450944 | bytes 7340032 | tf_op jit(solution)/shard_map/pallas_call | solution.py:700
  680.2 15.5 %shard_map.182.right_ref.refs_0_ = bf16[1024,768]{1,0:T(8,128)(2,1)S(1)} custom-call(bf16[1024,2048]{1,0:T(8,128)(2,1)} %copy-done.56, bf16[2,256,1024]{2,1,0:T(8,128)(2,1)S(1)} %copy-done.3, bf16[1024,768]{1,0:T(8,128)(2,1)S(1)} %copy-done.30, f32[1024,128]{1,0:T(8,128)S(1)} %copy-done.12, f32[1024,128]{1,0:T(8,128)S(1)} %copy-done.15, ...), custom_call_target="tpu_custom_call" | custom-call | flops 6442450944 | bytes 7340032 | tf_op jit(solution)/shard_map/pallas_call | solution.py:700
  735.3 18.3 %shard_map.185 = bf16[2,2048,384]{2,1,0:T(8,128)(2,1)} custom-call(bf16[1024,2048]{1,0:T(8,128)(2,1)} %slice_dynamic-update-slice_fusion.16.rows_ref.left_ref, bf16[1024,2048]{1,0:T(8,128)(2,1)} %collective-permute-done.16.rows_ref.left_other_ref, bf16[1024,768]{1,0:T(8,128)(2,1)S(1)} %copy-done.9, bf16[1024,768]{1,0:T(8,128)(2,1)S(1)} %copy-done.24), custom_call_target="tpu_custom_call" | custom-call | flops 6442450944 | bytes 14680064 | tf_op jit(solution)/shard_map/pallas_call | solution.py:849
  792.5 20.2 %collective-permute-done.53 = bf16[256,2048]{1,0:T(8,128)(2,1)} collective-permute-done((bf16[256,2048]{1,0:T(8,128)(2,1)}, bf16[256,2048]{1,0:T(8,128)(2,1)}, u32[]{:S(2)}, u32[]{:S(2)}) %collective-permute-start.53) | collective-permute-done | bytes 1048608 | tf_op jit(solution)/shard_map/ppermute | solution.py:465
  846.2 24.1 %collective-permute-done.61 = bf16[128,1024]{1,0:T(8,128)(2,1)S(1)} collective-permute-done((bf16[128,1024]{1,0:T(8,128)(2,1)S(1)}, bf16[128,1024]{1,0:T(8,128)(2,1)S(1)}, u32[]{:S(2)}, u32[]{:S(2)}) %collective-permute-start.61) | collective-permute-done | bytes 262176 | tf_op jit(solution)/shard_map/ppermute | solution.py:465
  879.6 17.6 %collective-permute-done.58 = bf16[128,2048]{1,0:T(8,128)(2,1)S(1)} collective-permute-done((bf16[128,2048]{1,0:T(8,128)(2,1)S(1)}, bf16[128,2048]{1,0:T(8,128)(2,1)S(1)}, u32[]{:S(2)}, u32[]{:S(2)}) %collective-permute-start.58) | collective-permute-done | bytes 524320 | tf_op jit(solution)/shard_map/ppermute | solution.py:465
  (506 shorter events, 395.2 us)
Async XLA Ops:
  7.2 360.9 %all-gather.2.cloned.1.call-start = ((), (), s32[]{:S(2)}) async-start(), calls=%async_computation.1 | async-start | bytes 10485760 | tf_op jit(solution)/shard_map/all_gather | solution.py:518
  40.5 42.4 %collective-permute-start.3 = (bf16[256,2048]{1,0:T(8,128)(2,1)S(1)}, bf16[256,2048]{1,0:T(8,128)(2,1)S(1)}, u32[]{:S(2)}, u32[]{:S(2)}) collective-permute-start(bf16[256,2048]{1,0:T(8,128)(2,1)S(1)} %fusion.7), channel_id=1, source_target_pairs={{0,2},{2,0},{1,3},{3,1},{4,6},{6,4},{5,7},{7,5},{8,10},{10,8},{9,1... | collective-permute-start | bytes 3145736 | tf_op jit(solution)/shard_map/ppermute | solution.py:465
  41.5 41.4 %collective-permute-start.4 = (bf16[256,2048]{1,0:T(8,128)(2,1)S(1)}, bf16[256,2048]{1,0:T(8,128)(2,1)S(1)}, u32[]{:S(2)}, u32[]{:S(2)}) collective-permute-start(bf16[256,2048]{1,0:T(8,128)(2,1)S(1)} %fusion.7), channel_id=1, source_target_pairs={{0,1},{1,0},{2,3},{3,2},{4,5},{5,4},{6,7},{7,6},{8,9},{9,8},{10,11... | collective-permute-start | bytes 3145736 | tf_op jit(solution)/shard_map/ppermute | solution.py:465
  43.1 38.2 %collective-permute-start.5 = (bf16[1024,384]{1,0:T(8,128)(2,1)S(1)}, bf16[1024,384]{1,0:T(8,128)(2,1)S(1)}, u32[]{:S(2)}, u32[]{:S(2)}) collective-permute-start(bf16[1024,384]{1,0:T(8,128)(2,1)S(1)} %fusion.21), channel_id=1, source_target_pairs={{0,4},{4,0},{1,5},{5,1},{2,6},{6,2},{3,7},{7,3},{8,12},{12,8},{9,1... | collective-permute-start | bytes 2359304 | tf_op jit(solution)/shard_map/ppermute | solution.py:465
  122.5 522.6 %reduce-scatter.2.cloned.1.call-start = ((), (), s32[]{:S(2)}) async-start(), calls=%async_computation.2 | async-start | bytes 10485760 | tf_op jit(solution)/shard_map/reduce_scatter | solution.py:523
  125.7 49.7 %collective-permute-start.14 = (bf16[256,2048]{1,0:T(8,128)(2,1)S(1)}, bf16[256,2048]{1,0:T(8,128)(2,1)}, u32[]{:S(2)}, u32[]{:S(2)}) collective-permute-start(bf16[256,2048]{1,0:T(8,128)(2,1)S(1)} %fusion.15), channel_id=1, source_target_pairs={{0,2},{2,0},{1,3},{3,1},{4,6},{6,4},{5,7},{7,5},{8,10},{10,8},{9,1... | collective-permute-start | bytes 3145736 | tf_op jit(solution)/shard_map/ppermute | solution.py:465
  125.8 49.6 %collective-permute-start.15 = (bf16[256,2048]{1,0:T(8,128)(2,1)S(1)}, bf16[256,2048]{1,0:T(8,128)(2,1)S(1)}, u32[]{:S(2)}, u32[]{:S(2)}) collective-permute-start(bf16[256,2048]{1,0:T(8,128)(2,1)S(1)} %fusion.15), channel_id=1, source_target_pairs={{0,1},{1,0},{2,3},{3,2},{4,5},{5,4},{6,7},{7,6},{8,9},{9,8},{10,11... | collective-permute-start | bytes 3145736 | tf_op jit(solution)/shard_map/ppermute | solution.py:465
  131.2 37.2 %collective-permute-start.12 = (bf16[128,1024]{1,0:T(8,128)(2,1)S(1)}, bf16[128,1024]{1,0:T(8,128)(2,1)S(1)}, u32[]{:S(2)}, u32[]{:S(2)}) collective-permute-start(bf16[128,1024]{1,0:T(8,128)(2,1)S(1)} %copy-done.80), channel_id=1, source_target_pairs={{0,16},{16,0},{1,17},{17,1},{2,18},{18,2},{3,19},{19,3},{4,20},{20... | collective-permute-start | bytes 786440 | tf_op jit(solution)/shard_map/ppermute | solution.py:465
  132.7 42.7 %collective-permute-start.13 = (bf16[128,1024]{1,0:T(8,128)(2,1)S(1)}, bf16[128,1024]{1,0:T(8,128)(2,1)S(1)}, u32[]{:S(2)}, u32[]{:S(2)}) collective-permute-start(bf16[128,1024]{1,0:T(8,128)(2,1)S(1)} %copy-done.80), channel_id=1, source_target_pairs={{0,4},{4,0},{1,5},{5,1},{2,6},{6,2},{3,7},{7,3},{8,12},{12,8},{9,1... | collective-permute-start | bytes 786440 | tf_op jit(solution)/shard_map/ppermute | solution.py:465
  190.6 103.9 %collective-permute-start.21 = (bf16[512,1024]{1,0:T(8,128)(2,1)S(1)}, bf16[512,1024]{1,0:T(8,128)(2,1)S(1)}, u32[]{:S(2)}, u32[]{:S(2)}) collective-permute-start(bf16[512,1024]{1,0:T(8,128)(2,1)S(1)} %pad_maximum_fusion.10), channel_id=1, source_target_pairs={{0,16},{16,0},{1,17},{17,1},{2,18},{18,2},{3,19},{19,3},{4,20},{20... | collective-permute-start | bytes 3145736 | tf_op jit(solution)/shard_map/ppermute | solution.py:465
  223.7 69.9 %collective-permute-start.20 = (bf16[256,2048]{1,0:T(8,128)(2,1)S(1)}, bf16[256,2048]{1,0:T(8,128)(2,1)S(1)}, u32[]{:S(2)}, u32[]{:S(2)}) collective-permute-start(bf16[256,2048]{1,0:T(8,128)(2,1)S(1)} %get-tuple-element.100), channel_id=1, source_target_pairs={{0,2},{2,0},{1,3},{3,1},{4,6},{6,4},{5,7},{7,5},{8,10},{10,8},{9,1... | collective-permute-start | bytes 3145736 | tf_op jit(solution)/shard_map/ppermute | solution.py:465
  230.4 135.2 %collective-permute-start.27 = (bf16[1024,2048]{1,0:T(8,128)(2,1)}, bf16[1024,2048]{1,0:T(8,128)(2,1)S(1)}, u32[]{:S(2)}, u32[]{:S(2)}) collective-permute-start(bf16[1024,2048]{1,0:T(8,128)(2,1)} %slice_dynamic-update-slice_fusion.6.grad_ref.right_ref), channel_id=1, source_target_pairs={{0,8},{8,0},{1,9},{9,1},{2,10},{10,2},{3,11},{11,3},{4,12},{12,4},... | collective-permute-start | bytes 12582920 | tf_op jit(solution)/shard_map/ppermute | solution.py:465
  295.1 47.6 %collective-permute-start.28 = (bf16[512,1024]{1,0:T(8,128)(2,1)S(1)}, bf16[512,1024]{1,0:T(8,128)(2,1)S(1)}, u32[]{:S(2)}, u32[]{:S(2)}) collective-permute-start(bf16[512,1024]{1,0:T(8,128)(2,1)S(1)} %pad_maximum_fusion.10), channel_id=1, source_target_pairs={{0,4},{4,0},{1,5},{5,1},{2,6},{6,2},{3,7},{7,3},{8,12},{12,8},{9,1... | collective-permute-start | bytes 3145736 | tf_op jit(solution)/shard_map/ppermute | solution.py:465
  490.3 47.5 %collective-permute-start.35 = (bf16[256,2048]{1,0:T(8,128)(2,1)S(1)}, bf16[256,2048]{1,0:T(8,128)(2,1)S(1)}, u32[]{:S(2)}, u32[]{:S(2)}) collective-permute-start(bf16[256,2048]{1,0:T(8,128)(2,1)S(1)} %get-tuple-element.117), channel_id=1, source_target_pairs={{0,2},{2,0},{1,3},{3,1},{4,6},{6,4},{5,7},{7,5},{8,10},{10,8},{9,1... | collective-permute-start | bytes 3145736 | tf_op jit(solution)/shard_map/ppermute | solution.py:465
  568.9 38.4 %collective-permute-start.40 = (bf16[1024,2048]{1,0:T(8,128)(2,1)S(1)}, bf16[1024,2048]{1,0:T(8,128)(2,1)S(1)}, u32[]{:S(2)}, u32[]{:S(2)}) collective-permute-start(bf16[1024,2048]{1,0:T(8,128)(2,1)S(1)} %copy-done.97), channel_id=1, source_target_pairs={{0,8},{8,0},{1,9},{9,1},{2,10},{10,2},{3,11},{11,3},{4,12},{12,4},... | collective-permute-start | bytes 12582920 | tf_op jit(solution)/shard_map/ppermute | solution.py:465
  568.9 38.2 %collective-permute-start.38 = (bf16[256,2048]{1,0:T(8,128)(2,1)S(1)}, bf16[256,2048]{1,0:T(8,128)(2,1)S(1)}, u32[]{:S(2)}, u32[]{:S(2)}) collective-permute-start(bf16[256,2048]{1,0:T(8,128)(2,1)S(1)} %fusion.16), channel_id=1, source_target_pairs={{0,2},{2,0},{1,3},{3,1},{4,6},{6,4},{5,7},{7,5},{8,10},{10,8},{9,1... | collective-permute-start | bytes 3145736 | tf_op jit(solution)/shard_map/ppermute | solution.py:465
  568.9 38.3 %collective-permute-start.39 = (bf16[256,2048]{1,0:T(8,128)(2,1)S(1)}, bf16[256,2048]{1,0:T(8,128)(2,1)S(1)}, u32[]{:S(2)}, u32[]{:S(2)}) collective-permute-start(bf16[256,2048]{1,0:T(8,128)(2,1)S(1)} %fusion.16), channel_id=1, source_target_pairs={{0,1},{1,0},{2,3},{3,2},{4,5},{5,4},{6,7},{7,6},{8,9},{9,8},{10,11... | collective-permute-start | bytes 3145736 | tf_op jit(solution)/shard_map/ppermute | solution.py:465
  673.5 80.1 %collective-permute-start.48 = (bf16[1024,2048]{1,0:T(8,128)(2,1)}, bf16[1024,2048]{1,0:T(8,128)(2,1)}, u32[]{:S(2)}, u32[]{:S(2)}) collective-permute-start(bf16[1024,2048]{1,0:T(8,128)(2,1)} %shard_map.184), channel_id=1, source_target_pairs={{0,8},{8,0},{1,9},{9,1},{2,10},{10,2},{3,11},{11,3},{4,12},{12,4},... | collective-permute-start | bytes 12582920 | tf_op jit(solution)/shard_map/ppermute | solution.py:465
  676.9 48.3 %collective-permute-start.49 = (bf16[2,512,1024]{2,1,0:T(8,128)(2,1)}, bf16[2,512,1024]{2,1,0:T(8,128)(2,1)}, u32[]{:S(2)}, u32[]{:S(2)}) collective-permute-start(bf16[2,512,1024]{2,1,0:T(8,128)(2,1)} %constant_dynamic-slice_fusion.6), channel_id=1, source_target_pairs={{0,16},{16,0},{1,17},{17,1},{2,18},{18,2},{3,19},{19,3},{4,20},{20... | collective-permute-start | bytes 6291464 | tf_op jit(solution)/shard_map/ppermute | solution.py:465
  731.7 48.4 %collective-permute-start.50 = (bf16[512,1024]{1,0:T(8,128)(2,1)}, bf16[512,1024]{1,0:T(8,128)(2,1)}, u32[]{:S(2)}, u32[]{:S(2)}) collective-permute-start(bf16[512,1024]{1,0:T(8,128)(2,1)} %fusion.19), channel_id=1, source_target_pairs={{0,4},{4,0},{1,5},{5,1},{2,6},{6,2},{3,7},{7,3},{8,12},{12,8},{9,1... | collective-permute-start | bytes 3145736 | tf_op jit(solution)/shard_map/ppermute | solution.py:465
  769.1 43.6 %collective-permute-start.53 = (bf16[256,2048]{1,0:T(8,128)(2,1)}, bf16[256,2048]{1,0:T(8,128)(2,1)}, u32[]{:S(2)}, u32[]{:S(2)}) collective-permute-start(bf16[256,2048]{1,0:T(8,128)(2,1)} %get-tuple-element.140), channel_id=1, source_target_pairs={{0,2},{2,0},{1,3},{3,1},{4,6},{6,4},{5,7},{7,5},{8,10},{10,8},{9,1... | collective-permute-start | bytes 3145736 | tf_op jit(solution)/shard_map/ppermute | solution.py:465
  771.0 44.3 %collective-permute-start.54 = (bf16[2,1024,384]{2,1,0:T(8,128)(2,1)}, bf16[2,1024,384]{2,1,0:T(8,128)(2,1)}, u32[]{:S(2)}, u32[]{:S(2)}) collective-permute-start(bf16[2,1024,384]{2,1,0:T(8,128)(2,1)} %constant_dynamic-slice_fusion.5), channel_id=1, source_target_pairs={{0,16},{16,0},{1,17},{17,1},{2,18},{18,2},{3,19},{19,3},{4,20},{20... | collective-permute-start | bytes 4718600 | tf_op jit(solution)/shard_map/ppermute | solution.py:465
  822.4 54.8 %collective-permute-start.59 = (bf16[1024,384]{1,0:T(8,128)(2,1)S(1)}, bf16[1024,384]{1,0:T(8,128)(2,1)S(1)}, u32[]{:S(2)}, u32[]{:S(2)}) collective-permute-start(bf16[1024,384]{1,0:T(8,128)(2,1)S(1)} %fusion.20), channel_id=1, source_target_pairs={{0,4},{4,0},{1,5},{5,1},{2,6},{6,2},{3,7},{7,3},{8,12},{12,8},{9,1... | collective-permute-start | bytes 2359304 | tf_op jit(solution)/shard_map/ppermute | solution.py:465
  838.5 40.5 %collective-permute-start.66 = (bf16[512,512]{1,0:T(8,128)(2,1)S(1)}, bf16[512,512]{1,0:T(8,128)(2,1)S(1)}, u32[]{:S(2)}, u32[]{:S(2)}) collective-permute-start(bf16[512,512]{1,0:T(8,128)(2,1)S(1)} %constant_dynamic-slice_fusion), channel_id=1, source_target_pairs={{0,2},{2,0},{1,3},{3,1},{4,6},{6,4},{5,7},{7,5},{8,10},{10,8},{9,1... | collective-permute-start | bytes 1572872 | tf_op jit(solution)/shard_map/ppermute | solution.py:465
  (146 other events, 2476.4 us)
Sparse Core Ops, SparseCore 0:
  122.6 166.9 all-gather.1
  475.1 154.5 reduce-scatter.1

commit v3 on v2

--- a/solution.py
+++ b/solution.py
@@ -513,16 +513,18 @@
     return join(first[None], second[None], spots["w"], 0)
 
 
-def spread(piece):
-    rows, columns = piece.shape
-    return lax.all_gather(piece, ("w", "x"), axis=0, tiled=True).reshape(2, 2 * rows, columns)
-
-
-def collect(grad):
+def corner_blocks(grad, w, x):
     _, rows, columns = grad.shape
-    return lax.psum_scatter(
-        grad.reshape(2 * rows, columns), ("w", "x"), scatter_dimension=0, tiled=True
-    )
+    rows //= 2
+    parts = grad.reshape(2, 2, rows, columns)
+    return [
+        lax.dynamic_slice(parts, (at_w, at_x, 0, 0), (1, 1, rows, columns))[0, 0]
+        for at_w, at_x in ((1 - w, 1 - x), (1 - w, x), (w, 1 - x), (w, x))
+    ]
+
+
+def plus(left, right):
+    return low_bits(wide_bits(left) + wide_bits(right))
 
 
 def weave(own, from_u, from_v, first_uv, second_uv):
@@ -578,21 +580,7 @@
     return pl.BlockSpec(shape, lambda *_: (0,) * len(shape))
 
 
-def tie_kernel(value_ref, *refs):
-    refs[-1][...] = value_ref[...]
-
-
-def tie(value, *held):
-    return pl.pallas_call(
-        tie_kernel,
-        in_specs=[whole(value.shape), *[pl.BlockSpec(memory_space=pl.ANY) for _ in held]],
-        out_specs=whole(value.shape),
-        out_shape=jax.ShapeDtypeStruct(value.shape, value.dtype),
-        compiler_params=pltpu.CompilerParams(vmem_limit_bytes=48 * 2**20),
-    )(value, *held)
-
-
-def kernel_call(kernel, grid, in_specs, out_specs, out_shape, flops, size, scratch=()):
+def kernel_call(kernel, grid, in_specs, out_specs, out_shape, flops, size, scratch=(), weight=1000):
     return pl.pallas_call(
         kernel,
         grid=grid,
@@ -601,7 +589,9 @@
         out_shape=out_shape,
         scratch_shapes=scratch,
         compiler_params=pltpu.CompilerParams(vmem_limit_bytes=48 * 2**20),
-        cost_estimate=pl.CostEstimate(flops=flops, bytes_accessed=size, transcendentals=0),
+        cost_estimate=pl.CostEstimate(
+            flops=flops // weight, bytes_accessed=size // weight, transcendentals=0
+        ),
     )
 
 
@@ -658,6 +648,7 @@
         ),
         2 * count * width * 2 * span + 8 * count * count * HEAD_DIM * 3,
         count * width * 2 + weight.size * 2,
+        weight=1,
     )(rows, weight, *tables, *held)
 
 
@@ -734,29 +725,28 @@
         out_ref[at, span:] = low_bits(grad_hidden * silu)
 
 
-def hidden_pass(rows, grads, wide, down, tile):
+def hidden_pass(rows, grads, wide, down):
     count, width = rows.shape
-    span = wide.shape[2] // 2
-    tiles = span // tile
+    tile = wide.shape[2] // 2
     return kernel_call(
         hidden_kernel,
-        (2, tiles),
+        (2,),
         [
             whole(rows.shape),
             whole(grads.shape),
-            pl.BlockSpec((1, width, 2 * tile), lambda w, t: (w, 0, t)),
-            pl.BlockSpec((2, tile, width // 2), lambda w, t: (0, tiles * w + t, 0)),
+            pl.BlockSpec((1, width, 2 * tile), lambda w: (w, 0, 0)),
+            pl.BlockSpec((2, tile, width // 2), lambda w: (0, w, 0)),
         ],
         (
-            pl.BlockSpec((count, tile), lambda w, t: (0, tiles * w + t)),
-            pl.BlockSpec((count, 2 * tile), lambda w, t: (0, tiles * w + t)),
+            pl.BlockSpec((count, tile), lambda w: (0, w)),
+            pl.BlockSpec((count, 2 * tile), lambda w: (0, w)),
         ),
         (
-            jax.ShapeDtypeStruct((count, 2 * span), jnp.bfloat16),
-            jax.ShapeDtypeStruct((count, 4 * span), jnp.bfloat16),
+            jax.ShapeDtypeStruct((count, 2 * tile), jnp.bfloat16),
+            jax.ShapeDtypeStruct((count, 4 * tile), jnp.bfloat16),
         ),
-        2 * count * width * 6 * span,
-        count * width * 8 + wide.size * 3,
+        2 * count * width * 6 * tile,
+        count * width * 4 + wide.size * 3,
     )(rows, grads, wide, down)
 
 
@@ -800,38 +790,40 @@
     )(*lefts, *weights, *added, *held)
 
 
-def ahead_kernel(added, left_ref, weight_ref, *refs):
+def ahead_kernel(counts, *refs):
     out_ref = refs[-1]
-    rows = left_ref.shape[0]
+    pairs, more = counts
+    lefts, weights = refs[:pairs], refs[pairs : 2 * pairs]
+    added = refs[2 * pairs : 2 * pairs + more]
+    rows = lefts[0].shape[0]
 
     @pl.loop(0, rows // TALL)
     def _(i):
         at = pl.ds(pl.multiple_of(i * TALL, TALL), TALL)
-        total = dot(left_ref[at, :], weight_ref[0])
-        if added:
-            total += wide_bits(refs[0][at, :])
+        total = sum(dot(left_ref[at, :], weight_ref[0]) for left_ref, weight_ref in zip(lefts, weights))
+        for added_ref in added:
+            total += wide_bits(added_ref[at, :])
         out_ref[at, :] = low_bits(total)
 
 
-def ahead_rows(left, weight, added=None):
-    count, depth = left.shape
-    span = weight.shape[2]
+def ahead_rows(lefts, weights, added=()):
+    count, depth = lefts[0].shape
+    span = weights[0].shape[2]
     tile = 512
     tiles = span // tile
-    more = [] if added is None else [added]
     return kernel_call(
-        functools.partial(ahead_kernel, len(more)),
+        functools.partial(ahead_kernel, (len(lefts), len(added))),
         (2, tiles),
         [
-            whole(left.shape),
-            pl.BlockSpec((1, depth, tile), lambda w, t: (w, 0, t)),
-            *[pl.BlockSpec((count, tile), lambda w, t: (0, w * tiles + t)) for _ in more],
+            *[whole(left.shape) for left in lefts],
+            *[pl.BlockSpec((1, depth, tile), lambda w, t: (w, 0, t)) for _ in weights],
+            *[pl.BlockSpec((count, tile), lambda w, t: (0, w * tiles + t)) for _ in added],
         ],
         pl.BlockSpec((count, tile), lambda w, t: (0, w * tiles + t)),
         jax.ShapeDtypeStruct((count, 2 * span), jnp.bfloat16),
-        2 * count * depth * 2 * span,
-        count * (2 * span + depth) * 2 + weight.size * 2,
-    )(left, weight, *more)
+        2 * count * depth * 2 * span * len(lefts),
+        len(lefts) * (count * (2 * span + depth) * 2 + weights[0].size * 2),
+    )(*lefts, *weights, *added)
 
 
 def outer_kernel(left_ref, left_other_ref, right_ref, right_other_ref, out_ref):
@@ -843,7 +835,7 @@
 def outer_rows(lefts, rights):
     count, depth = lefts[0].shape
     span = rights[0].shape[1] // 2
-    tile = 256
+    tile = min(depth, 512)
     left_spec = pl.BlockSpec((count, tile), lambda w, i: (0, i))
     right_spec = pl.BlockSpec((count, span), lambda w, i: (0, w))
     return kernel_call(
@@ -918,15 +910,17 @@
     norm_own = low_bits(normed_in)
     columns = join(columns_kept, columns_got, c, 0)
     qkv_piece = columns[:, :head_columns]
-    wide_piece = jnp.concatenate(
-        [
-            columns[:, at + start : at + start + tile]
-            for start in range(0, wide_columns, tile)
-            for at in (head_columns, head_columns + wide_columns)
-        ],
-        axis=1,
-    )
-    full_wide = spread(wide_piece)
+    wide_pieces = [
+        jnp.concatenate(
+            [
+                columns[:, at + start : at + start + tile]
+                for at in (head_columns, head_columns + wide_columns)
+            ],
+            axis=1,
+        )
+        for start in range(0, wide_columns, tile)
+    ]
+    size = wide_pieces[0].shape[0] // 2
     parts = join(parts_kept[0], parts_got, v, 2)
     parts_kept, parts_sent = both_halves(parts, c, 0)
     norm_u, norm_v, qkv_w, qkv_x, parts_got = stage(
@@ -941,109 +935,199 @@
     full_qkv = square(qkv_piece, qkv_w, qkv_x, qkv_wx, spots)
     parts = join(parts_kept[0], parts_got, u, 1)
     output_piece, down_piece = parts[:output_span], parts[output_span:]
+    down_pieces = [down_piece[: down_span // 2], down_piece[down_span // 2 :]]
     grad_out = wide_bits(jnp.concatenate([cotangent_kept[0], cotangent_got], axis=0)) * live
     grad_own = low_bits(grad_out)
 
-    norm_other, output_w, output_x = stage(
-        [(norm_in, "c"), (output_piece, "w"), (output_piece, "x")], [qkv_wx, cotangent_got]
-    )
-    grad_u, grad_v = stage([(grad_own, "u"), (grad_own, "v")], [qkv_wx])
+    wide_x0, output_x, output_w, wide_w0a, norm_other = stage(
+        [
+            (wide_pieces[0], "x"),
+            (output_piece, "x"),
+            (output_piece, "w"),
+            (wide_pieces[0][:size], "w"),
+            (norm_in, "c"),
+        ],
+        [qkv_wx, cotangent_got],
+    )
     first = attend(norm_in, full_qkv, tables)
+    output_w, norm_other, _ = lax.optimization_barrier((output_w, norm_other, first[0]))
+    output_wx = swap(output_w, "x")
     second = attend(norm_other, full_qkv, tables)
-    output_wx, grad_uv, down_x, down_w = stage(
-        [(output_w, "x"), (grad_u, "v"), (down_piece, "x"), (down_piece, "w")],
-        [output_x, grad_v, first[0], second[0]],
+    output_x, second, wide_w0a, wide_x0 = lax.optimization_barrier(
+        (output_x, second, wide_w0a, wide_x0)
     )
     norm_in = (norm_in, norm_other)
     turned, attended = zip(first, second)
     full_output = square(output_piece, output_w, output_x, output_wx, spots)
-    grad_all = weave(grad_own, grad_u, grad_v, grad_uv[:tok_rows], grad_uv[tok_rows:])
-    (other,) = stage([(ahead_rows(attended[1], full_output), "c")])
-    total = ahead_rows(attended[0], full_output, other)
-    from_v, from_u = stage(fold_sends(total))
-    (grad_other,) = stage([(grad_all, "c")], [other])
-    grad_all = (grad_all, grad_other)
+    other = swap(ahead_rows([attended[1]], [full_output]), "c")
+    wide_w0b, wide_x1, grad_u, grad_v = stage(
+        [
+            (wide_pieces[0][size:], "w"),
+            (wide_pieces[1], "x"),
+            (grad_own, "u"),
+            (grad_own, "v"),
+        ],
+        [wide_w0a, wide_x0, first[0], second[0]],
+    )
+    total = ahead_rows([attended[0]], [full_output], [other])
+    from_v, from_u, down_w0, down_x = stage(
+        fold_sends(total) + [(down_pieces[0], "w"), (down_piece, "x")],
+        [wide_w0b, wide_x1, grad_u, grad_v],
+    )
     kept, sends = fold(total, from_v, from_u)
-    from_u, from_v = stage(sends, [down_x])
-    (down_wx,) = stage([(down_w, "x")], [from_u])
-    full_down = square(down_piece, down_w, down_x, down_wx, spots)
+    from_u, from_v, grad_uv, grad_vu, wide_wx0 = stage(
+        sends
+        + corners(grad_u, grad_v)
+        + [(jnp.concatenate([wide_w0a, wide_w0b], axis=0), "x")],
+        [down_w0, down_x],
+    )
+    grad_all = weave(grad_own, grad_u, grad_v, grad_uv, grad_vu)
     after_attn = inputs + fold_end(kept, from_u, from_v)
     normed_mid, norm_mid_back = jax.vjp(layer_norm, after_attn)
     mid_own = low_bits(normed_mid)
-    mid_u, mid_v = stage([(mid_own, "u"), (mid_own, "v")])
-    mid_uv, mid_vu = stage(corners(mid_u, mid_v), [grad_other, down_wx])
-    mid_uv = tie(mid_uv, full_wide)
+    mid_u, mid_v, grad_other, down_wx0, wide_w1a = stage(
+        [
+            (mid_own, "u"),
+            (mid_own, "v"),
+            (grad_all, "c"),
+            (down_w0, "x"),
+            (wide_pieces[1][:size], "w"),
+        ],
+        [wide_wx0, grad_uv],
+    )
+    grad_all = (grad_all, grad_other)
+    mid_uv, mid_vu, down_w1, wide_wx1a = stage(
+        corners(mid_u, mid_v) + [(down_pieces[1], "w"), (wide_w1a, "x")], [grad_other, down_wx0]
+    )
     norm_mid = weave(mid_own, mid_u, mid_v, mid_uv, mid_vu)
-    norm_mid = (norm_mid, swap(norm_mid, "c"))
-
-    hidden, grad_wide = zip(
-        *[hidden_pass(rows, grads, full_wide, full_down, tile) for rows, grads in zip(norm_mid, grad_all)]
-    )
-    (other,) = stage([(back_rows([grad_wide[1]], [full_wide]), "c")], [grad_wide[0]])
-    wide_outer = outer_rows(norm_mid, grad_wide)
-    wide_total = collect(wide_outer)
-    other, _ = lax.optimization_barrier((other, wide_outer))
-    total = back_rows([grad_wide[0]], [full_wide], [other])
+    full_wide = [
+        square(wide_pieces[0], jnp.concatenate([wide_w0a, wide_w0b], axis=0), wide_x0, wide_wx0, spots)
+    ]
+    half_rows = down_span // 2
+    full_down = [square(down_pieces[0], down_w0, down_x[:half_rows], down_wx0, spots)]
+    norm_other, wide_w1b, down_wx1 = stage(
+        [(norm_mid, "c"), (wide_pieces[1][size:], "w"), (down_w1, "x")], [mid_uv, wide_wx1a]
+    )
+    norm_mid = (norm_mid, norm_other)
+
+    first = hidden_pass(norm_mid[0], grad_all[0], full_wide[0], full_down[0])
+    second = hidden_pass(norm_other, grad_all[1], full_wide[0], full_down[0])
+    second, wide_w1b = lax.optimization_barrier((second, wide_w1b))
+    passes = [(first, second)]
+    wide_outers = [outer_rows(norm_mid, [first[1], second[1]])]
+    far0, far_kept0, near0, near_kept0 = corner_blocks(wide_outers[0], w, x)
+    wide_wx1b = swap(wide_w1b, "x")
+    far_got0 = swap(far0, "x")
+    full_wide.append(
+        square(
+            wide_pieces[1],
+            jnp.concatenate([wide_w1a, wide_w1b], axis=0),
+            wide_x1,
+            jnp.concatenate([wide_wx1a, wide_wx1b], axis=0),
+            spots,
+        )
+    )
+    full_down.append(square(down_pieces[1], down_w1, down_x[half_rows:], down_wx1, spots))
+    first = hidden_pass(norm_mid[0], grad_all[0], full_wide[1], full_down[1])
+    second = hidden_pass(norm_mid[1], grad_all[1], full_wide[1], full_down[1])
+    passes.append((first, second))
+    grad_wide = [[made[side][1] for made in passes] for side in (0, 1)]
+    hidden = [[made[side][0] for made in passes] for side in (0, 1)]
+    far_got0, grad_wide[1] = lax.optimization_barrier((far_got0, grad_wide[1]))
+    far_sum0 = plus(far_kept0, far_got0)
+    wide_g0a, near_got0 = stage([(far_sum0[:size], "w"), (near0, "x")])
+    other = swap(back_rows(grad_wide[1], full_wide), "c")
+    wide_outers.append(outer_rows(norm_mid, [first[1], second[1]]))
+    other, wide_outers[1], wide_g0a, near_got0 = lax.optimization_barrier(
+        (other, wide_outers[1], wide_g0a, near_got0)
+    )
+    far1, far_kept1, near1, near_kept1 = corner_blocks(wide_outers[1], w, x)
+    wide_g0b, far_got1 = stage([(far_sum0[size:], "w"), (far1, "x")], [wide_g0a, near_got0])
+    total = back_rows(grad_wide[0], full_wide, [other])
     from_v, from_u = stage(fold_sends(total))
-    down_outer = outer_rows(hidden, grad_all)
-    down_kept, down_sent = both_halves(down_outer, x, 1)
+    down_outers = [outer_rows([made[0][0], made[1][0]], grad_all) for made in passes]
+    down_blocks = [corner_blocks(outer, w, x) for outer in down_outers]
+    down_far, down_far_kept, down_near, down_near_kept = (
+        jnp.concatenate(blocks, axis=0) for blocks in zip(*down_blocks)
+    )
+    far_sum1 = plus(far_kept1, far_got1)
     kept, sends = fold(total, from_v, from_u)
-    from_u, from_v = stage(sends, [down_outer])
-    (down_got,) = stage([(down_sent, "x")], [from_u])
+    from_u, from_v, wide_g1a, near_got1 = stage(
+        sends + [(far_sum1[:size], "w"), (near1, "x")], [wide_g0b, down_far]
+    )
     ahead = ahead_rows(hidden[1], full_down)
     grad_norm_mid = fold_end(kept, from_u, from_v)
     grad_after = grad_out + norm_mid_back(grad_norm_mid)[0]
     after_own = low_bits(grad_after)
-    after_u, after_v, other = stage([(after_own, "u"), (after_own, "v"), (ahead, "c")])
-    after_uv, after_vu = stage(corners(after_u, after_v), [other])
-    total = ahead_rows(hidden[0], full_down, other)
-    after_uv, after_vu, total = lax.optimization_barrier((after_uv, after_vu, total))
+    after_u, after_v, other, down_far_got = stage(
+        [(after_own, "u"), (after_own, "v"), (ahead, "c"), (down_far, "x")], [wide_g1a, near_got1]
+    )
+    down_sum = plus(down_far_kept, down_far_got)
+    after_uv, after_vu, wide_g1b, down_near_got = stage(
+        corners(after_u, after_v) + [(far_sum1[size:], "w"), (down_near, "x")], [other, down_far_got]
+    )
+    total = ahead_rows(hidden[0], full_down, [other])
     after_all = weave(after_own, after_u, after_v, after_uv, after_vu)
 
-    down_sum = wide_bits(down_kept) + wide_bits(down_got)
-    down_kept, down_sent = both_halves(down_sum, w, 0)
-    (after_other,) = stage([(after_all, "c")])
-    from_v, from_u = stage(fold_sends(total), [after_uv])
-    (down_got,) = stage([(low_bits(down_sent[0]), "w")], [after_other])
+    from_v, from_u, down_g0, after_other = stage(
+        fold_sends(total) + [(down_sum[:half_rows], "w"), (after_all, "c")], [wide_g1b, down_near_got]
+    )
     after_all = (after_all, after_other)
     first = attend_back(after_all[0], full_output, turned[0], tables)
+    output_outer = outer_rows(attended, after_all)
+    output_far, output_far_kept, output_near, output_near_kept = corner_blocks(output_outer, w, x)
     kept, sends = fold(total, from_v, from_u)
-    from_u, from_v = stage(sends, [first, after_other])
-    second = attend_back(after_other, full_output, turned[1], tables, wide_total)
+    from_u, from_v, down_g1, output_got = stage(
+        sends + [(down_sum[half_rows:], "w"), (output_far, "x")],
+        [first, after_other, down_g0, output_outer],
+    )
+    second = attend_back(after_other, full_output, turned[1], tables)
     grad_qkv = (first, second)
     ahead = back_rows([second], [full_qkv])
+    mixed = low_bits((after_attn + fold_end(kept, from_u, from_v)) * live)
+    other, mixed_got, output_got, output_near_got = stage(
+        [
+            (ahead, "c"),
+            (mixed[tok_rows:], "w"),
+            (plus(output_far_kept, output_got), "w"),
+            (output_near, "x"),
+        ],
+        [down_g1],
+    )
     qkv_outer = outer_rows(norm_in, grad_qkv)
-    mixed = low_bits((after_attn + fold_end(kept, from_u, from_v)) * live)
-    (other,) = stage([(ahead, "c")])
     other, qkv_outer = lax.optimization_barrier((other, qkv_outer))
-    (mixed_got,) = stage([(mixed[tok_rows:], "w")], [other, down_got])
-    output_outer = outer_rows(attended, after_all)
+    qkv_far, qkv_far_kept, qkv_near, qkv_near_kept = corner_blocks(qkv_outer, w, x)
+    qkv_got = swap(qkv_far, "x")
     total = back_rows([first], [full_qkv], [other])
-    qkv_kept, qkv_sent = both_halves(qkv_outer, x, 1)
-    output_kept, output_sent = both_halves(output_outer, x, 1)
-    from_v, from_u, qkv_got = stage(fold_sends(total) + [(qkv_sent, "x")], [mixed])
-    qkv_sum = wide_bits(qkv_kept) + wide_bits(qkv_got)
-    qkv_kept, qkv_sent = both_halves(qkv_sum, w, 0)
+    qkv_got, total = lax.optimization_barrier((qkv_got, total))
+    from_v, from_u, qkv_got = stage(
+        fold_sends(total) + [(plus(qkv_far_kept, qkv_got), "w")], [mixed_got, output_got]
+    )
     kept, sends = fold(total, from_v, from_u)
-    from_u, from_v, qkv_got, output_got = stage(
-        sends + [(low_bits(qkv_sent[0]), "w"), (output_sent, "x")], [mixed_got]
-    )
+    from_u, from_v, qkv_near_got = stage(sends + [(qkv_near, "x")])
     grad_norm_in = fold_end(kept, from_u, from_v)
     token_grad = grad_after + norm_in_back(grad_norm_in)[0]
-    output_sum = wide_bits(output_kept) + wide_bits(output_got)
-    output_kept, output_sent = both_halves(output_sum, w, 0)
-    token_got, output_got = stage(
-        [(low_bits(token_grad[tok_rows:]), "w"), (low_bits(output_sent[0]), "w")]
-    )
-    down_kept, down_got, wide_total, _ = lax.optimization_barrier(
-        (down_kept, down_got, wide_total, from_u)
-    )
-    down_total = low_bits(down_kept[0] + wide_bits(down_got))
-    qkv_total = qkv_kept[0] + wide_bits(qkv_got)
-    output_total = low_bits(output_kept[0] + wide_bits(output_got))
-
-    wide_parts = [wide_total[:, at : at + tile] for at in range(0, 2 * wide_columns, tile)]
-    wide_total = jnp.concatenate(wide_parts[0::2] + wide_parts[1::2], axis=1)
+    token_got = swap(low_bits(token_grad[tok_rows:]), "w")
+
+    def add_up(*values):
+        return sum(wide_bits(value) for value in values)
+
+    held = (
+        (near_kept0, near_got0, wide_g0a, wide_g0b),
+        (near_kept1, near_got1, wide_g1a, wide_g1b),
+        (down_near_kept, down_near_got, down_g0, down_g1),
+    )
+    held, _ = lax.optimization_barrier((held, from_u))
+    wide_totals = [
+        add_up(kept, got, jnp.concatenate([top, bottom], axis=0)) for kept, got, top, bottom in held
+    ]
+    down_total = low_bits(wide_totals.pop())
+    qkv_total = add_up(qkv_near_kept, qkv_near_got, qkv_got)
+    output_total = low_bits(add_up(output_near_kept, output_near_got, output_got))
+
+    wide_total = jnp.concatenate(
+        [part[:, at : at + tile] for at in (0, tile) for part in wide_totals], axis=1
+    )
 
     def columns_home(total, sizes):
         kept, sent = both_halves(total, c, 0)

time: 935 us -> 871 us (0.932)
  waiting for transfers between devices: 471 us -> 358 us
  starting transfers between devices: 72.8 us -> 97.4 us
  other arithmetic: 57.6 us -> 78.5 us
  local copies, waits for them, and re-layouts: 66.9 us -> 80.5 us
  between operations: 17.1 us -> 4.15 us
    ppermute x69 -> x93, waiting for transfers between devices: 471 us -> 358 us  [swap(): return lax.ppermute(value, axis, SWAP)]
    ppermute x69 -> x93, starting transfers between devices: 72.7 us -> 97.4 us  [swap(): return lax.ppermute(value, axis, SWAP)]
    squeeze x0 -> x5, local copies, waits for them, and re-layouts: none -> 9.71 us  [corner_blocks(): lax.dynamic_slice(parts, (at_w, at_x, 0, 0), (1, 1, rows, columns))[0, 0]]
    concatenate x25 -> x35, other arithmetic: 15.4 us -> 24.9 us  [join(): return jnp.concatenate([low, high], axis=axis)]
    pallas_call x7 -> x8, Pallas kernels: 66.4 us -> 73.8 us  [the longest x4 50.6 us: hidden_pass(): kernel_call(hidden_kernel, (2,), [whole(rows.shape), whole(grads.shape),...]
    unnamed x228 -> x311, local copies, waits for them, and re-layouts: 42.5 us -> 39.2 us
    pallas_call x4 -> x6, Pallas kernels: 65.4 us -> 62.7 us  [outer_rows(): kernel_call(outer_kernel, (2, depth // tile), [left_spec, left_spec, righ...]
  transfers between devices with their start and end apart: 71 -> 93, of which waited for: 32 -> 38; matrix products, arithmetic and copies ran while one was open for 10% -> 15% of each run, Pallas kernels for 20% -> 25%
where the time goes in v3:
time: 871 us; the launch traced here: 862 us
  waiting for transfers between devices  358 us (41%)
  Pallas kernels  243 us (28%)
  starting transfers between devices  97.4 us (11%)
  local copies, waits for them, and re-layouts  80.5 us (9%)
  other arithmetic  78.5 us (9%)
    ppermute x93, waiting for transfers between devices, swap(): return lax.ppermute(value, axis, SWAP)  358 us
    ppermute x93, starting transfers between devices, swap(): return lax.ppermute(value, axis, SWAP)  97.4 us
    pallas_call x6, Pallas kernels, outer_rows(): kernel_call(outer_kernel, (2, depth // tile), [left_spec, left_spec, righ...  62.7 us
    pallas_call x4, Pallas kernels, hidden_pass(): kernel_call(hidden_kernel, (2,), [whole(rows.shape), whole(grads.shape),...  50.6 us
    pallas_call x4, Pallas kernels, back_rows(): kernel_call(functools.partial(back_kernel, (len(lefts), len(added))), (wi...  43.8 us
    unnamed x311, local copies, waits for them, and re-layouts  39.2 us
    pallas_call x2, Pallas kernels, attend(): kernel_call(attend_kernel, (2,), [whole(rows.shape), pl.BlockSpec((1, wid...  31.9 us
    pallas_call x2, Pallas kernels, attend_back(): kernel_call(attend_back_kernel, (2,), [whole(grads.shape), pl.BlockSpec((...  31.1 us
  transfers between devices with their start and end apart: 93, of which 38 were waited for; matrix products, arithmetic and copies ran while one was open for 15% of the time, Pallas kernels for 25%

profile of v3, /device:TPU:0, one launch (start us, length us, event | category | flops | bytes accessed | tf_op | source)
XLA Modules:
  0.0 861.9 jit_solution(13400426379699744607)
XLA Ops:
  16.1 14.1 %collective-permute-done = bf16[128,2048]{1,0:T(8,128)(2,1)S(1)} collective-permute-done((bf16[128,2048]{1,0:T(8,128)(2,1)}, bf16[128,2048]{1,0:T(8,128)(2,1)S(1)}, u32[]{:S(2)}, u32[]{:S(2)}) %collective-permute-start) | collective-permute-done | bytes 524320 | tf_op jit(solution)/shard_map/ppermute | solution.py:465
  46.7 29.0 %collective-permute-done.5 = bf16[1024,384]{1,0:T(8,128)(2,1)S(1)} collective-permute-done((bf16[1024,384]{1,0:T(8,128)(2,1)S(1)}, bf16[1024,384]{1,0:T(8,128)(2,1)S(1)}, u32[]{:S(2)}, u32[]{:S(2)}) %collective-permute-start.5) | collective-permute-done | bytes 786464 | tf_op jit(solution)/shard_map/ppermute | solution.py:465
  86.2 18.6 %collective-permute-done.10 = bf16[640,512]{1,0:T(8,128)(2,1)S(1)} collective-permute-done((bf16[640,512]{1,0:T(8,128)(2,1)S(1)}, bf16[640,512]{1,0:T(8,128)(2,1)S(1)}, u32[]{:S(2)}, u32[]{:S(2)}) %collective-permute-start.10) | collective-permute-done | bytes 655392 | tf_op jit(solution)/shard_map/ppermute | solution.py:465
  123.5 16.0 %shard_map.169 = (bf16[1024,768]{1,0:T(8,128)(2,1)S(1)}, bf16[1024,256]{1,0:T(8,128)(2,1)S(1)}) custom-call(bf16[1024,2048]{1,0:T(8,128)(2,1)} %slice_dynamic-update-slice_fusion.12.rows_ref.left_ref, bf16[2,2048,384]{2,1,0:T(8,128)(2,1)} %pad_maximum_fusion.3.weight_ref.refs_1_, f32[1024,128]{1,0:T(8,128)S(1)} %pad_maximum_fusion.31.cos_ref, ...), custom_call_target="tpu_custom_call" | custom-call | flops 6442450944 | bytes 7340032 | tf_op jit(solution)/shard_map/pallas_call | solution.py:632
  147.5 15.9 %shard_map.170 = (bf16[1024,768]{1,0:T(8,128)(2,1)S(1)}, bf16[1024,256]{1,0:T(8,128)(2,1)S(1)}) custom-call(bf16[1024,2048]{1,0:T(8,128)(2,1)} %collective-permute-done.14.rows_ref.left_other_ref, bf16[2,2048,384]{2,1,0:T(8,128)(2,1)} %pad_maximum_fusion.3.weight_ref.refs_1_, f32[1024,128]{1,0:T(8,128)S(1)} %pad_maximum_fusion.31.cos_ref, ...), custom_call_target="tpu_custom_call" | custom-call | flops 6442450944 | bytes 7340032 | tf_op jit(solution)/shard_map/pallas_call | solution.py:632
  182.8 24.9 %collective-permute-done.19 = bf16[512,512]{1,0:T(8,128)(2,1)} collective-permute-done((bf16[512,512]{1,0:T(8,128)(2,1)}, bf16[512,512]{1,0:T(8,128)(2,1)}, u32[]{:S(2)}, u32[]{:S(2)}) %collective-permute-start.19) | collective-permute-done | bytes 524320 | tf_op jit(solution)/shard_map/ppermute | solution.py:465
  218.1 16.6 %collective-permute-done.23 = bf16[256,2048]{1,0:T(8,128)(2,1)S(1)} collective-permute-done((bf16[256,2048]{1,0:T(8,128)(2,1)S(1)}, bf16[256,2048]{1,0:T(8,128)(2,1)S(1)}, u32[]{:S(2)}, u32[]{:S(2)}) %collective-permute-start.23) | collective-permute-done | bytes 1048608 | tf_op jit(solution)/shard_map/ppermute | solution.py:465
  281.6 30.6 %collective-permute-done.32 = bf16[256,2048]{1,0:T(8,128)(2,1)S(1)} collective-permute-done((bf16[256,2048]{1,0:T(8,128)(2,1)S(1)}, bf16[256,2048]{1,0:T(8,128)(2,1)S(1)}, u32[]{:S(2)}, u32[]{:S(2)}) %collective-permute-start.32) | collective-permute-done | bytes 1048608 | tf_op jit(solution)/shard_map/ppermute | solution.py:465
  356.0 12.7 %shard_map.173 = (bf16[1024,512]{1,0:T(8,128)(2,1)S(1)}, bf16[1024,1024]{1,0:T(8,128)(2,1)S(1)}) custom-call(bf16[1024,2048]{1,0:T(8,128)(2,1)} %constant_dynamic-update-slice_fusion.7.rows_ref.left_ref, bf16[1024,2048]{1,0:T(8,128)(2,1)} %copy-done.31, bf16[2,2048,512]{2,1,0:T(8,128)(2,1)} %pad_maximum_fusion.wide_ref.refs_2_, ...), custom_call_target="tpu_custom_call" | custom-call | flops 6442450 | bytes 14680 | tf_op jit(solution)/shard_map/pallas_call | solution.py:731
  368.9 12.7 %shard_map.174 = (bf16[1024,512]{1,0:T(8,128)(2,1)S(1)}, bf16[1024,1024]{1,0:T(8,128)(2,1)S(1)}) custom-call(bf16[1024,2048]{1,0:T(8,128)(2,1)} %collective-permute-done.41.rows_ref.left_other_ref, bf16[1024,2048]{1,0:T(8,128)(2,1)} %copy-done.32, bf16[2,2048,512]{2,1,0:T(8,128)(2,1)} %pad_maximum_fusion.wide_ref.refs_2_, ...), custom_call_target="tpu_custom_call" | custom-call | flops 6442450 | bytes 14680 | tf_op jit(solution)/shard_map/pallas_call | solution.py:731
  384.5 15.1 %shard_map.176 = bf16[2,2048,512]{2,1,0:T(8,128)(2,1)} custom-call(bf16[1024,2048]{1,0:T(8,128)(2,1)} %constant_dynamic-update-slice_fusion.7.rows_ref.left_ref, bf16[1024,2048]{1,0:T(8,128)(2,1)} %collective-permute-done.41.rows_ref.left_other_ref, bf16[1024,1024]{1,0:T(8,128)(2,1)S(1)} %get-tuple-element.184.right_ref.refs_0_, ...), custom_call_target="tpu_custom_call" | custom-call | flops 8589934 | bytes 16777 | tf_op jit(solution)/shard_map/pallas_call | solution.py:841
  410.0 12.6 %shard_map.177 = (bf16[1024,512]{1,0:T(8,128)(2,1)S(1)}, bf16[1024,1024]{1,0:T(8,128)(2,1)S(1)}) custom-call(bf16[1024,2048]{1,0:T(8,128)(2,1)} %collective-permute-done.41.rows_ref.left_other_ref, bf16[1024,2048]{1,0:T(8,128)(2,1)} %copy-done.32, bf16[2,2048,512]{2,1,0:T(8,128)(2,1)} %pad_maximum_fusion.1.wide_ref.refs_3_, ...), custom_call_target="tpu_custom_call" | custom-call | flops 6442450 | bytes 14680 | tf_op jit(solution)/shard_map/pallas_call | solution.py:731
  428.4 12.8 %shard_map.178 = bf16[1024,2048]{1,0:T(8,128)(2,1)} custom-call(bf16[1024,1024]{1,0:T(8,128)(2,1)S(1)} %get-tuple-element.188.right_other_ref.refs_0_, bf16[1024,1024]{1,0:T(8,128)(2,1)S(1)} %get-tuple-element.189.refs_1_.right_other_ref, bf16[2,2048,512]{2,1,0:T(8,128)(2,1)} %pad_maximum_fusion.wide_ref.refs_2_, ...), custom_call_target="tpu_custom_call" | custom-call | flops 8589934 | bytes 20971 | tf_op jit(solution)/shard_map/pallas_call | solution.py:777
  460.2 14.3 %shard_map.179 = bf16[2,2048,512]{2,1,0:T(8,128)(2,1)} custom-call(bf16[1024,2048]{1,0:T(8,128)(2,1)} %constant_dynamic-update-slice_fusion.7.rows_ref.left_ref, bf16[1024,2048]{1,0:T(8,128)(2,1)} %collective-permute-done.41.rows_ref.left_other_ref, bf16[1024,1024]{1,0:T(8,128)(2,1)S(1)} %get-tuple-element.185.right_ref.refs_1_, bf16[1024,1024]{1,0:T(8,128)(2,1)S(1)} %copy-done.9), custom_call_target="tpu_custom_call" | custom-call | flops 8589934 | bytes 16777 | tf_op jit(solution)/shard_map/pallas_call | solution.py:841
  475.5 13.9 %shard_map.180 = bf16[1024,2048]{1,0:T(8,128)(2,1)} custom-call(bf16[1024,1024]{1,0:T(8,128)(2,1)S(1)} %get-tuple-element.184.right_ref.refs_0_, bf16[1024,1024]{1,0:T(8,128)(2,1)S(1)} %get-tuple-element.185.right_ref.refs_1_, bf16[2,2048,512]{2,1,0:T(8,128)(2,1)} %pad_maximum_fusion.wide_ref.refs_2_, ...), custom_call_target="tpu_custom_call" | custom-call | flops 8589934 | bytes 20971 | tf_op jit(solution)/shard_map/pallas_call | solution.py:777
  526.1 13.8 %collective-permute-done.52 = bf16[512,512]{1,0:T(8,128)(2,1)S(1)} collective-permute-done((bf16[512,512]{1,0:T(8,128)(2,1)S(1)}, bf16[512,512]{1,0:T(8,128)(2,1)S(1)}, u32[]{:S(2)}, u32[]{:S(2)}) %collective-permute-start.52) | collective-permute-done | bytes 524320 | tf_op jit(solution)/shard_map/ppermute | solution.py:465
  558.3 17.3 %collective-permute-done.55 = bf16[512,512]{1,0:T(8,128)(2,1)S(1)} collective-permute-done((bf16[512,512]{1,0:T(8,128)(2,1)S(1)}, bf16[512,512]{1,0:T(8,128)(2,1)S(1)}, u32[]{:S(2)}, u32[]{:S(2)}) %collective-permute-start.55) | collective-permute-done | bytes 524320 | tf_op jit(solution)/shard_map/ppermute | solution.py:465
  579.3 22.0 %collective-permute-done.58 = bf16[512,1024]{1,0:T(8,128)(2,1)S(1)} collective-permute-done((bf16[512,1024]{1,0:T(8,128)(2,1)S(1)}, bf16[512,1024]{1,0:T(8,128)(2,1)S(1)}, u32[]{:S(2)}, u32[]{:S(2)}) %collective-permute-start.58) | collective-permute-done | bytes 1048608 | tf_op jit(solution)/shard_map/ppermute | solution.py:465
  633.4 15.5 %shard_map.186.right_ref.refs_0_ = bf16[1024,768]{1,0:T(8,128)(2,1)S(1)} custom-call(bf16[1024,2048]{1,0:T(8,128)(2,1)} %copy-done.37, bf16[2,256,1024]{2,1,0:T(8,128)(2,1)S(1)} %pad_maximum_fusion.17.refs_1_.weight_ref, bf16[1024,768]{1,0:T(8,128)(2,1)S(1)} %copy-done.28, f32[1024,128]{1,0:T(8,128)S(1)} %copy-done.15, f32[1024,128]{1,0:T(8,128)S(1)} %copy-done.11, ...), custom_call_target="tpu_custom_call" | custom-call | flops 6442450 | bytes 7340 | tf_op jit(solution)/shard_map/pallas_call | solution.py:691
  679.9 15.7 %shard_map.187.refs_0_.right_other_ref = bf16[1024,768]{1,0:T(8,128)(2,1)S(1)} custom-call(bf16[1024,2048]{1,0:T(8,128)(2,1)} %collective-permute-done.67.right_other_ref.grad_ref, bf16[2,256,1024]{2,1,0:T(8,128)(2,1)S(1)} %copy-done.3, bf16[1024,768]{1,0:T(8,128)(2,1)S(1)} %copy-done.26, f32[1024,128]{1,0:T(8,128)S(1)} %copy-done.15, ...), custom_call_target="tpu_custom_call" | custom-call | flops 6442450 | bytes 7340 | tf_op jit(solution)/shard_map/pallas_call | solution.py:691
  713.1 14.1 %shard_map.189 = bf16[2,2048,384]{2,1,0:T(8,128)(2,1)} custom-call(bf16[1024,2048]{1,0:T(8,128)(2,1)} %slice_dynamic-update-slice_fusion.12.rows_ref.left_ref, bf16[1024,2048]{1,0:T(8,128)(2,1)} %collective-permute-done.14.rows_ref.left_other_ref, bf16[1024,768]{1,0:T(8,128)(2,1)S(1)} %copy-done.5, bf16[1024,768]{1,0:T(8,128)(2,1)S(1)} %copy-done.7), custom_call_target="tpu_custom_call" | custom-call | flops 6442450 | bytes 14680 | tf_op jit(solution)/shard_map/pallas_call | solution.py:841
  761.6 22.1 %collective-permute-done.77 = bf16[256,2048]{1,0:T(8,128)(2,1)S(1)} collective-permute-done((bf16[256,2048]{1,0:T(8,128)(2,1)S(1)}, bf16[256,2048]{1,0:T(8,128)(2,1)S(1)}, u32[]{:S(2)}, u32[]{:S(2)}) %collective-permute-start.77) | collective-permute-done | bytes 1048608 | tf_op jit(solution)/shard_map/ppermute | solution.py:465
  790.6 13.7 %collective-permute-done.79 = bf16[128,2048]{1,0:T(8,128)(2,1)S(1)} collective-permute-done((bf16[128,2048]{1,0:T(8,128)(2,1)S(1)}, bf16[128,2048]{1,0:T(8,128)(2,1)S(1)}, u32[]{:S(2)}, u32[]{:S(2)}) %collective-permute-start.79) | collective-permute-done | bytes 524320 | tf_op jit(solution)/shard_map/ppermute | solution.py:465
  829.1 14.7 %collective-permute-done.81 = bf16[128,2048]{1,0:T(8,128)(2,1)S(1)} collective-permute-done((bf16[128,2048]{1,0:T(8,128)(2,1)S(1)}, bf16[128,2048]{1,0:T(8,128)(2,1)S(1)}, u32[]{:S(2)}, u32[]{:S(2)}) %collective-permute-start.81) | collective-permute-done | bytes 524320 | tf_op jit(solution)/shard_map/ppermute | solution.py:465
  (665 shorter events, 449.1 us)
Async XLA Ops:
  34.9 42.4 %collective-permute-start.3 = (bf16[256,2048]{1,0:T(8,128)(2,1)S(1)}, bf16[256,2048]{1,0:T(8,128)(2,1)S(1)}, u32[]{:S(2)}, u32[]{:S(2)}) collective-permute-start(bf16[256,2048]{1,0:T(8,128)(2,1)S(1)} %fusion.5), channel_id=1, source_target_pairs={{0,2},{2,0},{1,3},{3,1},{4,6},{6,4},{5,7},{7,5},{8,10},{10,8},{9,1... | collective-permute-start | bytes 3145736 | tf_op jit(solution)/shard_map/ppermute | solution.py:465
  35.8 41.5 %collective-permute-start.4 = (bf16[256,2048]{1,0:T(8,128)(2,1)S(1)}, bf16[256,2048]{1,0:T(8,128)(2,1)S(1)}, u32[]{:S(2)}, u32[]{:S(2)}) collective-permute-start(bf16[256,2048]{1,0:T(8,128)(2,1)S(1)} %fusion.5), channel_id=1, source_target_pairs={{0,1},{1,0},{2,3},{3,2},{4,5},{5,4},{6,7},{7,6},{8,9},{9,8},{10,11... | collective-permute-start | bytes 3145736 | tf_op jit(solution)/shard_map/ppermute | solution.py:465
  38.2 37.5 %collective-permute-start.5 = (bf16[1024,384]{1,0:T(8,128)(2,1)S(1)}, bf16[1024,384]{1,0:T(8,128)(2,1)S(1)}, u32[]{:S(2)}, u32[]{:S(2)}) collective-permute-start(bf16[1024,384]{1,0:T(8,128)(2,1)S(1)} %fusion.23), channel_id=1, source_target_pairs={{0,4},{4,0},{1,5},{5,1},{2,6},{6,2},{3,7},{7,3},{8,12},{12,8},{9,1... | collective-permute-start | bytes 2359304 | tf_op jit(solution)/shard_map/ppermute | solution.py:465
  41.5 34.3 %collective-permute-start.7 = (bf16[1024,384]{1,0:T(8,128)(2,1)S(1)}, bf16[1024,384]{1,0:T(8,128)(2,1)S(1)}, u32[]{:S(2)}, u32[]{:S(2)}) collective-permute-start(bf16[1024,384]{1,0:T(8,128)(2,1)S(1)} %fusion.23), channel_id=1, source_target_pairs={{0,16},{16,0},{1,17},{17,1},{2,18},{18,2},{3,19},{19,3},{4,20},{20... | collective-permute-start | bytes 2359304 | tf_op jit(solution)/shard_map/ppermute | solution.py:465
  111.0 34.3 %collective-permute-start.14 = (bf16[1024,2048]{1,0:T(8,128)(2,1)}, bf16[1024,2048]{1,0:T(8,128)(2,1)}, u32[]{:S(2)}, u32[]{:S(2)}) collective-permute-start(bf16[1024,2048]{1,0:T(8,128)(2,1)} %slice_dynamic-update-slice_fusion.12.rows_ref.left_ref), channel_id=1, source_target_pairs={{0,8},{8,0},{1,9},{9,1},{2,10},{10,2},{3,11},{11,3},{4,12},{12,4},... | collective-permute-start | bytes 12582920 | tf_op jit(solution)/shard_map/ppermute | solution.py:465
  119.9 43.5 %collective-permute-start.16 = (bf16[1024,512]{1,0:T(8,128)(2,1)S(1)}, bf16[1024,512]{1,0:T(8,128)(2,1)S(1)}, u32[]{:S(2)}, u32[]{:S(2)}) collective-permute-start(bf16[1024,512]{1,0:T(8,128)(2,1)S(1)} %copy-done.97), channel_id=1, source_target_pairs={{0,16},{16,0},{1,17},{17,1},{2,18},{18,2},{3,19},{19,3},{4,20},{20... | collective-permute-start | bytes 3145736 | tf_op jit(solution)/shard_map/ppermute | solution.py:465
  121.4 42.0 %collective-permute-start.15 = (bf16[512,512]{1,0:T(8,128)(2,1)}, bf16[512,512]{1,0:T(8,128)(2,1)S(1)}, u32[]{:S(2)}, u32[]{:S(2)}) collective-permute-start(bf16[512,512]{1,0:T(8,128)(2,1)} %get-tuple-element.146), channel_id=1, source_target_pairs={{0,4},{4,0},{1,5},{5,1},{2,6},{6,2},{3,7},{7,3},{8,12},{12,8},{9,1... | collective-permute-start | bytes 1572872 | tf_op jit(solution)/shard_map/ppermute | solution.py:465
  123.5 39.9 %collective-permute-start.12 = (bf16[128,1024]{1,0:T(8,128)(2,1)}, bf16[128,1024]{1,0:T(8,128)(2,1)S(1)}, u32[]{:S(2)}, u32[]{:S(2)}) collective-permute-start(bf16[128,1024]{1,0:T(8,128)(2,1)} %pad_maximum_fusion.38), channel_id=1, source_target_pairs={{0,16},{16,0},{1,17},{17,1},{2,18},{18,2},{3,19},{19,3},{4,20},{20... | collective-permute-start | bytes 786440 | tf_op jit(solution)/shard_map/ppermute | solution.py:465
  172.8 34.9 %collective-permute-start.20 = (bf16[1024,512]{1,0:T(8,128)(2,1)S(1)}, bf16[1024,512]{1,0:T(8,128)(2,1)}, u32[]{:S(2)}, u32[]{:S(2)}) collective-permute-start(bf16[1024,512]{1,0:T(8,128)(2,1)S(1)} %fusion.22), channel_id=1, source_target_pairs={{0,16},{16,0},{1,17},{17,1},{2,18},{18,2},{3,19},{19,3},{4,20},{20... | collective-permute-start | bytes 3145736 | tf_op jit(solution)/shard_map/ppermute | solution.py:465
  172.9 37.0 %collective-permute-start.21 = (bf16[256,2048]{1,0:T(8,128)(2,1)S(1)}, bf16[256,2048]{1,0:T(8,128)(2,1)}, u32[]{:S(2)}, u32[]{:S(2)}) collective-permute-start(bf16[256,2048]{1,0:T(8,128)(2,1)S(1)} %fusion.14), channel_id=1, source_target_pairs={{0,2},{2,0},{1,3},{3,1},{4,6},{6,4},{5,7},{7,5},{8,10},{10,8},{9,1... | collective-permute-start | bytes 3145736 | tf_op jit(solution)/shard_map/ppermute | solution.py:465
  173.0 36.9 %collective-permute-start.22 = (bf16[256,2048]{1,0:T(8,128)(2,1)S(1)}, bf16[256,2048]{1,0:T(8,128)(2,1)S(1)}, u32[]{:S(2)}, u32[]{:S(2)}) collective-permute-start(bf16[256,2048]{1,0:T(8,128)(2,1)S(1)} %fusion.14), channel_id=1, source_target_pairs={{0,1},{1,0},{2,3},{3,2},{4,5},{5,4},{6,7},{7,6},{8,9},{9,8},{10,11... | collective-permute-start | bytes 3145736 | tf_op jit(solution)/shard_map/ppermute | solution.py:465
  211.6 35.4 %collective-permute-start.24 = (bf16[256,2048]{1,0:T(8,128)(2,1)S(1)}, bf16[256,2048]{1,0:T(8,128)(2,1)S(1)}, u32[]{:S(2)}, u32[]{:S(2)}) collective-permute-start(bf16[256,2048]{1,0:T(8,128)(2,1)S(1)} %get-tuple-element.159), channel_id=1, source_target_pairs={{0,2},{2,0},{1,3},{3,1},{4,6},{6,4},{5,7},{7,5},{8,10},{10,8},{9,1... | collective-permute-start | bytes 3145736 | tf_op jit(solution)/shard_map/ppermute | solution.py:465
  214.7 33.2 %collective-permute-start.26 = (bf16[512,1024]{1,0:T(8,128)(2,1)S(1)}, bf16[512,1024]{1,0:T(8,128)(2,1)S(1)}, u32[]{:S(2)}, u32[]{:S(2)}) collective-permute-start(bf16[512,1024]{1,0:T(8,128)(2,1)S(1)} %copy-done.99), channel_id=1, source_target_pairs={{0,16},{16,0},{1,17},{17,1},{2,18},{18,2},{3,19},{19,3},{4,20},{20... | collective-permute-start | bytes 3145736 | tf_op jit(solution)/shard_map/ppermute | solution.py:465
  216.3 31.6 %collective-permute-start.25 = (bf16[256,1024]{1,0:T(8,128)(2,1)S(1)}, bf16[256,1024]{1,0:T(8,128)(2,1)S(1)}, u32[]{:S(2)}, u32[]{:S(2)}) collective-permute-start(bf16[256,1024]{1,0:T(8,128)(2,1)S(1)} %fusion.41), channel_id=1, source_target_pairs={{0,4},{4,0},{1,5},{5,1},{2,6},{6,2},{3,7},{7,3},{8,12},{12,8},{9,1... | collective-permute-start | bytes 1572872 | tf_op jit(solution)/shard_map/ppermute | solution.py:465
  275.4 38.7 %collective-permute-start.35 = (bf16[1024,2048]{1,0:T(8,128)(2,1)S(1)}, bf16[1024,2048]{1,0:T(8,128)(2,1)S(1)}, u32[]{:S(2)}, u32[]{:S(2)}) collective-permute-start(bf16[1024,2048]{1,0:T(8,128)(2,1)S(1)} %constant_dynamic-update-slice_fusion.3.grad_ref.right_ref), channel_id=1, source_target_pairs={{0,8},{8,0},{1,9},{9,1},{2,10},{10,2},{3,11},{11,3},{4,12},{12,4},... | collective-permute-start | bytes 12582920 | tf_op jit(solution)/shard_map/ppermute | solution.py:465
  275.4 36.8 %collective-permute-start.32 = (bf16[256,2048]{1,0:T(8,128)(2,1)S(1)}, bf16[256,2048]{1,0:T(8,128)(2,1)S(1)}, u32[]{:S(2)}, u32[]{:S(2)}) collective-permute-start(bf16[256,2048]{1,0:T(8,128)(2,1)S(1)} %multiply_convert_fusion), channel_id=1, source_target_pairs={{0,2},{2,0},{1,3},{3,1},{4,6},{6,4},{5,7},{7,5},{8,10},{10,8},{9,1... | collective-permute-start | bytes 3145736 | tf_op jit(solution)/shard_map/ppermute | solution.py:465
  276.3 36.8 %collective-permute-start.33 = (bf16[256,2048]{1,0:T(8,128)(2,1)S(1)}, bf16[256,2048]{1,0:T(8,128)(2,1)S(1)}, u32[]{:S(2)}, u32[]{:S(2)}) collective-permute-start(bf16[256,2048]{1,0:T(8,128)(2,1)S(1)} %multiply_convert_fusion), channel_id=1, source_target_pairs={{0,1},{1,0},{2,3},{3,2},{4,5},{5,4},{6,7},{7,6},{8,9},{9,8},{10,11... | collective-permute-start | bytes 3145736 | tf_op jit(solution)/shard_map/ppermute | solution.py:465
  279.0 35.1 %collective-permute-start.34 = (bf16[512,512]{1,0:T(8,128)(2,1)S(1)}, bf16[512,512]{1,0:T(8,128)(2,1)S(1)}, u32[]{:S(2)}, u32[]{:S(2)}) collective-permute-start(bf16[512,512]{1,0:T(8,128)(2,1)S(1)} %get-tuple-element.169), channel_id=1, source_target_pairs={{0,4},{4,0},{1,5},{5,1},{2,6},{6,2},{3,7},{7,3},{8,12},{12,8},{9,1... | collective-permute-start | bytes 1572872 | tf_op jit(solution)/shard_map/ppermute | solution.py:465
  280.1 33.9 %collective-permute-start.36 = (bf16[256,1024]{1,0:T(8,128)(2,1)S(1)}, bf16[256,1024]{1,0:T(8,128)(2,1)S(1)}, u32[]{:S(2)}, u32[]{:S(2)}) collective-permute-start(bf16[256,1024]{1,0:T(8,128)(2,1)S(1)} %collective-permute-done.25), channel_id=1, source_target_pairs={{0,16},{16,0},{1,17},{17,1},{2,18},{18,2},{3,19},{19,3},{4,20},{20... | collective-permute-start | bytes 1572872 | tf_op jit(solution)/shard_map/ppermute | solution.py:465
  441.1 33.4 %collective-permute-start.46 = (bf16[1024,2048]{1,0:T(8,128)(2,1)}, bf16[1024,2048]{1,0:T(8,128)(2,1)}, u32[]{:S(2)}, u32[]{:S(2)}) collective-permute-start(bf16[1024,2048]{1,0:T(8,128)(2,1)} %shard_map.178), channel_id=1, source_target_pairs={{0,8},{8,0},{1,9},{9,1},{2,10},{10,2},{3,11},{11,3},{4,12},{12,4},... | collective-permute-start | bytes 12582920 | tf_op jit(solution)/shard_map/ppermute | solution.py:465
  632.5 36.3 %collective-permute-start.67 = (bf16[1024,2048]{1,0:T(8,128)(2,1)S(1)}, bf16[1024,2048]{1,0:T(8,128)(2,1)}, u32[]{:S(2)}, u32[]{:S(2)}) collective-permute-start(bf16[1024,2048]{1,0:T(8,128)(2,1)S(1)} %constant_dynamic-update-slice_fusion.15.right_ref.grad_ref), channel_id=1, source_target_pairs={{0,8},{8,0},{1,9},{9,1},{2,10},{10,2},{3,11},{11,3},{4,12},{12,4},... | collective-permute-start | bytes 12582920 | tf_op jit(solution)/shard_map/ppermute | solution.py:465
  786.0 41.3 %collective-permute-start.83 = (bf16[1024,384]{1,0:T(8,128)(2,1)S(1)}, bf16[1024,384]{1,0:T(8,128)(2,1)S(1)}, u32[]{:S(2)}, u32[]{:S(2)}) collective-permute-start(bf16[1024,384]{1,0:T(8,128)(2,1)S(1)} %fusion.16), channel_id=1, source_target_pairs={{0,4},{4,0},{1,5},{5,1},{2,6},{6,2},{3,7},{7,3},{8,12},{12,8},{9,1... | collective-permute-start | bytes 2359304 | tf_op jit(solution)/shard_map/ppermute | solution.py:465
  788.3 39.0 %collective-permute-start.82 = (bf16[1024,384]{1,0:T(8,128)(2,1)S(1)}, bf16[1024,384]{1,0:T(8,128)(2,1)S(1)}, u32[]{:S(2)}, u32[]{:S(2)}) collective-permute-start(bf16[1024,384]{1,0:T(8,128)(2,1)S(1)} %get-tuple-element.234), channel_id=1, source_target_pairs={{0,16},{16,0},{1,17},{17,1},{2,18},{18,2},{3,19},{19,3},{4,20},{20... | collective-permute-start | bytes 2359304 | tf_op jit(solution)/shard_map/ppermute | solution.py:465
  810.4 39.1 %collective-permute-start.89 = (bf16[512,1024]{1,0:T(8,128)(2,1)S(1)}, bf16[512,1024]{1,0:T(8,128)(2,1)S(1)}, u32[]{:S(2)}, u32[]{:S(2)}) collective-permute-start(bf16[512,1024]{1,0:T(8,128)(2,1)S(1)} %dynamic-slice_convert_fusion), channel_id=1, source_target_pairs={{0,8},{8,0},{1,9},{9,1},{2,10},{10,2},{3,11},{11,3},{4,12},{12,4},... | collective-permute-start | bytes 3145736 | tf_op jit(solution)/shard_map/ppermute | solution.py:465
  (209 other events, 3707.3 us)

commit v4 on v3

--- a/solution.py
+++ b/solution.py
@@ -939,65 +939,54 @@
     grad_out = wide_bits(jnp.concatenate([cotangent_kept[0], cotangent_got], axis=0)) * live
     grad_own = low_bits(grad_out)
 
-    wide_x0, output_x, output_w, wide_w0a, norm_other = stage(
+    output_x, output_w, grad_u, grad_v, norm_other = stage(
         [
-            (wide_pieces[0], "x"),
             (output_piece, "x"),
             (output_piece, "w"),
-            (wide_pieces[0][:size], "w"),
+            (grad_own, "u"),
+            (grad_own, "v"),
             (norm_in, "c"),
         ],
         [qkv_wx, cotangent_got],
     )
     first = attend(norm_in, full_qkv, tables)
     output_w, norm_other, _ = lax.optimization_barrier((output_w, norm_other, first[0]))
-    output_wx = swap(output_w, "x")
+    output_wx, wide_w0a = stage([(output_w, "x"), (wide_pieces[0][:size], "w")])
     second = attend(norm_other, full_qkv, tables)
-    output_x, second, wide_w0a, wide_x0 = lax.optimization_barrier(
-        (output_x, second, wide_w0a, wide_x0)
+    output_x, second, grad_u, grad_v, wide_w0a = lax.optimization_barrier(
+        (output_x, second, grad_u, grad_v, wide_w0a)
     )
     norm_in = (norm_in, norm_other)
     turned, attended = zip(first, second)
     full_output = square(output_piece, output_w, output_x, output_wx, spots)
-    other = swap(ahead_rows([attended[1]], [full_output]), "c")
-    wide_w0b, wide_x1, grad_u, grad_v = stage(
-        [
-            (wide_pieces[0][size:], "w"),
-            (wide_pieces[1], "x"),
-            (grad_own, "u"),
-            (grad_own, "v"),
-        ],
-        [wide_w0a, wide_x0, first[0], second[0]],
+    other, grad_uv, grad_vu = stage(
+        [(ahead_rows([attended[1]], [full_output]), "c")] + corners(grad_u, grad_v)
     )
     total = ahead_rows([attended[0]], [full_output], [other])
-    from_v, from_u, down_w0, down_x = stage(
-        fold_sends(total) + [(down_pieces[0], "w"), (down_piece, "x")],
-        [wide_w0b, wide_x1, grad_u, grad_v],
-    )
+    grad_uv, grad_vu, total = lax.optimization_barrier((grad_uv, grad_vu, total))
+    grad_all = weave(grad_own, grad_u, grad_v, grad_uv, grad_vu)
+    from_v, from_u, wide_w0b, wide_x0, grad_other = stage(
+        fold_sends(total)
+        + [(wide_pieces[0][size:], "w"), (wide_pieces[0], "x"), (grad_all, "c")],
+        [wide_w0a],
+    )
+    grad_all = (grad_all, grad_other)
     kept, sends = fold(total, from_v, from_u)
-    from_u, from_v, grad_uv, grad_vu, wide_wx0 = stage(
+    from_u, from_v, down_w0, wide_wx0 = stage(
         sends
-        + corners(grad_u, grad_v)
-        + [(jnp.concatenate([wide_w0a, wide_w0b], axis=0), "x")],
-        [down_w0, down_x],
-    )
-    grad_all = weave(grad_own, grad_u, grad_v, grad_uv, grad_vu)
+        + [(down_pieces[0], "w"), (jnp.concatenate([wide_w0a, wide_w0b], axis=0), "x")],
+        [wide_x0, grad_other],
+    )
     after_attn = inputs + fold_end(kept, from_u, from_v)
     normed_mid, norm_mid_back = jax.vjp(layer_norm, after_attn)
     mid_own = low_bits(normed_mid)
-    mid_u, mid_v, grad_other, down_wx0, wide_w1a = stage(
-        [
-            (mid_own, "u"),
-            (mid_own, "v"),
-            (grad_all, "c"),
-            (down_w0, "x"),
-            (wide_pieces[1][:size], "w"),
-        ],
-        [wide_wx0, grad_uv],
-    )
-    grad_all = (grad_all, grad_other)
-    mid_uv, mid_vu, down_w1, wide_wx1a = stage(
-        corners(mid_u, mid_v) + [(down_pieces[1], "w"), (wide_w1a, "x")], [grad_other, down_wx0]
+    mid_u, mid_v, wide_w1a, down_x = stage(
+        [(mid_own, "u"), (mid_own, "v"), (wide_pieces[1][:size], "w"), (down_piece, "x")],
+        [wide_wx0, down_w0],
+    )
+    mid_uv, mid_vu, down_w1, down_wx0, wide_wx1a = stage(
+        corners(mid_u, mid_v) + [(down_pieces[1], "w"), (down_w0, "x"), (wide_w1a, "x")],
+        [down_x],
     )
     norm_mid = weave(mid_own, mid_u, mid_v, mid_uv, mid_vu)
     full_wide = [
@@ -1005,8 +994,14 @@
     ]
     half_rows = down_span // 2
     full_down = [square(down_pieces[0], down_w0, down_x[:half_rows], down_wx0, spots)]
-    norm_other, wide_w1b, down_wx1 = stage(
-        [(norm_mid, "c"), (wide_pieces[1][size:], "w"), (down_w1, "x")], [mid_uv, wide_wx1a]
+    norm_other, wide_w1b, wide_x1, down_wx1 = stage(
+        [
+            (norm_mid, "c"),
+            (wide_pieces[1][size:], "w"),
+            (wide_pieces[1], "x"),
+            (down_w1, "x"),
+        ],
+        [mid_uv, wide_wx1a, down_wx0],
     )
     norm_mid = (norm_mid, norm_other)
 
@@ -1042,9 +1037,9 @@
         (other, wide_outers[1], wide_g0a, near_got0)
     )
     far1, far_kept1, near1, near_kept1 = corner_blocks(wide_outers[1], w, x)
-    wide_g0b, far_got1 = stage([(far_sum0[size:], "w"), (far1, "x")], [wide_g0a, near_got0])
     total = back_rows(grad_wide[0], full_wide, [other])
-    from_v, from_u = stage(fold_sends(total))
+    from_v, from_u, far_got1 = stage(fold_sends(total) + [(far1, "x")])
+    ahead = ahead_rows(hidden[1], full_down)
     down_outers = [outer_rows([made[0][0], made[1][0]], grad_all) for made in passes]
     down_blocks = [corner_blocks(outer, w, x) for outer in down_outers]
     down_far, down_far_kept, down_near, down_near_kept = (
@@ -1052,19 +1047,25 @@
     )
     far_sum1 = plus(far_kept1, far_got1)
     kept, sends = fold(total, from_v, from_u)
-    from_u, from_v, wide_g1a, near_got1 = stage(
-        sends + [(far_sum1[:size], "w"), (near1, "x")], [wide_g0b, down_far]
-    )
-    ahead = ahead_rows(hidden[1], full_down)
+    from_u, from_v, wide_g0b, near_got1 = stage(
+        sends + [(far_sum0[size:], "w"), (near1, "x")], [down_far, ahead, far_got1]
+    )
     grad_norm_mid = fold_end(kept, from_u, from_v)
     grad_after = grad_out + norm_mid_back(grad_norm_mid)[0]
     after_own = low_bits(grad_after)
-    after_u, after_v, other, down_far_got = stage(
-        [(after_own, "u"), (after_own, "v"), (ahead, "c"), (down_far, "x")], [wide_g1a, near_got1]
+    after_u, after_v, other, wide_g1a, down_far_got = stage(
+        [
+            (after_own, "u"),
+            (after_own, "v"),
+            (ahead, "c"),
+            (far_sum1[:size], "w"),
+            (down_far, "x"),
+        ],
+        [wide_g0b, near_got1],
     )
     down_sum = plus(down_far_kept, down_far_got)
     after_uv, after_vu, wide_g1b, down_near_got = stage(
-        corners(after_u, after_v) + [(far_sum1[size:], "w"), (down_near, "x")], [other, down_far_got]
+        corners(after_u, after_v) + [(far_sum1[size:], "w"), (down_near, "x")], [other, down_far_got, wide_g1a]
     )
     total = ahead_rows(hidden[0], full_down, [other])
     after_all = weave(after_own, after_u, after_v, after_uv, after_vu)
@@ -1101,7 +1102,7 @@
     total = back_rows([first], [full_qkv], [other])
     qkv_got, total = lax.optimization_barrier((qkv_got, total))
     from_v, from_u, qkv_got = stage(
-        fold_sends(total) + [(plus(qkv_far_kept, qkv_got), "w")], [mixed_got, output_got]
+        fold_sends(total) + [(plus(qkv_far_kept, qkv_got), "w")]
     )
     kept, sends = fold(total, from_v, from_u)
     from_u, from_v, qkv_near_got = stage(sends + [(qkv_near, "x")])

time: 871 us -> 854 us (0.980)
  waiting for transfers between devices: 358 us -> 343 us
  other arithmetic: 78.5 us -> 67.8 us
  local copies, waits for them, and re-layouts: 80.5 us -> 91 us
    ppermute x93, waiting for transfers between devices: 358 us -> 343 us  [swap(): return lax.ppermute(value, axis, SWAP)]
    unnamed x311 -> x323, local copies, waits for them, and re-layouts: 39.2 us -> 49.4 us
  transfers between devices with their start and end apart: 93 -> 93, of which waited for: 38 -> 40; matrix products, arithmetic and copies ran while one was open for 15% -> 14% of each run, Pallas kernels for 25% -> 25%
where the time goes in v4:
time: 854 us; the launch traced here: 844 us
  waiting for transfers between devices  343 us (40%)
  Pallas kernels  243 us (28%)
  starting transfers between devices  94.9 us (11%)
  local copies, waits for them, and re-layouts  91 us (11%)
  other arithmetic  67.8 us (8%)
    ppermute x93, waiting for transfers between devices, swap(): return lax.ppermute(value, axis, SWAP)  343 us
    ppermute x93, starting transfers between devices, swap(): return lax.ppermute(value, axis, SWAP)  94.9 us
    pallas_call x6, Pallas kernels, outer_rows(): kernel_call(outer_kernel, (2, depth // tile), [left_spec, left_spec, righ...  62.2 us
    pallas_call x4, Pallas kernels, hidden_pass(): kernel_call(hidden_kernel, (2,), [whole(rows.shape), whole(grads.shape),...  51.3 us
    unnamed x323, local copies, waits for them, and re-layouts  49.4 us
    pallas_call x4, Pallas kernels, back_rows(): kernel_call(functools.partial(back_kernel, (len(lefts), len(added))), (wi...  43.9 us
    pallas_call x2, Pallas kernels, attend(): kernel_call(attend_kernel, (2,), [whole(rows.shape), pl.BlockSpec((1, wid...  31.9 us
    pallas_call x2, Pallas kernels, attend_back(): kernel_call(attend_back_kernel, (2,), [whole(grads.shape), pl.BlockSpec((...  31.4 us
  transfers between devices with their start and end apart: 93, of which 40 were waited for; matrix products, arithmetic and copies ran while one was open for 14% of the time, Pallas kernels for 25%

profile of v4, /device:TPU:0, one launch (start us, length us, event | category | flops | bytes accessed | tf_op | source)
XLA Modules:
  0.0 843.9 jit_solution(14773287721232961052)
XLA Ops:
  16.4 13.9 %collective-permute-done = bf16[128,2048]{1,0:T(8,128)(2,1)S(1)} collective-permute-done((bf16[128,2048]{1,0:T(8,128)(2,1)}, bf16[128,2048]{1,0:T(8,128)(2,1)S(1)}, u32[]{:S(2)}, u32[]{:S(2)}) %collective-permute-start) | collective-permute-done | bytes 524320 | tf_op jit(solution)/shard_map/ppermute | solution.py:465
  45.7 32.2 %collective-permute-done.5 = bf16[1024,384]{1,0:T(8,128)(2,1)S(1)} collective-permute-done((bf16[1024,384]{1,0:T(8,128)(2,1)S(1)}, bf16[1024,384]{1,0:T(8,128)(2,1)S(1)}, u32[]{:S(2)}, u32[]{:S(2)}) %collective-permute-start.5) | collective-permute-done | bytes 786464 | tf_op jit(solution)/shard_map/ppermute | solution.py:465
  88.2 19.4 %collective-permute-done.9 = bf16[128,2048]{1,0:T(8,128)(2,1)S(1)} collective-permute-done((bf16[128,2048]{1,0:T(8,128)(2,1)S(1)}, bf16[128,2048]{1,0:T(8,128)(2,1)S(1)}, u32[]{:S(2)}, u32[]{:S(2)}) %collective-permute-start.9) | collective-permute-done | bytes 524320 | tf_op jit(solution)/shard_map/ppermute | solution.py:465
  131.6 16.0 %shard_map.169 = (bf16[1024,768]{1,0:T(8,128)(2,1)S(1)}, bf16[1024,256]{1,0:T(8,128)(2,1)S(1)}) custom-call(bf16[1024,2048]{1,0:T(8,128)(2,1)} %slice_dynamic-update-slice_fusion.10.rows_ref.left_ref, bf16[2,2048,384]{2,1,0:T(8,128)(2,1)} %pad_maximum_fusion.3.weight_ref.refs_1_, f32[1024,128]{1,0:T(8,128)S(1)} %pad_maximum_fusion.31.cos_ref, ...), custom_call_target="tpu_custom_call" | custom-call | flops 6442450944 | bytes 7340032 | tf_op jit(solution)/shard_map/pallas_call | solution.py:632
  150.4 15.9 %shard_map.170 = (bf16[1024,768]{1,0:T(8,128)(2,1)S(1)}, bf16[1024,256]{1,0:T(8,128)(2,1)S(1)}) custom-call(bf16[1024,2048]{1,0:T(8,128)(2,1)} %collective-permute-done.14.rows_ref.left_other_ref, bf16[2,2048,384]{2,1,0:T(8,128)(2,1)} %pad_maximum_fusion.3.weight_ref.refs_1_, f32[1024,128]{1,0:T(8,128)S(1)} %pad_maximum_fusion.31.cos_ref, ...), custom_call_target="tpu_custom_call" | custom-call | flops 6442450944 | bytes 7340032 | tf_op jit(solution)/shard_map/pallas_call | solution.py:632
  203.7 32.0 %collective-permute-done.24 = bf16[512,512]{1,0:T(8,128)(2,1)S(1)} collective-permute-done((bf16[512,512]{1,0:T(8,128)(2,1)S(1)}, bf16[512,512]{1,0:T(8,128)(2,1)S(1)}, u32[]{:S(2)}, u32[]{:S(2)}) %collective-permute-start.24) | collective-permute-done | bytes 524320 | tf_op jit(solution)/shard_map/ppermute | solution.py:465
  245.3 13.1 %collective-permute-done.27 = bf16[128,2048]{1,0:T(8,128)(2,1)S(1)} collective-permute-done((bf16[128,2048]{1,0:T(8,128)(2,1)S(1)}, bf16[128,2048]{1,0:T(8,128)(2,1)S(1)}, u32[]{:S(2)}, u32[]{:S(2)}) %collective-permute-start.27) | collective-permute-done | bytes 524320 | tf_op jit(solution)/shard_map/ppermute | solution.py:465
  273.3 30.4 %collective-permute-done.31 = bf16[256,2048]{1,0:T(8,128)(2,1)S(1)} collective-permute-done((bf16[256,2048]{1,0:T(8,128)(2,1)S(1)}, bf16[256,2048]{1,0:T(8,128)(2,1)S(1)}, u32[]{:S(2)}, u32[]{:S(2)}) %collective-permute-start.31) | collective-permute-done | bytes 1048608 | tf_op jit(solution)/shard_map/ppermute | solution.py:465
  343.1 12.7 %shard_map.173 = (bf16[1024,512]{1,0:T(8,128)(2,1)S(1)}, bf16[1024,1024]{1,0:T(8,128)(2,1)S(1)}) custom-call(bf16[1024,2048]{1,0:T(8,128)(2,1)} %constant_dynamic-update-slice_fusion.7.rows_ref.left_ref, bf16[1024,2048]{1,0:T(8,128)(2,1)} %copy-done.31, bf16[2,2048,512]{2,1,0:T(8,128)(2,1)} %pad_maximum_fusion.wide_ref.refs_2_, ...), custom_call_target="tpu_custom_call" | custom-call | flops 6442450 | bytes 14680 | tf_op jit(solution)/shard_map/pallas_call | solution.py:731
  357.9 13.4 %shard_map.174 = (bf16[1024,512]{1,0:T(8,128)(2,1)S(1)}, bf16[1024,1024]{1,0:T(8,128)(2,1)S(1)}) custom-call(bf16[1024,2048]{1,0:T(8,128)(2,1)} %collective-permute-done.41.rows_ref.left_other_ref, bf16[1024,2048]{1,0:T(8,128)(2,1)} %copy-done.32, bf16[2,2048,512]{2,1,0:T(8,128)(2,1)} %pad_maximum_fusion.wide_ref.refs_2_, ...), custom_call_target="tpu_custom_call" | custom-call | flops 6442450 | bytes 14680 | tf_op jit(solution)/shard_map/pallas_call | solution.py:731
  378.8 14.3 %shard_map.176 = bf16[2,2048,512]{2,1,0:T(8,128)(2,1)} custom-call(bf16[1024,2048]{1,0:T(8,128)(2,1)} %constant_dynamic-update-slice_fusion.7.rows_ref.left_ref, bf16[1024,2048]{1,0:T(8,128)(2,1)} %collective-permute-done.41.rows_ref.left_other_ref, bf16[1024,1024]{1,0:T(8,128)(2,1)S(1)} %get-tuple-element.195.right_ref.refs_0_, ...), custom_call_target="tpu_custom_call" | custom-call | flops 8589934 | bytes 16777 | tf_op jit(solution)/shard_map/pallas_call | solution.py:841
  403.1 12.6 %shard_map.177 = (bf16[1024,512]{1,0:T(8,128)(2,1)S(1)}, bf16[1024,1024]{1,0:T(8,128)(2,1)S(1)}) custom-call(bf16[1024,2048]{1,0:T(8,128)(2,1)} %collective-permute-done.41.rows_ref.left_other_ref, bf16[1024,2048]{1,0:T(8,128)(2,1)} %copy-done.32, bf16[2,2048,512]{2,1,0:T(8,128)(2,1)} %pad_maximum_fusion.1.wide_ref.refs_3_, ...), custom_call_target="tpu_custom_call" | custom-call | flops 6442450 | bytes 14680 | tf_op jit(solution)/shard_map/pallas_call | solution.py:731
  421.4 12.8 %shard_map.178 = bf16[1024,2048]{1,0:T(8,128)(2,1)} custom-call(bf16[1024,1024]{1,0:T(8,128)(2,1)S(1)} %get-tuple-element.199.right_other_ref.refs_0_, bf16[1024,1024]{1,0:T(8,128)(2,1)S(1)} %get-tuple-element.200.refs_1_.right_other_ref, bf16[2,2048,512]{2,1,0:T(8,128)(2,1)} %pad_maximum_fusion.wide_ref.refs_2_, ...), custom_call_target="tpu_custom_call" | custom-call | flops 8589934 | bytes 20971 | tf_op jit(solution)/shard_map/pallas_call | solution.py:777
  440.9 12.6 %shard_map.175 = (bf16[1024,512]{1,0:T(8,128)(2,1)S(1)}, bf16[1024,1024]{1,0:T(8,128)(2,1)S(1)}) custom-call(bf16[1024,2048]{1,0:T(8,128)(2,1)} %constant_dynamic-update-slice_fusion.7.rows_ref.left_ref, bf16[1024,2048]{1,0:T(8,128)(2,1)} %copy-done.31, bf16[2,2048,512]{2,1,0:T(8,128)(2,1)} %pad_maximum_fusion.1.wide_ref.refs_3_, ...), custom_call_target="tpu_custom_call" | custom-call | flops 6442450 | bytes 14680 | tf_op jit(solution)/shard_map/pallas_call | solution.py:731
  453.6 14.8 %shard_map.179 = bf16[2,2048,512]{2,1,0:T(8,128)(2,1)} custom-call(bf16[1024,2048]{1,0:T(8,128)(2,1)} %constant_dynamic-update-slice_fusion.7.rows_ref.left_ref, bf16[1024,2048]{1,0:T(8,128)(2,1)} %collective-permute-done.41.rows_ref.left_other_ref, bf16[1024,1024]{1,0:T(8,128)(2,1)S(1)} %get-tuple-element.196.right_ref.refs_1_, bf16[1024,1024]{1,0:T(8,128)(2,1)S(1)} %copy-done.9), custom_call_target="tpu_custom_call" | custom-call | flops 8589934 | bytes 16777 | tf_op jit(solution)/shard_map/pallas_call | solution.py:841
  468.4 14.1 %shard_map.180 = bf16[1024,2048]{1,0:T(8,128)(2,1)} custom-call(bf16[1024,1024]{1,0:T(8,128)(2,1)S(1)} %get-tuple-element.195.right_ref.refs_0_, bf16[1024,1024]{1,0:T(8,128)(2,1)S(1)} %get-tuple-element.196.right_ref.refs_1_, bf16[2,2048,512]{2,1,0:T(8,128)(2,1)} %pad_maximum_fusion.wide_ref.refs_2_, ...), custom_call_target="tpu_custom_call" | custom-call | flops 8589934 | bytes 20971 | tf_op jit(solution)/shard_map/pallas_call | solution.py:777
  524.6 12.0 %collective-permute-done.52 = bf16[128,2048]{1,0:T(8,128)(2,1)S(1)} collective-permute-done((bf16[128,2048]{1,0:T(8,128)(2,1)S(1)}, bf16[128,2048]{1,0:T(8,128)(2,1)S(1)}, u32[]{:S(2)}, u32[]{:S(2)}) %collective-permute-start.52) | collective-permute-done | bytes 524320 | tf_op jit(solution)/shard_map/ppermute | solution.py:465
  552.6 18.8 %collective-permute-done.57 = bf16[512,1024]{1,0:T(8,128)(2,1)S(1)} collective-permute-done((bf16[512,1024]{1,0:T(8,128)(2,1)S(1)}, bf16[512,1024]{1,0:T(8,128)(2,1)S(1)}, u32[]{:S(2)}, u32[]{:S(2)}) %collective-permute-start.57) | collective-permute-done | bytes 1048608 | tf_op jit(solution)/shard_map/ppermute | solution.py:465
  571.8 10.8 %collective-permute-done.58 = bf16[256,2048]{1,0:T(8,128)(2,1)S(1)} collective-permute-done((bf16[256,2048]{1,0:T(8,128)(2,1)S(1)}, bf16[256,2048]{1,0:T(8,128)(2,1)S(1)}, u32[]{:S(2)}, u32[]{:S(2)}) %collective-permute-start.58) | collective-permute-done | bytes 1048608 | tf_op jit(solution)/shard_map/ppermute | solution.py:465
  614.9 15.8 %shard_map.186.right_ref.refs_0_ = bf16[1024,768]{1,0:T(8,128)(2,1)S(1)} custom-call(bf16[1024,2048]{1,0:T(8,128)(2,1)} %constant_dynamic-update-slice_fusion.15.right_ref.grad_ref, bf16[2,256,1024]{2,1,0:T(8,128)(2,1)S(1)} %pad_maximum_fusion.18.refs_1_.weight_ref, bf16[1024,768]{1,0:T(8,128)(2,1)S(1)} %copy-done.28, f32[1024,128]{1,0:T(8,128)S(1)} %copy-done.15, ...), custom_call_target="tpu_custom_call" | custom-call | flops 6442450 | bytes 7340 | tf_op jit(solution)/shard_map/pallas_call | solution.py:691
  662.9 15.7 %shard_map.187.refs_0_.right_other_ref = bf16[1024,768]{1,0:T(8,128)(2,1)S(1)} custom-call(bf16[1024,2048]{1,0:T(8,128)(2,1)} %collective-permute-done.67.right_other_ref.grad_ref, bf16[2,256,1024]{2,1,0:T(8,128)(2,1)S(1)} %copy-done.3, bf16[1024,768]{1,0:T(8,128)(2,1)S(1)} %copy-done.26, f32[1024,128]{1,0:T(8,128)S(1)} %copy-done.15, ...), custom_call_target="tpu_custom_call" | custom-call | flops 6442450 | bytes 7340 | tf_op jit(solution)/shard_map/pallas_call | solution.py:691
  693.9 14.1 %shard_map.189 = bf16[2,2048,384]{2,1,0:T(8,128)(2,1)} custom-call(bf16[1024,2048]{1,0:T(8,128)(2,1)} %slice_dynamic-update-slice_fusion.10.rows_ref.left_ref, bf16[1024,2048]{1,0:T(8,128)(2,1)} %collective-permute-done.14.rows_ref.left_other_ref, bf16[1024,768]{1,0:T(8,128)(2,1)S(1)} %copy-done.5, bf16[1024,768]{1,0:T(8,128)(2,1)S(1)} %copy-done.7), custom_call_target="tpu_custom_call" | custom-call | flops 6442450 | bytes 14680 | tf_op jit(solution)/shard_map/pallas_call | solution.py:841
  740.9 16.6 %collective-permute-done.76 = bf16[256,2048]{1,0:T(8,128)(2,1)S(1)} collective-permute-done((bf16[256,2048]{1,0:T(8,128)(2,1)S(1)}, bf16[256,2048]{1,0:T(8,128)(2,1)S(1)}, u32[]{:S(2)}, u32[]{:S(2)}) %collective-permute-start.76) | collective-permute-done | bytes 1048608 | tf_op jit(solution)/shard_map/ppermute | solution.py:465
  768.9 18.1 %collective-permute-done.78 = bf16[128,2048]{1,0:T(8,128)(2,1)S(1)} collective-permute-done((bf16[128,2048]{1,0:T(8,128)(2,1)S(1)}, bf16[128,2048]{1,0:T(8,128)(2,1)S(1)}, u32[]{:S(2)}, u32[]{:S(2)}) %collective-permute-start.78) | collective-permute-done | bytes 524320 | tf_op jit(solution)/shard_map/ppermute | solution.py:465
  (677 shorter events, 437.7 us)
Async XLA Ops:
  36.9 42.4 %collective-permute-start.4 = (bf16[256,2048]{1,0:T(8,128)(2,1)S(1)}, bf16[256,2048]{1,0:T(8,128)(2,1)S(1)}, u32[]{:S(2)}, u32[]{:S(2)}) collective-permute-start(bf16[256,2048]{1,0:T(8,128)(2,1)S(1)} %fusion.5), channel_id=1, source_target_pairs={{0,2},{2,0},{1,3},{3,1},{4,6},{6,4},{5,7},{7,5},{8,10},{10,8},{9,1... | collective-permute-start | bytes 3145736 | tf_op jit(solution)/shard_map/ppermute | solution.py:465
  38.1 41.3 %collective-permute-start.6 = (bf16[256,2048]{1,0:T(8,128)(2,1)S(1)}, bf16[256,2048]{1,0:T(8,128)(2,1)S(1)}, u32[]{:S(2)}, u32[]{:S(2)}) collective-permute-start(bf16[256,2048]{1,0:T(8,128)(2,1)S(1)} %fusion.5), channel_id=1, source_target_pairs={{0,1},{1,0},{2,3},{3,2},{4,5},{5,4},{6,7},{7,6},{8,9},{9,8},{10,11... | collective-permute-start | bytes 3145736 | tf_op jit(solution)/shard_map/ppermute | solution.py:465
  39.7 38.3 %collective-permute-start.5 = (bf16[1024,384]{1,0:T(8,128)(2,1)S(1)}, bf16[1024,384]{1,0:T(8,128)(2,1)S(1)}, u32[]{:S(2)}, u32[]{:S(2)}) collective-permute-start(bf16[1024,384]{1,0:T(8,128)(2,1)S(1)} %fusion.23), channel_id=1, source_target_pairs={{0,4},{4,0},{1,5},{5,1},{2,6},{6,2},{3,7},{7,3},{8,12},{12,8},{9,1... | collective-permute-start | bytes 2359304 | tf_op jit(solution)/shard_map/ppermute | solution.py:465
  42.8 35.2 %collective-permute-start.7 = (bf16[1024,384]{1,0:T(8,128)(2,1)S(1)}, bf16[1024,384]{1,0:T(8,128)(2,1)S(1)}, u32[]{:S(2)}, u32[]{:S(2)}) collective-permute-start(bf16[1024,384]{1,0:T(8,128)(2,1)S(1)} %fusion.23), channel_id=1, source_target_pairs={{0,16},{16,0},{1,17},{17,1},{2,18},{18,2},{3,19},{19,3},{4,20},{20... | collective-permute-start | bytes 2359304 | tf_op jit(solution)/shard_map/ppermute | solution.py:465
  79.3 35.6 %collective-permute-start.11 = (bf16[1024,384]{1,0:T(8,128)(2,1)S(1)}, bf16[1024,384]{1,0:T(8,128)(2,1)S(1)}, u32[]{:S(2)}, u32[]{:S(2)}) collective-permute-start(bf16[1024,384]{1,0:T(8,128)(2,1)S(1)} %collective-permute-done.5), channel_id=1, source_target_pairs={{0,16},{16,0},{1,17},{17,1},{2,18},{18,2},{3,19},{19,3},{4,20},{20... | collective-permute-start | bytes 2359304 | tf_op jit(solution)/shard_map/ppermute | solution.py:465
  128.9 39.0 %collective-permute-start.15 = (bf16[256,2048]{1,0:T(8,128)(2,1)S(1)}, bf16[256,2048]{1,0:T(8,128)(2,1)}, u32[]{:S(2)}, u32[]{:S(2)}) collective-permute-start(bf16[256,2048]{1,0:T(8,128)(2,1)S(1)} %copy-done.66), channel_id=1, source_target_pairs={{0,2},{2,0},{1,3},{3,1},{4,6},{6,4},{5,7},{7,5},{8,10},{10,8},{9,1... | collective-permute-start | bytes 3145736 | tf_op jit(solution)/shard_map/ppermute | solution.py:465
  130.6 37.3 %collective-permute-start.16 = (bf16[256,2048]{1,0:T(8,128)(2,1)S(1)}, bf16[256,2048]{1,0:T(8,128)(2,1)S(1)}, u32[]{:S(2)}, u32[]{:S(2)}) collective-permute-start(bf16[256,2048]{1,0:T(8,128)(2,1)S(1)} %copy-done.66), channel_id=1, source_target_pairs={{0,1},{1,0},{2,3},{3,2},{4,5},{5,4},{6,7},{7,6},{8,9},{9,8},{10,11... | collective-permute-start | bytes 3145736 | tf_op jit(solution)/shard_map/ppermute | solution.py:465
  131.1 36.8 %collective-permute-start.12 = (bf16[128,1024]{1,0:T(8,128)(2,1)S(1)}, bf16[128,1024]{1,0:T(8,128)(2,1)}, u32[]{:S(2)}, u32[]{:S(2)}) collective-permute-start(bf16[128,1024]{1,0:T(8,128)(2,1)S(1)} %pad_maximum_fusion.38), channel_id=1, source_target_pairs={{0,16},{16,0},{1,17},{17,1},{2,18},{18,2},{3,19},{19,3},{4,20},{20... | collective-permute-start | bytes 786440 | tf_op jit(solution)/shard_map/ppermute | solution.py:465
  200.8 38.1 %collective-permute-start.26 = (bf16[1024,2048]{1,0:T(8,128)(2,1)S(1)}, bf16[1024,2048]{1,0:T(8,128)(2,1)S(1)}, u32[]{:S(2)}, u32[]{:S(2)}) collective-permute-start(bf16[1024,2048]{1,0:T(8,128)(2,1)S(1)} %constant_dynamic-update-slice_fusion.1.grad_ref.right_ref), channel_id=1, source_target_pairs={{0,8},{8,0},{1,9},{9,1},{2,10},{10,2},{3,11},{11,3},{4,12},{12,4},... | collective-permute-start | bytes 12582920 | tf_op jit(solution)/shard_map/ppermute | solution.py:465
  200.9 34.9 %collective-permute-start.22 = (bf16[256,2048]{1,0:T(8,128)(2,1)S(1)}, bf16[256,2048]{1,0:T(8,128)(2,1)S(1)}, u32[]{:S(2)}, u32[]{:S(2)}) collective-permute-start(bf16[256,2048]{1,0:T(8,128)(2,1)S(1)} %get-tuple-element.168), channel_id=1, source_target_pairs={{0,1},{1,0},{2,3},{3,2},{4,5},{5,4},{6,7},{7,6},{8,9},{9,8},{10,11... | collective-permute-start | bytes 3145736 | tf_op jit(solution)/shard_map/ppermute | solution.py:465
  201.5 36.5 %collective-permute-start.23 = (bf16[256,2048]{1,0:T(8,128)(2,1)S(1)}, bf16[256,2048]{1,0:T(8,128)(2,1)S(1)}, u32[]{:S(2)}, u32[]{:S(2)}) collective-permute-start(bf16[256,2048]{1,0:T(8,128)(2,1)S(1)} %get-tuple-element.169), channel_id=1, source_target_pairs={{0,2},{2,0},{1,3},{3,1},{4,6},{6,4},{5,7},{7,5},{8,10},{10,8},{9,1... | collective-permute-start | bytes 3145736 | tf_op jit(solution)/shard_map/ppermute | solution.py:465
  202.1 36.8 %collective-permute-start.25 = (bf16[1024,512]{1,0:T(8,128)(2,1)S(1)}, bf16[1024,512]{1,0:T(8,128)(2,1)S(1)}, u32[]{:S(2)}, u32[]{:S(2)}) collective-permute-start(bf16[1024,512]{1,0:T(8,128)(2,1)S(1)} %copy-done.100), channel_id=1, source_target_pairs={{0,16},{16,0},{1,17},{17,1},{2,18},{18,2},{3,19},{19,3},{4,20},{20... | collective-permute-start | bytes 3145736 | tf_op jit(solution)/shard_map/ppermute | solution.py:465
  269.1 34.5 %collective-permute-start.31 = (bf16[256,2048]{1,0:T(8,128)(2,1)S(1)}, bf16[256,2048]{1,0:T(8,128)(2,1)S(1)}, u32[]{:S(2)}, u32[]{:S(2)}) collective-permute-start(bf16[256,2048]{1,0:T(8,128)(2,1)S(1)} %multiply_convert_fusion), channel_id=1, source_target_pairs={{0,2},{2,0},{1,3},{3,1},{4,6},{6,4},{5,7},{7,5},{8,10},{10,8},{9,1... | collective-permute-start | bytes 3145736 | tf_op jit(solution)/shard_map/ppermute | solution.py:465
  269.2 35.4 %collective-permute-start.34 = (bf16[512,1024]{1,0:T(8,128)(2,1)S(1)}, bf16[512,1024]{1,0:T(8,128)(2,1)S(1)}, u32[]{:S(2)}, u32[]{:S(2)}) collective-permute-start(bf16[512,1024]{1,0:T(8,128)(2,1)S(1)} %fusion.20), channel_id=1, source_target_pairs={{0,16},{16,0},{1,17},{17,1},{2,18},{18,2},{3,19},{19,3},{4,20},{20... | collective-permute-start | bytes 3145736 | tf_op jit(solution)/shard_map/ppermute | solution.py:465
  269.8 35.9 %collective-permute-start.32 = (bf16[256,2048]{1,0:T(8,128)(2,1)S(1)}, bf16[256,2048]{1,0:T(8,128)(2,1)S(1)}, u32[]{:S(2)}, u32[]{:S(2)}) collective-permute-start(bf16[256,2048]{1,0:T(8,128)(2,1)S(1)} %multiply_convert_fusion), channel_id=1, source_target_pairs={{0,1},{1,0},{2,3},{3,2},{4,5},{5,4},{6,7},{7,6},{8,9},{9,8},{10,11... | collective-permute-start | bytes 3145736 | tf_op jit(solution)/shard_map/ppermute | solution.py:465
  341.7 35.8 %collective-permute-start.40 = (bf16[1024,512]{1,0:T(8,128)(2,1)S(1)}, bf16[1024,512]{1,0:T(8,128)(2,1)}, u32[]{:S(2)}, u32[]{:S(2)}) collective-permute-start(bf16[1024,512]{1,0:T(8,128)(2,1)S(1)} %copy-done.51), channel_id=1, source_target_pairs={{0,16},{16,0},{1,17},{17,1},{2,18},{18,2},{3,19},{19,3},{4,20},{20... | collective-permute-start | bytes 3145736 | tf_op jit(solution)/shard_map/ppermute | solution.py:465
  545.7 40.2 %collective-permute-start.56 = (bf16[1024,2048]{1,0:T(8,128)(2,1)S(1)}, bf16[1024,2048]{1,0:T(8,128)(2,1)S(1)}, u32[]{:S(2)}, u32[]{:S(2)}) collective-permute-start(bf16[1024,2048]{1,0:T(8,128)(2,1)S(1)} %copy-done.68), channel_id=1, source_target_pairs={{0,8},{8,0},{1,9},{9,1},{2,10},{10,2},{3,11},{11,3},{4,12},{12,4},... | collective-permute-start | bytes 12582920 | tf_op jit(solution)/shard_map/ppermute | solution.py:465
  546.2 36.5 %collective-permute-start.58 = (bf16[256,2048]{1,0:T(8,128)(2,1)S(1)}, bf16[256,2048]{1,0:T(8,128)(2,1)S(1)}, u32[]{:S(2)}, u32[]{:S(2)}) collective-permute-start(bf16[256,2048]{1,0:T(8,128)(2,1)S(1)} %fusion.17), channel_id=1, source_target_pairs={{0,2},{2,0},{1,3},{3,1},{4,6},{6,4},{5,7},{7,5},{8,10},{10,8},{9,1... | collective-permute-start | bytes 3145736 | tf_op jit(solution)/shard_map/ppermute | solution.py:465
  547.2 37.6 %collective-permute-start.59 = (bf16[256,2048]{1,0:T(8,128)(2,1)S(1)}, bf16[256,2048]{1,0:T(8,128)(2,1)S(1)}, u32[]{:S(2)}, u32[]{:S(2)}) collective-permute-start(bf16[256,2048]{1,0:T(8,128)(2,1)S(1)} %fusion.17), channel_id=1, source_target_pairs={{0,1},{1,0},{2,3},{3,2},{4,5},{5,4},{6,7},{7,6},{8,9},{9,8},{10,11... | collective-permute-start | bytes 3145736 | tf_op jit(solution)/shard_map/ppermute | solution.py:465
  548.5 37.4 %collective-permute-start.60 = (bf16[512,512]{1,0:T(8,128)(2,1)S(1)}, bf16[512,512]{1,0:T(8,128)(2,1)S(1)}, u32[]{:S(2)}, u32[]{:S(2)}) collective-permute-start(bf16[512,512]{1,0:T(8,128)(2,1)S(1)} %get-tuple-element.219), channel_id=1, source_target_pairs={{0,4},{4,0},{1,5},{5,1},{2,6},{6,2},{3,7},{7,3},{8,12},{12,8},{9,1... | collective-permute-start | bytes 1572872 | tf_op jit(solution)/shard_map/ppermute | solution.py:465
  613.7 37.0 %collective-permute-start.67 = (bf16[1024,2048]{1,0:T(8,128)(2,1)}, bf16[1024,2048]{1,0:T(8,128)(2,1)}, u32[]{:S(2)}, u32[]{:S(2)}) collective-permute-start(bf16[1024,2048]{1,0:T(8,128)(2,1)} %constant_dynamic-update-slice_fusion.15.right_ref.grad_ref), channel_id=1, source_target_pairs={{0,8},{8,0},{1,9},{9,1},{2,10},{10,2},{3,11},{11,3},{4,12},{12,4},... | collective-permute-start | bytes 12582920 | tf_op jit(solution)/shard_map/ppermute | solution.py:465
  764.1 38.3 %collective-permute-start.82 = (bf16[1024,384]{1,0:T(8,128)(2,1)S(1)}, bf16[1024,384]{1,0:T(8,128)(2,1)S(1)}, u32[]{:S(2)}, u32[]{:S(2)}) collective-permute-start(bf16[1024,384]{1,0:T(8,128)(2,1)S(1)} %fusion.16), channel_id=1, source_target_pairs={{0,4},{4,0},{1,5},{5,1},{2,6},{6,2},{3,7},{7,3},{8,12},{12,8},{9,1... | collective-permute-start | bytes 2359304 | tf_op jit(solution)/shard_map/ppermute | solution.py:465
  767.1 35.3 %collective-permute-start.81 = (bf16[1024,384]{1,0:T(8,128)(2,1)S(1)}, bf16[1024,384]{1,0:T(8,128)(2,1)S(1)}, u32[]{:S(2)}, u32[]{:S(2)}) collective-permute-start(bf16[1024,384]{1,0:T(8,128)(2,1)S(1)} %get-tuple-element.243), channel_id=1, source_target_pairs={{0,16},{16,0},{1,17},{17,1},{2,18},{18,2},{3,19},{19,3},{4,20},{20... | collective-permute-start | bytes 2359304 | tf_op jit(solution)/shard_map/ppermute | solution.py:465
  792.9 36.7 %collective-permute-start.89 = (bf16[512,1024]{1,0:T(8,128)(2,1)S(1)}, bf16[512,1024]{1,0:T(8,128)(2,1)S(1)}, u32[]{:S(2)}, u32[]{:S(2)}) collective-permute-start(bf16[512,1024]{1,0:T(8,128)(2,1)S(1)} %dynamic-slice_convert_fusion), channel_id=1, source_target_pairs={{0,8},{8,0},{1,9},{9,1},{2,10},{10,2},{3,11},{11,3},{4,12},{12,4},... | collective-permute-start | bytes 3145736 | tf_op jit(solution)/shard_map/ppermute | solution.py:465
  (215 other events, 3604.8 us)

commit v5 on v4

--- a/solution.py
+++ b/solution.py
@@ -1135,25 +1135,32 @@
         return join_columns(kept, swap(low_bits(sent), "c"), c, sizes)
 
     def rows_home(total):
-        kept, sent = both_halves(total, u, 1)
+        count = total.shape[1] // 4
+        even = jnp.concatenate([total[:, :count], total[:, 2 * count : 3 * count]], axis=1)
+        odd = jnp.concatenate([total[:, count : 2 * count], total[:, 3 * count :]], axis=1)
+        sent = jnp.where(v == 0, odd, even)
+        parts = join(jnp.where(v == 0, even, odd)[None], swap(sent, "v")[None], v, 0)
+        kept, sent = both_halves(parts, u, 2)
         parts = join(kept[None], swap(sent, "u")[None], u, 0)
         kept, sent = both_halves(parts, c, 0)
-        parts = join(kept, swap(sent, "c"), c, 0)
-        kept, sent = both_halves(parts, v, 2)
-        return wide_bits(join(kept[None], swap(sent, "v")[None], v, 0))
+        return wide_bits(join(kept[0][:, None], swap(sent, "c")[0][:, None], c, 1))
 
     gate_grad, up_grad = columns_home(wide_total, (wide_columns,) * 2)
     query_grad, key_grad, value_grad = columns_home(qkv_total, (HEAD_DIM,) * 3)
+    output_grad, down_grad = rows_home(output_total), rows_home(down_total)
+    token_got, gate_grad, up_grad, down_grad, output_grad = lax.optimization_barrier(
+        (token_got, gate_grad, up_grad, down_grad, output_grad)
+    )
     return (
         join(mixed[None, :tok_rows], mixed_got[None], w, 0),
         join(token_grad[None, :tok_rows], wide_bits(token_got)[None], w, 0),
         query_grad,
         key_grad,
         value_grad,
-        rows_home(output_total).reshape(output_weight.shape),
+        output_grad.reshape(output_weight.shape),
         gate_grad,
         up_grad,
-        rows_home(down_total).reshape(down_weight.shape),
+        down_grad.reshape(down_weight.shape),
     )
 
 

time: 854 us -> 848 us (level)
    unnamed x323 -> x329, local copies, waits for them, and re-layouts: 49.4 us -> 49.1 us
    concatenate x35 -> x33, other arithmetic: 23.4 us -> 23.3 us  [join(): return jnp.concatenate([low, high], axis=axis)]
  transfers between devices with their start and end apart: 93 -> 93, of which waited for: 40 -> 35; matrix products, arithmetic and copies ran while one was open for 14% -> 13% of each run, Pallas kernels for 25% -> 25%
where the time goes in v5:
time: 848 us; the launch traced here: 838 us
  waiting for transfers between devices  339 us (40%)
  Pallas kernels  243 us (29%)
  starting transfers between devices  95.5 us (11%)
  local copies, waits for them, and re-layouts  92.1 us (11%)
  other arithmetic  64.9 us (8%)
    ppermute x93, waiting for transfers between devices, swap(): return lax.ppermute(value, axis, SWAP)  339 us
    ppermute x93, starting transfers between devices, swap(): return lax.ppermute(value, axis, SWAP)  95.5 us
    pallas_call x6, Pallas kernels, outer_rows(): kernel_call(outer_kernel, (2, depth // tile), [left_spec, left_spec, righ...  62.2 us
    pallas_call x4, Pallas kernels, hidden_pass(): kernel_call(hidden_kernel, (2,), [whole(rows.shape), whole(grads.shape),...  51.3 us
    unnamed x329, local copies, waits for them, and re-layouts  49.1 us
    pallas_call x4, Pallas kernels, back_rows(): kernel_call(functools.partial(back_kernel, (len(lefts), len(added))), (wi...  44.1 us
    pallas_call x2, Pallas kernels, attend(): kernel_call(attend_kernel, (2,), [whole(rows.shape), pl.BlockSpec((1, wid...  31.9 us
    pallas_call x2, Pallas kernels, attend_back(): kernel_call(attend_back_kernel, (2,), [whole(grads.shape), pl.BlockSpec((...  31 us
  transfers between devices with their start and end apart: 93, of which 35 were waited for; matrix products, arithmetic and copies ran while one was open for 13% of the time, Pallas kernels for 25%

profile of v5, /device:TPU:0, one launch (start us, length us, event | category | flops | bytes accessed | tf_op | source)
XLA Modules:
  0.0 838.1 jit_solution(2364761400487026539)
XLA Ops:
  16.4 13.9 %collective-permute-done = bf16[128,2048]{1,0:T(8,128)(2,1)S(1)} collective-permute-done((bf16[128,2048]{1,0:T(8,128)(2,1)}, bf16[128,2048]{1,0:T(8,128)(2,1)S(1)}, u32[]{:S(2)}, u32[]{:S(2)}) %collective-permute-start) | collective-permute-done | bytes 524320 | tf_op jit(solution)/shard_map/ppermute | solution.py:465
  45.7 32.3 %collective-permute-done.5 = bf16[1024,384]{1,0:T(8,128)(2,1)S(1)} collective-permute-done((bf16[1024,384]{1,0:T(8,128)(2,1)S(1)}, bf16[1024,384]{1,0:T(8,128)(2,1)S(1)}, u32[]{:S(2)}, u32[]{:S(2)}) %collective-permute-start.5) | collective-permute-done | bytes 786464 | tf_op jit(solution)/shard_map/ppermute | solution.py:465
  88.2 19.4 %collective-permute-done.9 = bf16[128,2048]{1,0:T(8,128)(2,1)S(1)} collective-permute-done((bf16[128,2048]{1,0:T(8,128)(2,1)S(1)}, bf16[128,2048]{1,0:T(8,128)(2,1)S(1)}, u32[]{:S(2)}, u32[]{:S(2)}) %collective-permute-start.9) | collective-permute-done | bytes 524320 | tf_op jit(solution)/shard_map/ppermute | solution.py:465
  131.6 16.0 %shard_map.169 = (bf16[1024,768]{1,0:T(8,128)(2,1)S(1)}, bf16[1024,256]{1,0:T(8,128)(2,1)S(1)}) custom-call(bf16[1024,2048]{1,0:T(8,128)(2,1)} %slice_dynamic-update-slice_fusion.10.rows_ref.left_ref, bf16[2,2048,384]{2,1,0:T(8,128)(2,1)} %pad_maximum_fusion.3.weight_ref.refs_1_, f32[1024,128]{1,0:T(8,128)S(1)} %pad_maximum_fusion.30.cos_ref, ...), custom_call_target="tpu_custom_call" | custom-call | flops 6442450944 | bytes 7340032 | tf_op jit(solution)/shard_map/pallas_call | solution.py:632
  150.4 15.9 %shard_map.170 = (bf16[1024,768]{1,0:T(8,128)(2,1)S(1)}, bf16[1024,256]{1,0:T(8,128)(2,1)S(1)}) custom-call(bf16[1024,2048]{1,0:T(8,128)(2,1)} %collective-permute-done.14.rows_ref.left_other_ref, bf16[2,2048,384]{2,1,0:T(8,128)(2,1)} %pad_maximum_fusion.3.weight_ref.refs_1_, f32[1024,128]{1,0:T(8,128)S(1)} %pad_maximum_fusion.30.cos_ref, ...), custom_call_target="tpu_custom_call" | custom-call | flops 6442450944 | bytes 7340032 | tf_op jit(solution)/shard_map/pallas_call | solution.py:632
  203.7 32.0 %collective-permute-done.24 = bf16[512,512]{1,0:T(8,128)(2,1)S(1)} collective-permute-done((bf16[512,512]{1,0:T(8,128)(2,1)S(1)}, bf16[512,512]{1,0:T(8,128)(2,1)S(1)}, u32[]{:S(2)}, u32[]{:S(2)}) %collective-permute-start.24) | collective-permute-done | bytes 524320 | tf_op jit(solution)/shard_map/ppermute | solution.py:465
  245.3 13.1 %collective-permute-done.27 = bf16[128,2048]{1,0:T(8,128)(2,1)S(1)} collective-permute-done((bf16[128,2048]{1,0:T(8,128)(2,1)S(1)}, bf16[128,2048]{1,0:T(8,128)(2,1)S(1)}, u32[]{:S(2)}, u32[]{:S(2)}) %collective-permute-start.27) | collective-permute-done | bytes 524320 | tf_op jit(solution)/shard_map/ppermute | solution.py:465
  273.2 30.4 %collective-permute-done.31 = bf16[256,2048]{1,0:T(8,128)(2,1)S(1)} collective-permute-done((bf16[256,2048]{1,0:T(8,128)(2,1)S(1)}, bf16[256,2048]{1,0:T(8,128)(2,1)S(1)}, u32[]{:S(2)}, u32[]{:S(2)}) %collective-permute-start.31) | collective-permute-done | bytes 1048608 | tf_op jit(solution)/shard_map/ppermute | solution.py:465
  343.2 12.7 %shard_map.173 = (bf16[1024,512]{1,0:T(8,128)(2,1)S(1)}, bf16[1024,1024]{1,0:T(8,128)(2,1)S(1)}) custom-call(bf16[1024,2048]{1,0:T(8,128)(2,1)} %constant_dynamic-update-slice_fusion.7.rows_ref.left_ref, bf16[1024,2048]{1,0:T(8,128)(2,1)} %copy-done.29, bf16[2,2048,512]{2,1,0:T(8,128)(2,1)} %pad_maximum_fusion.wide_ref.refs_2_, ...), custom_call_target="tpu_custom_call" | custom-call | flops 6442450 | bytes 14680 | tf_op jit(solution)/shard_map/pallas_call | solution.py:731
  358.0 13.4 %shard_map.174 = (bf16[1024,512]{1,0:T(8,128)(2,1)S(1)}, bf16[1024,1024]{1,0:T(8,128)(2,1)S(1)}) custom-call(bf16[1024,2048]{1,0:T(8,128)(2,1)} %collective-permute-done.41.rows_ref.left_other_ref, bf16[1024,2048]{1,0:T(8,128)(2,1)} %copy-done.30, bf16[2,2048,512]{2,1,0:T(8,128)(2,1)} %pad_maximum_fusion.wide_ref.refs_2_, ...), custom_call_target="tpu_custom_call" | custom-call | flops 6442450 | bytes 14680 | tf_op jit(solution)/shard_map/pallas_call | solution.py:731
  378.9 14.4 %shard_map.176 = bf16[2,2048,512]{2,1,0:T(8,128)(2,1)} custom-call(bf16[1024,2048]{1,0:T(8,128)(2,1)} %constant_dynamic-update-slice_fusion.7.rows_ref.left_ref, bf16[1024,2048]{1,0:T(8,128)(2,1)} %collective-permute-done.41.rows_ref.left_other_ref, bf16[1024,1024]{1,0:T(8,128)(2,1)S(1)} %get-tuple-element.200.right_ref.refs_0_, ...), custom_call_target="tpu_custom_call" | custom-call | flops 8589934 | bytes 16777 | tf_op jit(solution)/shard_map/pallas_call | solution.py:841
  403.2 12.6 %shard_map.177 = (bf16[1024,512]{1,0:T(8,128)(2,1)S(1)}, bf16[1024,1024]{1,0:T(8,128)(2,1)S(1)}) custom-call(bf16[1024,2048]{1,0:T(8,128)(2,1)} %collective-permute-done.41.rows_ref.left_other_ref, bf16[1024,2048]{1,0:T(8,128)(2,1)} %copy-done.30, bf16[2,2048,512]{2,1,0:T(8,128)(2,1)} %pad_maximum_fusion.1.wide_ref.refs_3_, ...), custom_call_target="tpu_custom_call" | custom-call | flops 6442450 | bytes 14680 | tf_op jit(solution)/shard_map/pallas_call | solution.py:731
  421.5 12.8 %shard_map.178 = bf16[1024,2048]{1,0:T(8,128)(2,1)} custom-call(bf16[1024,1024]{1,0:T(8,128)(2,1)S(1)} %get-tuple-element.204.right_other_ref.refs_0_, bf16[1024,1024]{1,0:T(8,128)(2,1)S(1)} %get-tuple-element.205.refs_1_.right_other_ref, bf16[2,2048,512]{2,1,0:T(8,128)(2,1)} %pad_maximum_fusion.wide_ref.refs_2_, ...), custom_call_target="tpu_custom_call" | custom-call | flops 8589934 | bytes 20971 | tf_op jit(solution)/shard_map/pallas_call | solution.py:777
  441.0 12.6 %shard_map.175 = (bf16[1024,512]{1,0:T(8,128)(2,1)S(1)}, bf16[1024,1024]{1,0:T(8,128)(2,1)S(1)}) custom-call(bf16[1024,2048]{1,0:T(8,128)(2,1)} %constant_dynamic-update-slice_fusion.7.rows_ref.left_ref, bf16[1024,2048]{1,0:T(8,128)(2,1)} %copy-done.29, bf16[2,2048,512]{2,1,0:T(8,128)(2,1)} %pad_maximum_fusion.1.wide_ref.refs_3_, ...), custom_call_target="tpu_custom_call" | custom-call | flops 6442450 | bytes 14680 | tf_op jit(solution)/shard_map/pallas_call | solution.py:731
  453.7 14.8 %shard_map.179 = bf16[2,2048,512]{2,1,0:T(8,128)(2,1)} custom-call(bf16[1024,2048]{1,0:T(8,128)(2,1)} %constant_dynamic-update-slice_fusion.7.rows_ref.left_ref, bf16[1024,2048]{1,0:T(8,128)(2,1)} %collective-permute-done.41.rows_ref.left_other_ref, bf16[1024,1024]{1,0:T(8,128)(2,1)S(1)} %get-tuple-element.201.right_ref.refs_1_, bf16[1024,1024]{1,0:T(8,128)(2,1)S(1)} %copy-done.7), custom_call_target="tpu_custom_call" | custom-call | flops 8589934 | bytes 16777 | tf_op jit(solution)/shard_map/pallas_call | solution.py:841
  468.5 14.1 %shard_map.180 = bf16[1024,2048]{1,0:T(8,128)(2,1)} custom-call(bf16[1024,1024]{1,0:T(8,128)(2,1)S(1)} %get-tuple-element.200.right_ref.refs_0_, bf16[1024,1024]{1,0:T(8,128)(2,1)S(1)} %get-tuple-element.201.right_ref.refs_1_, bf16[2,2048,512]{2,1,0:T(8,128)(2,1)} %pad_maximum_fusion.wide_ref.refs_2_, ...), custom_call_target="tpu_custom_call" | custom-call | flops 8589934 | bytes 20971 | tf_op jit(solution)/shard_map/pallas_call | solution.py:777
  524.8 12.1 %collective-permute-done.52 = bf16[128,2048]{1,0:T(8,128)(2,1)S(1)} collective-permute-done((bf16[128,2048]{1,0:T(8,128)(2,1)S(1)}, bf16[128,2048]{1,0:T(8,128)(2,1)S(1)}, u32[]{:S(2)}, u32[]{:S(2)}) %collective-permute-start.52) | collective-permute-done | bytes 524320 | tf_op jit(solution)/shard_map/ppermute | solution.py:465
  551.8 19.7 %collective-permute-done.57 = bf16[512,1024]{1,0:T(8,128)(2,1)S(1)} collective-permute-done((bf16[512,1024]{1,0:T(8,128)(2,1)S(1)}, bf16[512,1024]{1,0:T(8,128)(2,1)S(1)}, u32[]{:S(2)}, u32[]{:S(2)}) %collective-permute-start.57) | collective-permute-done | bytes 1048608 | tf_op jit(solution)/shard_map/ppermute | solution.py:465
  616.0 15.3 %shard_map.186.right_ref.refs_0_ = bf16[1024,768]{1,0:T(8,128)(2,1)S(1)} custom-call(bf16[1024,2048]{1,0:T(8,128)(2,1)} %constant_dynamic-update-slice_fusion.15.right_ref.grad_ref, bf16[2,256,1024]{2,1,0:T(8,128)(2,1)S(1)} %pad_maximum_fusion.18.refs_1_.weight_ref, bf16[1024,768]{1,0:T(8,128)(2,1)S(1)} %copy-done.25, f32[1024,128]{1,0:T(8,128)S(1)} %copy-done.13, ...), custom_call_target="tpu_custom_call" | custom-call | flops 6442450 | bytes 7340 | tf_op jit(solution)/shard_map/pallas_call | solution.py:691
  664.7 15.7 %shard_map.187.refs_0_.right_other_ref = bf16[1024,768]{1,0:T(8,128)(2,1)S(1)} custom-call(bf16[1024,2048]{1,0:T(8,128)(2,1)} %copy-done.44, bf16[2,256,1024]{2,1,0:T(8,128)(2,1)S(1)} %copy-done.3, bf16[1024,768]{1,0:T(8,128)(2,1)S(1)} %copy-done.23, f32[1024,128]{1,0:T(8,128)S(1)} %copy-done.13, f32[1024,128]{1,0:T(8,128)S(1)} %copy-done.9, ...), custom_call_target="tpu_custom_call" | custom-call | flops 6442450 | bytes 7340 | tf_op jit(solution)/shard_map/pallas_call | solution.py:691
  690.9 14.1 %shard_map.189 = bf16[2,2048,384]{2,1,0:T(8,128)(2,1)} custom-call(bf16[1024,2048]{1,0:T(8,128)(2,1)} %slice_dynamic-update-slice_fusion.10.rows_ref.left_ref, bf16[1024,2048]{1,0:T(8,128)(2,1)} %collective-permute-done.14.rows_ref.left_other_ref, bf16[1024,768]{1,0:T(8,128)(2,1)S(1)} %shard_map.186.right_ref.refs_0_, ...), custom_call_target="tpu_custom_call" | custom-call | flops 6442450 | bytes 14680 | tf_op jit(solution)/shard_map/pallas_call | solution.py:841
  734.7 27.1 %collective-permute-done.88 = bf16[2,128,256]{2,1,0:T(8,128)(2,1)S(1)} collective-permute-done((bf16[2,128,256]{2,1,0:T(8,128)(2,1)S(1)}, bf16[2,128,256]{2,1,0:T(8,128)(2,1)S(1)}, u32[]{:S(2)}, u32[]{:S(2)}) %collective-permute-start.88) | collective-permute-done | bytes 131104 | tf_op jit(solution)/shard_map/ppermute | solution.py:465
  769.3 17.3 %collective-permute-done.78 = bf16[128,2048]{1,0:T(8,128)(2,1)S(1)} collective-permute-done((bf16[128,2048]{1,0:T(8,128)(2,1)S(1)}, bf16[128,2048]{1,0:T(8,128)(2,1)S(1)}, u32[]{:S(2)}, u32[]{:S(2)}) %collective-permute-start.78) | collective-permute-done | bytes 524320 | tf_op jit(solution)/shard_map/ppermute | solution.py:465
  808.6 20.9 %collective-permute-done.83 = bf16[2,512,256]{2,1,0:T(8,128)(2,1)S(1)} collective-permute-done((bf16[2,512,256]{2,1,0:T(8,128)(2,1)S(1)}, bf16[2,512,256]{2,1,0:T(8,128)(2,1)S(1)}, u32[]{:S(2)}, u32[]{:S(2)}) %collective-permute-start.83) | collective-permute-done | bytes 524320 | tf_op jit(solution)/shard_map/ppermute | solution.py:465
  (684 shorter events, 411.6 us)
Async XLA Ops:
  36.9 42.4 %collective-permute-start.4 = (bf16[256,2048]{1,0:T(8,128)(2,1)S(1)}, bf16[256,2048]{1,0:T(8,128)(2,1)S(1)}, u32[]{:S(2)}, u32[]{:S(2)}) collective-permute-start(bf16[256,2048]{1,0:T(8,128)(2,1)S(1)} %fusion.5), channel_id=1, source_target_pairs={{0,2},{2,0},{1,3},{3,1},{4,6},{6,4},{5,7},{7,5},{8,10},{10,8},{9,1... | collective-permute-start | bytes 3145736 | tf_op jit(solution)/shard_map/ppermute | solution.py:465
  38.1 41.2 %collective-permute-start.6 = (bf16[256,2048]{1,0:T(8,128)(2,1)S(1)}, bf16[256,2048]{1,0:T(8,128)(2,1)S(1)}, u32[]{:S(2)}, u32[]{:S(2)}) collective-permute-start(bf16[256,2048]{1,0:T(8,128)(2,1)S(1)} %fusion.5), channel_id=1, source_target_pairs={{0,1},{1,0},{2,3},{3,2},{4,5},{5,4},{6,7},{7,6},{8,9},{9,8},{10,11... | collective-permute-start | bytes 3145736 | tf_op jit(solution)/shard_map/ppermute | solution.py:465
  39.7 38.3 %collective-permute-start.5 = (bf16[1024,384]{1,0:T(8,128)(2,1)S(1)}, bf16[1024,384]{1,0:T(8,128)(2,1)S(1)}, u32[]{:S(2)}, u32[]{:S(2)}) collective-permute-start(bf16[1024,384]{1,0:T(8,128)(2,1)S(1)} %fusion.23), channel_id=1, source_target_pairs={{0,4},{4,0},{1,5},{5,1},{2,6},{6,2},{3,7},{7,3},{8,12},{12,8},{9,1... | collective-permute-start | bytes 2359304 | tf_op jit(solution)/shard_map/ppermute | solution.py:465
  42.7 35.2 %collective-permute-start.7 = (bf16[1024,384]{1,0:T(8,128)(2,1)S(1)}, bf16[1024,384]{1,0:T(8,128)(2,1)S(1)}, u32[]{:S(2)}, u32[]{:S(2)}) collective-permute-start(bf16[1024,384]{1,0:T(8,128)(2,1)S(1)} %fusion.23), channel_id=1, source_target_pairs={{0,16},{16,0},{1,17},{17,1},{2,18},{18,2},{3,19},{19,3},{4,20},{20... | collective-permute-start | bytes 2359304 | tf_op jit(solution)/shard_map/ppermute | solution.py:465
  79.3 35.6 %collective-permute-start.11 = (bf16[1024,384]{1,0:T(8,128)(2,1)S(1)}, bf16[1024,384]{1,0:T(8,128)(2,1)S(1)}, u32[]{:S(2)}, u32[]{:S(2)}) collective-permute-start(bf16[1024,384]{1,0:T(8,128)(2,1)S(1)} %collective-permute-done.5), channel_id=1, source_target_pairs={{0,16},{16,0},{1,17},{17,1},{2,18},{18,2},{3,19},{19,3},{4,20},{20... | collective-permute-start | bytes 2359304 | tf_op jit(solution)/shard_map/ppermute | solution.py:465
  128.9 39.0 %collective-permute-start.15 = (bf16[256,2048]{1,0:T(8,128)(2,1)S(1)}, bf16[256,2048]{1,0:T(8,128)(2,1)}, u32[]{:S(2)}, u32[]{:S(2)}) collective-permute-start(bf16[256,2048]{1,0:T(8,128)(2,1)S(1)} %copy-done.66), channel_id=1, source_target_pairs={{0,2},{2,0},{1,3},{3,1},{4,6},{6,4},{5,7},{7,5},{8,10},{10,8},{9,1... | collective-permute-start | bytes 3145736 | tf_op jit(solution)/shard_map/ppermute | solution.py:465
  130.5 37.3 %collective-permute-start.16 = (bf16[256,2048]{1,0:T(8,128)(2,1)S(1)}, bf16[256,2048]{1,0:T(8,128)(2,1)S(1)}, u32[]{:S(2)}, u32[]{:S(2)}) collective-permute-start(bf16[256,2048]{1,0:T(8,128)(2,1)S(1)} %copy-done.66), channel_id=1, source_target_pairs={{0,1},{1,0},{2,3},{3,2},{4,5},{5,4},{6,7},{7,6},{8,9},{9,8},{10,11... | collective-permute-start | bytes 3145736 | tf_op jit(solution)/shard_map/ppermute | solution.py:465
  131.0 36.8 %collective-permute-start.12 = (bf16[128,1024]{1,0:T(8,128)(2,1)S(1)}, bf16[128,1024]{1,0:T(8,128)(2,1)}, u32[]{:S(2)}, u32[]{:S(2)}) collective-permute-start(bf16[128,1024]{1,0:T(8,128)(2,1)S(1)} %pad_maximum_fusion.39), channel_id=1, source_target_pairs={{0,16},{16,0},{1,17},{17,1},{2,18},{18,2},{3,19},{19,3},{4,20},{20... | collective-permute-start | bytes 786440 | tf_op jit(solution)/shard_map/ppermute | solution.py:465
  200.8 38.1 %collective-permute-start.26 = (bf16[1024,2048]{1,0:T(8,128)(2,1)S(1)}, bf16[1024,2048]{1,0:T(8,128)(2,1)S(1)}, u32[]{:S(2)}, u32[]{:S(2)}) collective-permute-start(bf16[1024,2048]{1,0:T(8,128)(2,1)S(1)} %constant_dynamic-update-slice_fusion.1.grad_ref.right_ref), channel_id=1, source_target_pairs={{0,8},{8,0},{1,9},{9,1},{2,10},{10,2},{3,11},{11,3},{4,12},{12,4},... | collective-permute-start | bytes 12582920 | tf_op jit(solution)/shard_map/ppermute | solution.py:465
  200.9 34.9 %collective-permute-start.22 = (bf16[256,2048]{1,0:T(8,128)(2,1)S(1)}, bf16[256,2048]{1,0:T(8,128)(2,1)S(1)}, u32[]{:S(2)}, u32[]{:S(2)}) collective-permute-start(bf16[256,2048]{1,0:T(8,128)(2,1)S(1)} %get-tuple-element.173), channel_id=1, source_target_pairs={{0,1},{1,0},{2,3},{3,2},{4,5},{5,4},{6,7},{7,6},{8,9},{9,8},{10,11... | collective-permute-start | bytes 3145736 | tf_op jit(solution)/shard_map/ppermute | solution.py:465
  201.4 36.5 %collective-permute-start.23 = (bf16[256,2048]{1,0:T(8,128)(2,1)S(1)}, bf16[256,2048]{1,0:T(8,128)(2,1)S(1)}, u32[]{:S(2)}, u32[]{:S(2)}) collective-permute-start(bf16[256,2048]{1,0:T(8,128)(2,1)S(1)} %get-tuple-element.174), channel_id=1, source_target_pairs={{0,2},{2,0},{1,3},{3,1},{4,6},{6,4},{5,7},{7,5},{8,10},{10,8},{9,1... | collective-permute-start | bytes 3145736 | tf_op jit(solution)/shard_map/ppermute | solution.py:465
  202.1 36.7 %collective-permute-start.25 = (bf16[1024,512]{1,0:T(8,128)(2,1)S(1)}, bf16[1024,512]{1,0:T(8,128)(2,1)S(1)}, u32[]{:S(2)}, u32[]{:S(2)}) collective-permute-start(bf16[1024,512]{1,0:T(8,128)(2,1)S(1)} %copy-done.100), channel_id=1, source_target_pairs={{0,16},{16,0},{1,17},{17,1},{2,18},{18,2},{3,19},{19,3},{4,20},{20... | collective-permute-start | bytes 3145736 | tf_op jit(solution)/shard_map/ppermute | solution.py:465
  269.2 35.4 %collective-permute-start.34 = (bf16[512,1024]{1,0:T(8,128)(2,1)S(1)}, bf16[512,1024]{1,0:T(8,128)(2,1)S(1)}, u32[]{:S(2)}, u32[]{:S(2)}) collective-permute-start(bf16[512,1024]{1,0:T(8,128)(2,1)S(1)} %fusion.20), channel_id=1, source_target_pairs={{0,16},{16,0},{1,17},{17,1},{2,18},{18,2},{3,19},{19,3},{4,20},{20... | collective-permute-start | bytes 3145736 | tf_op jit(solution)/shard_map/ppermute | solution.py:465
  269.8 35.9 %collective-permute-start.32 = (bf16[256,2048]{1,0:T(8,128)(2,1)S(1)}, bf16[256,2048]{1,0:T(8,128)(2,1)S(1)}, u32[]{:S(2)}, u32[]{:S(2)}) collective-permute-start(bf16[256,2048]{1,0:T(8,128)(2,1)S(1)} %multiply_convert_fusion), channel_id=1, source_target_pairs={{0,1},{1,0},{2,3},{3,2},{4,5},{5,4},{6,7},{7,6},{8,9},{9,8},{10,11... | collective-permute-start | bytes 3145736 | tf_op jit(solution)/shard_map/ppermute | solution.py:465
  341.7 35.8 %collective-permute-start.40 = (bf16[1024,512]{1,0:T(8,128)(2,1)S(1)}, bf16[1024,512]{1,0:T(8,128)(2,1)}, u32[]{:S(2)}, u32[]{:S(2)}) collective-permute-start(bf16[1024,512]{1,0:T(8,128)(2,1)S(1)} %copy-done.50), channel_id=1, source_target_pairs={{0,16},{16,0},{1,17},{17,1},{2,18},{18,2},{3,19},{19,3},{4,20},{20... | collective-permute-start | bytes 3145736 | tf_op jit(solution)/shard_map/ppermute | solution.py:465
  545.9 40.1 %collective-permute-start.56 = (bf16[1024,2048]{1,0:T(8,128)(2,1)S(1)}, bf16[1024,2048]{1,0:T(8,128)(2,1)S(1)}, u32[]{:S(2)}, u32[]{:S(2)}) collective-permute-start(bf16[1024,2048]{1,0:T(8,128)(2,1)S(1)} %copy-done.68), channel_id=1, source_target_pairs={{0,8},{8,0},{1,9},{9,1},{2,10},{10,2},{3,11},{11,3},{4,12},{12,4},... | collective-permute-start | bytes 12582920 | tf_op jit(solution)/shard_map/ppermute | solution.py:465
  546.4 36.5 %collective-permute-start.58 = (bf16[256,2048]{1,0:T(8,128)(2,1)S(1)}, bf16[256,2048]{1,0:T(8,128)(2,1)S(1)}, u32[]{:S(2)}, u32[]{:S(2)}) collective-permute-start(bf16[256,2048]{1,0:T(8,128)(2,1)S(1)} %fusion.17), channel_id=1, source_target_pairs={{0,2},{2,0},{1,3},{3,1},{4,6},{6,4},{5,7},{7,5},{8,10},{10,8},{9,1... | collective-permute-start | bytes 3145736 | tf_op jit(solution)/shard_map/ppermute | solution.py:465
  546.5 38.4 %collective-permute-start.59 = (bf16[256,2048]{1,0:T(8,128)(2,1)S(1)}, bf16[256,2048]{1,0:T(8,128)(2,1)S(1)}, u32[]{:S(2)}, u32[]{:S(2)}) collective-permute-start(bf16[256,2048]{1,0:T(8,128)(2,1)S(1)} %fusion.17), channel_id=1, source_target_pairs={{0,1},{1,0},{2,3},{3,2},{4,5},{5,4},{6,7},{7,6},{8,9},{9,8},{10,11... | collective-permute-start | bytes 3145736 | tf_op jit(solution)/shard_map/ppermute | solution.py:465
  547.8 38.1 %collective-permute-start.60 = (bf16[512,512]{1,0:T(8,128)(2,1)S(1)}, bf16[512,512]{1,0:T(8,128)(2,1)S(1)}, u32[]{:S(2)}, u32[]{:S(2)}) collective-permute-start(bf16[512,512]{1,0:T(8,128)(2,1)S(1)} %get-tuple-element.224), channel_id=1, source_target_pairs={{0,4},{4,0},{1,5},{5,1},{2,6},{6,2},{3,7},{7,3},{8,12},{12,8},{9,1... | collective-permute-start | bytes 1572872 | tf_op jit(solution)/shard_map/ppermute | solution.py:465
  614.5 36.9 %collective-permute-start.67 = (bf16[1024,2048]{1,0:T(8,128)(2,1)}, bf16[1024,2048]{1,0:T(8,128)(2,1)S(1)}, u32[]{:S(2)}, u32[]{:S(2)}) collective-permute-start(bf16[1024,2048]{1,0:T(8,128)(2,1)} %constant_dynamic-update-slice_fusion.15.right_ref.grad_ref), channel_id=1, source_target_pairs={{0,8},{8,0},{1,9},{9,1},{2,10},{10,2},{3,11},{11,3},{4,12},{12,4},... | collective-permute-start | bytes 12582920 | tf_op jit(solution)/shard_map/ppermute | solution.py:465
  711.0 51.0 %collective-permute-start.73 = (bf16[128,2048]{1,0:T(8,128)(2,1)}, bf16[128,2048]{1,0:T(8,128)(2,1)S(1)}, u32[]{:S(2)}, u32[]{:S(2)}) collective-permute-start(bf16[128,2048]{1,0:T(8,128)(2,1)} %slice.506), channel_id=1, source_target_pairs={{0,4},{4,0},{1,5},{5,1},{2,6},{6,2},{3,7},{7,3},{8,12},{12,8},{9,1... | collective-permute-start | bytes 1572872 | tf_op jit(solution)/shard_map/ppermute | solution.py:465
  764.4 37.8 %collective-permute-start.91 = (bf16[1024,384]{1,0:T(8,128)(2,1)S(1)}, bf16[1024,384]{1,0:T(8,128)(2,1)S(1)}, u32[]{:S(2)}, u32[]{:S(2)}) collective-permute-start(bf16[1024,384]{1,0:T(8,128)(2,1)S(1)} %fusion.16), channel_id=1, source_target_pairs={{0,4},{4,0},{1,5},{5,1},{2,6},{6,2},{3,7},{7,3},{8,12},{12,8},{9,1... | collective-permute-start | bytes 2359304 | tf_op jit(solution)/shard_map/ppermute | solution.py:465
  766.9 35.3 %collective-permute-start.90 = (bf16[1024,384]{1,0:T(8,128)(2,1)S(1)}, bf16[1024,384]{1,0:T(8,128)(2,1)S(1)}, u32[]{:S(2)}, u32[]{:S(2)}) collective-permute-start(bf16[1024,384]{1,0:T(8,128)(2,1)S(1)} %copy-done.105), channel_id=1, source_target_pairs={{0,16},{16,0},{1,17},{17,1},{2,18},{18,2},{3,19},{19,3},{4,20},{20... | collective-permute-start | bytes 2359304 | tf_op jit(solution)/shard_map/ppermute | solution.py:465
  794.0 36.0 %collective-permute-start.81 = (bf16[512,1024]{1,0:T(8,128)(2,1)S(1)}, bf16[512,1024]{1,0:T(8,128)(2,1)S(1)}, u32[]{:S(2)}, u32[]{:S(2)}) collective-permute-start(bf16[512,1024]{1,0:T(8,128)(2,1)S(1)} %dynamic-slice_convert_fusion), channel_id=1, source_target_pairs={{0,8},{8,0},{1,9},{9,1},{2,10},{10,2},{3,11},{11,3},{4,12},{12,4},... | collective-permute-start | bytes 3145736 | tf_op jit(solution)/shard_map/ppermute | solution.py:465
  (218 other events, 3663.9 us)

commit v6 on v5

--- a/solution.py
+++ b/solution.py
@@ -622,7 +622,7 @@
         scores = scores * HEAD_DIM ** (-0.5)
         scores = jnp.where(pos_col_ref[at, :] >= key_pos, scores, -1e30)
         shifted = jnp.exp(scores - jnp.max(scores, axis=1, keepdims=True))
-        soft = shifted / jnp.sum(shifted, axis=1, keepdims=True)
+        soft = shifted * (1.0 / jnp.sum(shifted, axis=1, keepdims=True))
         out_ref[at, :] = low_bits(dot(low_bits(soft), turned_ref[:, 2 * HEAD_DIM :]))
 
 
@@ -673,7 +673,7 @@
         scores = dot(keys, queries, ACROSS) * scale
         scores = jnp.where(pos_row_ref[:, at] >= key_pos, scores, -1e30)
         shifted = jnp.exp(scores - jnp.max(scores, axis=0, keepdims=True))
-        soft = shifted / jnp.sum(shifted, axis=0, keepdims=True)
+        soft = shifted * (1.0 / jnp.sum(shifted, axis=0, keepdims=True))
         grad_soft = dot(values, grads, ACROSS)
         centre = jnp.sum(soft * grad_soft, axis=0, keepdims=True)
         grad_scores = low_bits(soft * (grad_soft - centre) * scale)

time: 848 us -> 848 us (level)
  no operation moved by 1% of the time
where the time goes in v6:
time: 848 us; the launch traced here: 838 us
  waiting for transfers between devices  339 us (40%)
  Pallas kernels  243 us (29%)
  starting transfers between devices  95.5 us (11%)
  local copies, waits for them, and re-layouts  92.1 us (11%)
  other arithmetic  64.9 us (8%)
    ppermute x93, waiting for transfers between devices, swap(): return lax.ppermute(value, axis, SWAP)  339 us
    ppermute x93, starting transfers between devices, swap(): return lax.ppermute(value, axis, SWAP)  95.5 us
    pallas_call x6, Pallas kernels, outer_rows(): kernel_call(outer_kernel, (2, depth // tile), [left_spec, left_spec, righ...  62.2 us
    pallas_call x4, Pallas kernels, hidden_pass(): kernel_call(hidden_kernel, (2,), [whole(rows.shape), whole(grads.shape),...  51.3 us
    unnamed x329, local copies, waits for them, and re-layouts  49.1 us
    pallas_call x4, Pallas kernels, back_rows(): kernel_call(functools.partial(back_kernel, (len(lefts), len(added))), (wi...  44.1 us
    pallas_call x2, Pallas kernels, attend(): kernel_call(attend_kernel, (2,), [whole(rows.shape), pl.BlockSpec((1, wid...  31.9 us
    pallas_call x2, Pallas kernels, attend_back(): kernel_call(attend_back_kernel, (2,), [whole(grads.shape), pl.BlockSpec((...  31 us
  transfers between devices with their start and end apart: 93, of which 35 were waited for; matrix products, arithmetic and copies ran while one was open for 13% of the time, Pallas kernels for 25%

profile of v6, /device:TPU:0, one launch (start us, length us, event | category | flops | bytes accessed | tf_op | source)
XLA Modules:
  0.0 838.1 jit_solution(2364761400487026539)
XLA Ops:
  16.4 13.9 %collective-permute-done = bf16[128,2048]{1,0:T(8,128)(2,1)S(1)} collective-permute-done((bf16[128,2048]{1,0:T(8,128)(2,1)}, bf16[128,2048]{1,0:T(8,128)(2,1)S(1)}, u32[]{:S(2)}, u32[]{:S(2)}) %collective-permute-start) | collective-permute-done | bytes 524320 | tf_op jit(solution)/shard_map/ppermute | solution.py:465
  45.7 32.3 %collective-permute-done.5 = bf16[1024,384]{1,0:T(8,128)(2,1)S(1)} collective-permute-done((bf16[1024,384]{1,0:T(8,128)(2,1)S(1)}, bf16[1024,384]{1,0:T(8,128)(2,1)S(1)}, u32[]{:S(2)}, u32[]{:S(2)}) %collective-permute-start.5) | collective-permute-done | bytes 786464 | tf_op jit(solution)/shard_map/ppermute | solution.py:465
  88.2 19.4 %collective-permute-done.9 = bf16[128,2048]{1,0:T(8,128)(2,1)S(1)} collective-permute-done((bf16[128,2048]{1,0:T(8,128)(2,1)S(1)}, bf16[128,2048]{1,0:T(8,128)(2,1)S(1)}, u32[]{:S(2)}, u32[]{:S(2)}) %collective-permute-start.9) | collective-permute-done | bytes 524320 | tf_op jit(solution)/shard_map/ppermute | solution.py:465
  131.6 16.0 %shard_map.169 = (bf16[1024,768]{1,0:T(8,128)(2,1)S(1)}, bf16[1024,256]{1,0:T(8,128)(2,1)S(1)}) custom-call(bf16[1024,2048]{1,0:T(8,128)(2,1)} %slice_dynamic-update-slice_fusion.10.rows_ref.left_ref, bf16[2,2048,384]{2,1,0:T(8,128)(2,1)} %pad_maximum_fusion.3.weight_ref.refs_1_, f32[1024,128]{1,0:T(8,128)S(1)} %pad_maximum_fusion.30.cos_ref, ...), custom_call_target="tpu_custom_call" | custom-call | flops 6442450944 | bytes 7340032 | tf_op jit(solution)/shard_map/pallas_call | solution.py:632
  150.4 15.9 %shard_map.170 = (bf16[1024,768]{1,0:T(8,128)(2,1)S(1)}, bf16[1024,256]{1,0:T(8,128)(2,1)S(1)}) custom-call(bf16[1024,2048]{1,0:T(8,128)(2,1)} %collective-permute-done.14.rows_ref.left_other_ref, bf16[2,2048,384]{2,1,0:T(8,128)(2,1)} %pad_maximum_fusion.3.weight_ref.refs_1_, f32[1024,128]{1,0:T(8,128)S(1)} %pad_maximum_fusion.30.cos_ref, ...), custom_call_target="tpu_custom_call" | custom-call | flops 6442450944 | bytes 7340032 | tf_op jit(solution)/shard_map/pallas_call | solution.py:632
  203.7 32.0 %collective-permute-done.24 = bf16[512,512]{1,0:T(8,128)(2,1)S(1)} collective-permute-done((bf16[512,512]{1,0:T(8,128)(2,1)S(1)}, bf16[512,512]{1,0:T(8,128)(2,1)S(1)}, u32[]{:S(2)}, u32[]{:S(2)}) %collective-permute-start.24) | collective-permute-done | bytes 524320 | tf_op jit(solution)/shard_map/ppermute | solution.py:465
  245.3 13.1 %collective-permute-done.27 = bf16[128,2048]{1,0:T(8,128)(2,1)S(1)} collective-permute-done((bf16[128,2048]{1,0:T(8,128)(2,1)S(1)}, bf16[128,2048]{1,0:T(8,128)(2,1)S(1)}, u32[]{:S(2)}, u32[]{:S(2)}) %collective-permute-start.27) | collective-permute-done | bytes 524320 | tf_op jit(solution)/shard_map/ppermute | solution.py:465
  273.2 30.4 %collective-permute-done.31 = bf16[256,2048]{1,0:T(8,128)(2,1)S(1)} collective-permute-done((bf16[256,2048]{1,0:T(8,128)(2,1)S(1)}, bf16[256,2048]{1,0:T(8,128)(2,1)S(1)}, u32[]{:S(2)}, u32[]{:S(2)}) %collective-permute-start.31) | collective-permute-done | bytes 1048608 | tf_op jit(solution)/shard_map/ppermute | solution.py:465
  343.2 12.7 %shard_map.173 = (bf16[1024,512]{1,0:T(8,128)(2,1)S(1)}, bf16[1024,1024]{1,0:T(8,128)(2,1)S(1)}) custom-call(bf16[1024,2048]{1,0:T(8,128)(2,1)} %constant_dynamic-update-slice_fusion.7.rows_ref.left_ref, bf16[1024,2048]{1,0:T(8,128)(2,1)} %copy-done.29, bf16[2,2048,512]{2,1,0:T(8,128)(2,1)} %pad_maximum_fusion.wide_ref.refs_2_, ...), custom_call_target="tpu_custom_call" | custom-call | flops 6442450 | bytes 14680 | tf_op jit(solution)/shard_map/pallas_call | solution.py:731
  358.0 13.4 %shard_map.174 = (bf16[1024,512]{1,0:T(8,128)(2,1)S(1)}, bf16[1024,1024]{1,0:T(8,128)(2,1)S(1)}) custom-call(bf16[1024,2048]{1,0:T(8,128)(2,1)} %collective-permute-done.41.rows_ref.left_other_ref, bf16[1024,2048]{1,0:T(8,128)(2,1)} %copy-done.30, bf16[2,2048,512]{2,1,0:T(8,128)(2,1)} %pad_maximum_fusion.wide_ref.refs_2_, ...), custom_call_target="tpu_custom_call" | custom-call | flops 6442450 | bytes 14680 | tf_op jit(solution)/shard_map/pallas_call | solution.py:731
  378.9 14.4 %shard_map.176 = bf16[2,2048,512]{2,1,0:T(8,128)(2,1)} custom-call(bf16[1024,2048]{1,0:T(8,128)(2,1)} %constant_dynamic-update-slice_fusion.7.rows_ref.left_ref, bf16[1024,2048]{1,0:T(8,128)(2,1)} %collective-permute-done.41.rows_ref.left_other_ref, bf16[1024,1024]{1,0:T(8,128)(2,1)S(1)} %get-tuple-element.200.right_ref.refs_0_, ...), custom_call_target="tpu_custom_call" | custom-call | flops 8589934 | bytes 16777 | tf_op jit(solution)/shard_map/pallas_call | solution.py:841
  403.2 12.6 %shard_map.177 = (bf16[1024,512]{1,0:T(8,128)(2,1)S(1)}, bf16[1024,1024]{1,0:T(8,128)(2,1)S(1)}) custom-call(bf16[1024,2048]{1,0:T(8,128)(2,1)} %collective-permute-done.41.rows_ref.left_other_ref, bf16[1024,2048]{1,0:T(8,128)(2,1)} %copy-done.30, bf16[2,2048,512]{2,1,0:T(8,128)(2,1)} %pad_maximum_fusion.1.wide_ref.refs_3_, ...), custom_call_target="tpu_custom_call" | custom-call | flops 6442450 | bytes 14680 | tf_op jit(solution)/shard_map/pallas_call | solution.py:731
  421.5 12.8 %shard_map.178 = bf16[1024,2048]{1,0:T(8,128)(2,1)} custom-call(bf16[1024,1024]{1,0:T(8,128)(2,1)S(1)} %get-tuple-element.204.right_other_ref.refs_0_, bf16[1024,1024]{1,0:T(8,128)(2,1)S(1)} %get-tuple-element.205.refs_1_.right_other_ref, bf16[2,2048,512]{2,1,0:T(8,128)(2,1)} %pad_maximum_fusion.wide_ref.refs_2_, ...), custom_call_target="tpu_custom_call" | custom-call | flops 8589934 | bytes 20971 | tf_op jit(solution)/shard_map/pallas_call | solution.py:777
  441.0 12.6 %shard_map.175 = (bf16[1024,512]{1,0:T(8,128)(2,1)S(1)}, bf16[1024,1024]{1,0:T(8,128)(2,1)S(1)}) custom-call(bf16[1024,2048]{1,0:T(8,128)(2,1)} %constant_dynamic-update-slice_fusion.7.rows_ref.left_ref, bf16[1024,2048]{1,0:T(8,128)(2,1)} %copy-done.29, bf16[2,2048,512]{2,1,0:T(8,128)(2,1)} %pad_maximum_fusion.1.wide_ref.refs_3_, ...), custom_call_target="tpu_custom_call" | custom-call | flops 6442450 | bytes 14680 | tf_op jit(solution)/shard_map/pallas_call | solution.py:731
  453.7 14.8 %shard_map.179 = bf16[2,2048,512]{2,1,0:T(8,128)(2,1)} custom-call(bf16[1024,2048]{1,0:T(8,128)(2,1)} %constant_dynamic-update-slice_fusion.7.rows_ref.left_ref, bf16[1024,2048]{1,0:T(8,128)(2,1)} %collective-permute-done.41.rows_ref.left_other_ref, bf16[1024,1024]{1,0:T(8,128)(2,1)S(1)} %get-tuple-element.201.right_ref.refs_1_, bf16[1024,1024]{1,0:T(8,128)(2,1)S(1)} %copy-done.7), custom_call_target="tpu_custom_call" | custom-call | flops 8589934 | bytes 16777 | tf_op jit(solution)/shard_map/pallas_call | solution.py:841
  468.5 14.1 %shard_map.180 = bf16[1024,2048]{1,0:T(8,128)(2,1)} custom-call(bf16[1024,1024]{1,0:T(8,128)(2,1)S(1)} %get-tuple-element.200.right_ref.refs_0_, bf16[1024,1024]{1,0:T(8,128)(2,1)S(1)} %get-tuple-element.201.right_ref.refs_1_, bf16[2,2048,512]{2,1,0:T(8,128)(2,1)} %pad_maximum_fusion.wide_ref.refs_2_, ...), custom_call_target="tpu_custom_call" | custom-call | flops 8589934 | bytes 20971 | tf_op jit(solution)/shard_map/pallas_call | solution.py:777
  524.8 12.1 %collective-permute-done.52 = bf16[128,2048]{1,0:T(8,128)(2,1)S(1)} collective-permute-done((bf16[128,2048]{1,0:T(8,128)(2,1)S(1)}, bf16[128,2048]{1,0:T(8,128)(2,1)S(1)}, u32[]{:S(2)}, u32[]{:S(2)}) %collective-permute-start.52) | collective-permute-done | bytes 524320 | tf_op jit(solution)/shard_map/ppermute | solution.py:465
  551.8 19.7 %collective-permute-done.57 = bf16[512,1024]{1,0:T(8,128)(2,1)S(1)} collective-permute-done((bf16[512,1024]{1,0:T(8,128)(2,1)S(1)}, bf16[512,1024]{1,0:T(8,128)(2,1)S(1)}, u32[]{:S(2)}, u32[]{:S(2)}) %collective-permute-start.57) | collective-permute-done | bytes 1048608 | tf_op jit(solution)/shard_map/ppermute | solution.py:465
  616.0 15.3 %shard_map.186.right_ref.refs_0_ = bf16[1024,768]{1,0:T(8,128)(2,1)S(1)} custom-call(bf16[1024,2048]{1,0:T(8,128)(2,1)} %constant_dynamic-update-slice_fusion.15.right_ref.grad_ref, bf16[2,256,1024]{2,1,0:T(8,128)(2,1)S(1)} %pad_maximum_fusion.18.refs_1_.weight_ref, bf16[1024,768]{1,0:T(8,128)(2,1)S(1)} %copy-done.25, f32[1024,128]{1,0:T(8,128)S(1)} %copy-done.13, ...), custom_call_target="tpu_custom_call" | custom-call | flops 6442450 | bytes 7340 | tf_op jit(solution)/shard_map/pallas_call | solution.py:691
  664.7 15.7 %shard_map.187.refs_0_.right_other_ref = bf16[1024,768]{1,0:T(8,128)(2,1)S(1)} custom-call(bf16[1024,2048]{1,0:T(8,128)(2,1)} %copy-done.44, bf16[2,256,1024]{2,1,0:T(8,128)(2,1)S(1)} %copy-done.3, bf16[1024,768]{1,0:T(8,128)(2,1)S(1)} %copy-done.23, f32[1024,128]{1,0:T(8,128)S(1)} %copy-done.13, f32[1024,128]{1,0:T(8,128)S(1)} %copy-done.9, ...), custom_call_target="tpu_custom_call" | custom-call | flops 6442450 | bytes 7340 | tf_op jit(solution)/shard_map/pallas_call | solution.py:691
  690.9 14.1 %shard_map.189 = bf16[2,2048,384]{2,1,0:T(8,128)(2,1)} custom-call(bf16[1024,2048]{1,0:T(8,128)(2,1)} %slice_dynamic-update-slice_fusion.10.rows_ref.left_ref, bf16[1024,2048]{1,0:T(8,128)(2,1)} %collective-permute-done.14.rows_ref.left_other_ref, bf16[1024,768]{1,0:T(8,128)(2,1)S(1)} %shard_map.186.right_ref.refs_0_, ...), custom_call_target="tpu_custom_call" | custom-call | flops 6442450 | bytes 14680 | tf_op jit(solution)/shard_map/pallas_call | solution.py:841
  734.7 27.1 %collective-permute-done.88 = bf16[2,128,256]{2,1,0:T(8,128)(2,1)S(1)} collective-permute-done((bf16[2,128,256]{2,1,0:T(8,128)(2,1)S(1)}, bf16[2,128,256]{2,1,0:T(8,128)(2,1)S(1)}, u32[]{:S(2)}, u32[]{:S(2)}) %collective-permute-start.88) | collective-permute-done | bytes 131104 | tf_op jit(solution)/shard_map/ppermute | solution.py:465
  769.3 17.3 %collective-permute-done.78 = bf16[128,2048]{1,0:T(8,128)(2,1)S(1)} collective-permute-done((bf16[128,2048]{1,0:T(8,128)(2,1)S(1)}, bf16[128,2048]{1,0:T(8,128)(2,1)S(1)}, u32[]{:S(2)}, u32[]{:S(2)}) %collective-permute-start.78) | collective-permute-done | bytes 524320 | tf_op jit(solution)/shard_map/ppermute | solution.py:465
  808.6 20.9 %collective-permute-done.83 = bf16[2,512,256]{2,1,0:T(8,128)(2,1)S(1)} collective-permute-done((bf16[2,512,256]{2,1,0:T(8,128)(2,1)S(1)}, bf16[2,512,256]{2,1,0:T(8,128)(2,1)S(1)}, u32[]{:S(2)}, u32[]{:S(2)}) %collective-permute-start.83) | collective-permute-done | bytes 524320 | tf_op jit(solution)/shard_map/ppermute | solution.py:465
  (684 shorter events, 411.6 us)
Async XLA Ops:
  36.9 42.4 %collective-permute-start.4 = (bf16[256,2048]{1,0:T(8,128)(2,1)S(1)}, bf16[256,2048]{1,0:T(8,128)(2,1)S(1)}, u32[]{:S(2)}, u32[]{:S(2)}) collective-permute-start(bf16[256,2048]{1,0:T(8,128)(2,1)S(1)} %fusion.5), channel_id=1, source_target_pairs={{0,2},{2,0},{1,3},{3,1},{4,6},{6,4},{5,7},{7,5},{8,10},{10,8},{9,1... | collective-permute-start | bytes 3145736 | tf_op jit(solution)/shard_map/ppermute | solution.py:465
  38.1 41.2 %collective-permute-start.6 = (bf16[256,2048]{1,0:T(8,128)(2,1)S(1)}, bf16[256,2048]{1,0:T(8,128)(2,1)S(1)}, u32[]{:S(2)}, u32[]{:S(2)}) collective-permute-start(bf16[256,2048]{1,0:T(8,128)(2,1)S(1)} %fusion.5), channel_id=1, source_target_pairs={{0,1},{1,0},{2,3},{3,2},{4,5},{5,4},{6,7},{7,6},{8,9},{9,8},{10,11... | collective-permute-start | bytes 3145736 | tf_op jit(solution)/shard_map/ppermute | solution.py:465
  39.7 38.3 %collective-permute-start.5 = (bf16[1024,384]{1,0:T(8,128)(2,1)S(1)}, bf16[1024,384]{1,0:T(8,128)(2,1)S(1)}, u32[]{:S(2)}, u32[]{:S(2)}) collective-permute-start(bf16[1024,384]{1,0:T(8,128)(2,1)S(1)} %fusion.23), channel_id=1, source_target_pairs={{0,4},{4,0},{1,5},{5,1},{2,6},{6,2},{3,7},{7,3},{8,12},{12,8},{9,1... | collective-permute-start | bytes 2359304 | tf_op jit(solution)/shard_map/ppermute | solution.py:465
  42.7 35.2 %collective-permute-start.7 = (bf16[1024,384]{1,0:T(8,128)(2,1)S(1)}, bf16[1024,384]{1,0:T(8,128)(2,1)S(1)}, u32[]{:S(2)}, u32[]{:S(2)}) collective-permute-start(bf16[1024,384]{1,0:T(8,128)(2,1)S(1)} %fusion.23), channel_id=1, source_target_pairs={{0,16},{16,0},{1,17},{17,1},{2,18},{18,2},{3,19},{19,3},{4,20},{20... | collective-permute-start | bytes 2359304 | tf_op jit(solution)/shard_map/ppermute | solution.py:465
  79.3 35.6 %collective-permute-start.11 = (bf16[1024,384]{1,0:T(8,128)(2,1)S(1)}, bf16[1024,384]{1,0:T(8,128)(2,1)S(1)}, u32[]{:S(2)}, u32[]{:S(2)}) collective-permute-start(bf16[1024,384]{1,0:T(8,128)(2,1)S(1)} %collective-permute-done.5), channel_id=1, source_target_pairs={{0,16},{16,0},{1,17},{17,1},{2,18},{18,2},{3,19},{19,3},{4,20},{20... | collective-permute-start | bytes 2359304 | tf_op jit(solution)/shard_map/ppermute | solution.py:465
  128.9 39.0 %collective-permute-start.15 = (bf16[256,2048]{1,0:T(8,128)(2,1)S(1)}, bf16[256,2048]{1,0:T(8,128)(2,1)}, u32[]{:S(2)}, u32[]{:S(2)}) collective-permute-start(bf16[256,2048]{1,0:T(8,128)(2,1)S(1)} %copy-done.66), channel_id=1, source_target_pairs={{0,2},{2,0},{1,3},{3,1},{4,6},{6,4},{5,7},{7,5},{8,10},{10,8},{9,1... | collective-permute-start | bytes 3145736 | tf_op jit(solution)/shard_map/ppermute | solution.py:465
  130.5 37.3 %collective-permute-start.16 = (bf16[256,2048]{1,0:T(8,128)(2,1)S(1)}, bf16[256,2048]{1,0:T(8,128)(2,1)S(1)}, u32[]{:S(2)}, u32[]{:S(2)}) collective-permute-start(bf16[256,2048]{1,0:T(8,128)(2,1)S(1)} %copy-done.66), channel_id=1, source_target_pairs={{0,1},{1,0},{2,3},{3,2},{4,5},{5,4},{6,7},{7,6},{8,9},{9,8},{10,11... | collective-permute-start | bytes 3145736 | tf_op jit(solution)/shard_map/ppermute | solution.py:465
  131.0 36.8 %collective-permute-start.12 = (bf16[128,1024]{1,0:T(8,128)(2,1)S(1)}, bf16[128,1024]{1,0:T(8,128)(2,1)}, u32[]{:S(2)}, u32[]{:S(2)}) collective-permute-start(bf16[128,1024]{1,0:T(8,128)(2,1)S(1)} %pad_maximum_fusion.39), channel_id=1, source_target_pairs={{0,16},{16,0},{1,17},{17,1},{2,18},{18,2},{3,19},{19,3},{4,20},{20... | collective-permute-start | bytes 786440 | tf_op jit(solution)/shard_map/ppermute | solution.py:465
  200.8 38.1 %collective-permute-start.26 = (bf16[1024,2048]{1,0:T(8,128)(2,1)S(1)}, bf16[1024,2048]{1,0:T(8,128)(2,1)S(1)}, u32[]{:S(2)}, u32[]{:S(2)}) collective-permute-start(bf16[1024,2048]{1,0:T(8,128)(2,1)S(1)} %constant_dynamic-update-slice_fusion.1.grad_ref.right_ref), channel_id=1, source_target_pairs={{0,8},{8,0},{1,9},{9,1},{2,10},{10,2},{3,11},{11,3},{4,12},{12,4},... | collective-permute-start | bytes 12582920 | tf_op jit(solution)/shard_map/ppermute | solution.py:465
  200.9 34.9 %collective-permute-start.22 = (bf16[256,2048]{1,0:T(8,128)(2,1)S(1)}, bf16[256,2048]{1,0:T(8,128)(2,1)S(1)}, u32[]{:S(2)}, u32[]{:S(2)}) collective-permute-start(bf16[256,2048]{1,0:T(8,128)(2,1)S(1)} %get-tuple-element.173), channel_id=1, source_target_pairs={{0,1},{1,0},{2,3},{3,2},{4,5},{5,4},{6,7},{7,6},{8,9},{9,8},{10,11... | collective-permute-start | bytes 3145736 | tf_op jit(solution)/shard_map/ppermute | solution.py:465
  201.4 36.5 %collective-permute-start.23 = (bf16[256,2048]{1,0:T(8,128)(2,1)S(1)}, bf16[256,2048]{1,0:T(8,128)(2,1)S(1)}, u32[]{:S(2)}, u32[]{:S(2)}) collective-permute-start(bf16[256,2048]{1,0:T(8,128)(2,1)S(1)} %get-tuple-element.174), channel_id=1, source_target_pairs={{0,2},{2,0},{1,3},{3,1},{4,6},{6,4},{5,7},{7,5},{8,10},{10,8},{9,1... | collective-permute-start | bytes 3145736 | tf_op jit(solution)/shard_map/ppermute | solution.py:465
  202.1 36.7 %collective-permute-start.25 = (bf16[1024,512]{1,0:T(8,128)(2,1)S(1)}, bf16[1024,512]{1,0:T(8,128)(2,1)S(1)}, u32[]{:S(2)}, u32[]{:S(2)}) collective-permute-start(bf16[1024,512]{1,0:T(8,128)(2,1)S(1)} %copy-done.100), channel_id=1, source_target_pairs={{0,16},{16,0},{1,17},{17,1},{2,18},{18,2},{3,19},{19,3},{4,20},{20... | collective-permute-start | bytes 3145736 | tf_op jit(solution)/shard_map/ppermute | solution.py:465
  269.2 35.4 %collective-permute-start.34 = (bf16[512,1024]{1,0:T(8,128)(2,1)S(1)}, bf16[512,1024]{1,0:T(8,128)(2,1)S(1)}, u32[]{:S(2)}, u32[]{:S(2)}) collective-permute-start(bf16[512,1024]{1,0:T(8,128)(2,1)S(1)} %fusion.20), channel_id=1, source_target_pairs={{0,16},{16,0},{1,17},{17,1},{2,18},{18,2},{3,19},{19,3},{4,20},{20... | collective-permute-start | bytes 3145736 | tf_op jit(solution)/shard_map/ppermute | solution.py:465
  269.8 35.9 %collective-permute-start.32 = (bf16[256,2048]{1,0:T(8,128)(2,1)S(1)}, bf16[256,2048]{1,0:T(8,128)(2,1)S(1)}, u32[]{:S(2)}, u32[]{:S(2)}) collective-permute-start(bf16[256,2048]{1,0:T(8,128)(2,1)S(1)} %multiply_convert_fusion), channel_id=1, source_target_pairs={{0,1},{1,0},{2,3},{3,2},{4,5},{5,4},{6,7},{7,6},{8,9},{9,8},{10,11... | collective-permute-start | bytes 3145736 | tf_op jit(solution)/shard_map/ppermute | solution.py:465
  341.7 35.8 %collective-permute-start.40 = (bf16[1024,512]{1,0:T(8,128)(2,1)S(1)}, bf16[1024,512]{1,0:T(8,128)(2,1)}, u32[]{:S(2)}, u32[]{:S(2)}) collective-permute-start(bf16[1024,512]{1,0:T(8,128)(2,1)S(1)} %copy-done.50), channel_id=1, source_target_pairs={{0,16},{16,0},{1,17},{17,1},{2,18},{18,2},{3,19},{19,3},{4,20},{20... | collective-permute-start | bytes 3145736 | tf_op jit(solution)/shard_map/ppermute | solution.py:465
  545.9 40.1 %collective-permute-start.56 = (bf16[1024,2048]{1,0:T(8,128)(2,1)S(1)}, bf16[1024,2048]{1,0:T(8,128)(2,1)S(1)}, u32[]{:S(2)}, u32[]{:S(2)}) collective-permute-start(bf16[1024,2048]{1,0:T(8,128)(2,1)S(1)} %copy-done.68), channel_id=1, source_target_pairs={{0,8},{8,0},{1,9},{9,1},{2,10},{10,2},{3,11},{11,3},{4,12},{12,4},... | collective-permute-start | bytes 12582920 | tf_op jit(solution)/shard_map/ppermute | solution.py:465
  546.4 36.5 %collective-permute-start.58 = (bf16[256,2048]{1,0:T(8,128)(2,1)S(1)}, bf16[256,2048]{1,0:T(8,128)(2,1)S(1)}, u32[]{:S(2)}, u32[]{:S(2)}) collective-permute-start(bf16[256,2048]{1,0:T(8,128)(2,1)S(1)} %fusion.17), channel_id=1, source_target_pairs={{0,2},{2,0},{1,3},{3,1},{4,6},{6,4},{5,7},{7,5},{8,10},{10,8},{9,1... | collective-permute-start | bytes 3145736 | tf_op jit(solution)/shard_map/ppermute | solution.py:465
  546.5 38.4 %collective-permute-start.59 = (bf16[256,2048]{1,0:T(8,128)(2,1)S(1)}, bf16[256,2048]{1,0:T(8,128)(2,1)S(1)}, u32[]{:S(2)}, u32[]{:S(2)}) collective-permute-start(bf16[256,2048]{1,0:T(8,128)(2,1)S(1)} %fusion.17), channel_id=1, source_target_pairs={{0,1},{1,0},{2,3},{3,2},{4,5},{5,4},{6,7},{7,6},{8,9},{9,8},{10,11... | collective-permute-start | bytes 3145736 | tf_op jit(solution)/shard_map/ppermute | solution.py:465
  547.8 38.1 %collective-permute-start.60 = (bf16[512,512]{1,0:T(8,128)(2,1)S(1)}, bf16[512,512]{1,0:T(8,128)(2,1)S(1)}, u32[]{:S(2)}, u32[]{:S(2)}) collective-permute-start(bf16[512,512]{1,0:T(8,128)(2,1)S(1)} %get-tuple-element.224), channel_id=1, source_target_pairs={{0,4},{4,0},{1,5},{5,1},{2,6},{6,2},{3,7},{7,3},{8,12},{12,8},{9,1... | collective-permute-start | bytes 1572872 | tf_op jit(solution)/shard_map/ppermute | solution.py:465
  614.5 36.9 %collective-permute-start.67 = (bf16[1024,2048]{1,0:T(8,128)(2,1)}, bf16[1024,2048]{1,0:T(8,128)(2,1)S(1)}, u32[]{:S(2)}, u32[]{:S(2)}) collective-permute-start(bf16[1024,2048]{1,0:T(8,128)(2,1)} %constant_dynamic-update-slice_fusion.15.right_ref.grad_ref), channel_id=1, source_target_pairs={{0,8},{8,0},{1,9},{9,1},{2,10},{10,2},{3,11},{11,3},{4,12},{12,4},... | collective-permute-start | bytes 12582920 | tf_op jit(solution)/shard_map/ppermute | solution.py:465
  711.0 51.0 %collective-permute-start.73 = (bf16[128,2048]{1,0:T(8,128)(2,1)}, bf16[128,2048]{1,0:T(8,128)(2,1)S(1)}, u32[]{:S(2)}, u32[]{:S(2)}) collective-permute-start(bf16[128,2048]{1,0:T(8,128)(2,1)} %slice.506), channel_id=1, source_target_pairs={{0,4},{4,0},{1,5},{5,1},{2,6},{6,2},{3,7},{7,3},{8,12},{12,8},{9,1... | collective-permute-start | bytes 1572872 | tf_op jit(solution)/shard_map/ppermute | solution.py:465
  764.4 37.8 %collective-permute-start.91 = (bf16[1024,384]{1,0:T(8,128)(2,1)S(1)}, bf16[1024,384]{1,0:T(8,128)(2,1)S(1)}, u32[]{:S(2)}, u32[]{:S(2)}) collective-permute-start(bf16[1024,384]{1,0:T(8,128)(2,1)S(1)} %fusion.16), channel_id=1, source_target_pairs={{0,4},{4,0},{1,5},{5,1},{2,6},{6,2},{3,7},{7,3},{8,12},{12,8},{9,1... | collective-permute-start | bytes 2359304 | tf_op jit(solution)/shard_map/ppermute | solution.py:465
  766.9 35.3 %collective-permute-start.90 = (bf16[1024,384]{1,0:T(8,128)(2,1)S(1)}, bf16[1024,384]{1,0:T(8,128)(2,1)S(1)}, u32[]{:S(2)}, u32[]{:S(2)}) collective-permute-start(bf16[1024,384]{1,0:T(8,128)(2,1)S(1)} %copy-done.105), channel_id=1, source_target_pairs={{0,16},{16,0},{1,17},{17,1},{2,18},{18,2},{3,19},{19,3},{4,20},{20... | collective-permute-start | bytes 2359304 | tf_op jit(solution)/shard_map/ppermute | solution.py:465
  794.0 36.0 %collective-permute-start.81 = (bf16[512,1024]{1,0:T(8,128)(2,1)S(1)}, bf16[512,1024]{1,0:T(8,128)(2,1)S(1)}, u32[]{:S(2)}, u32[]{:S(2)}) collective-permute-start(bf16[512,1024]{1,0:T(8,128)(2,1)S(1)} %dynamic-slice_convert_fusion), channel_id=1, source_target_pairs={{0,8},{8,0},{1,9},{9,1},{2,10},{10,2},{3,11},{11,3},{4,12},{12,4},... | collective-permute-start | bytes 3145736 | tf_op jit(solution)/shard_map/ppermute | solution.py:465
  (218 other events, 3663.9 us)

commit v7 on v6

--- a/solution.py
+++ b/solution.py
@@ -835,7 +835,7 @@
 def outer_rows(lefts, rights):
     count, depth = lefts[0].shape
     span = rights[0].shape[1] // 2
-    tile = min(depth, 512)
+    tile = min(depth, 1024)
     left_spec = pl.BlockSpec((count, tile), lambda w, i: (0, i))
     right_spec = pl.BlockSpec((count, span), lambda w, i: (0, w))
     return kernel_call(

time: 848 us -> 843 us (level)
  transfers between devices with their start and end apart: 93 -> 93, of which waited for: 35 -> 35; matrix products, arithmetic and copies ran while one was open for 13% -> 14% of each run, Pallas kernels for 25% -> 25%
where the time goes in v7:
time: 843 us; the launch traced here: 834 us
  waiting for transfers between devices  339 us (40%)
  Pallas kernels  239 us (28%)
  starting transfers between devices  95.6 us (11%)
  local copies, waits for them, and re-layouts  92.1 us (11%)
  other arithmetic  65.1 us (8%)
    ppermute x93, waiting for transfers between devices, swap(): return lax.ppermute(value, axis, SWAP)  339 us
    ppermute x93, starting transfers between devices, swap(): return lax.ppermute(value, axis, SWAP)  95.6 us
    pallas_call x6, Pallas kernels, outer_rows(): kernel_call(outer_kernel, (2, depth // tile), [left_spec, left_spec, righ...  58.4 us
    pallas_call x4, Pallas kernels, hidden_pass(): kernel_call(hidden_kernel, (2,), [whole(rows.shape), whole(grads.shape),...  51.3 us
    unnamed x329, local copies, waits for them, and re-layouts  49.1 us
    pallas_call x4, Pallas kernels, back_rows(): kernel_call(functools.partial(back_kernel, (len(lefts), len(added))), (wi...  44 us
    pallas_call x2, Pallas kernels, attend(): kernel_call(attend_kernel, (2,), [whole(rows.shape), pl.BlockSpec((1, wid...  31.9 us
    pallas_call x2, Pallas kernels, attend_back(): kernel_call(attend_back_kernel, (2,), [whole(grads.shape), pl.BlockSpec((...  31.5 us
  transfers between devices with their start and end apart: 93, of which 35 were waited for; matrix products, arithmetic and copies ran while one was open for 14% of the time, Pallas kernels for 25%

profile of v7, /device:TPU:0, one launch (start us, length us, event | category | flops | bytes accessed | tf_op | source)
XLA Modules:
  0.0 834.4 jit_solution(7812955916455184575)
XLA Ops:
  16.4 13.9 %collective-permute-done = bf16[128,2048]{1,0:T(8,128)(2,1)S(1)} collective-permute-done((bf16[128,2048]{1,0:T(8,128)(2,1)}, bf16[128,2048]{1,0:T(8,128)(2,1)S(1)}, u32[]{:S(2)}, u32[]{:S(2)}) %collective-permute-start) | collective-permute-done | bytes 524320 | tf_op jit(solution)/shard_map/ppermute | solution.py:465
  45.7 32.3 %collective-permute-done.5 = bf16[1024,384]{1,0:T(8,128)(2,1)S(1)} collective-permute-done((bf16[1024,384]{1,0:T(8,128)(2,1)S(1)}, bf16[1024,384]{1,0:T(8,128)(2,1)S(1)}, u32[]{:S(2)}, u32[]{:S(2)}) %collective-permute-start.5) | collective-permute-done | bytes 786464 | tf_op jit(solution)/shard_map/ppermute | solution.py:465
  88.2 19.4 %collective-permute-done.9 = bf16[128,2048]{1,0:T(8,128)(2,1)S(1)} collective-permute-done((bf16[128,2048]{1,0:T(8,128)(2,1)S(1)}, bf16[128,2048]{1,0:T(8,128)(2,1)S(1)}, u32[]{:S(2)}, u32[]{:S(2)}) %collective-permute-start.9) | collective-permute-done | bytes 524320 | tf_op jit(solution)/shard_map/ppermute | solution.py:465
  131.6 16.1 %shard_map.169 = (bf16[1024,768]{1,0:T(8,128)(2,1)S(1)}, bf16[1024,256]{1,0:T(8,128)(2,1)S(1)}) custom-call(bf16[1024,2048]{1,0:T(8,128)(2,1)} %slice_dynamic-update-slice_fusion.10.rows_ref.left_ref, bf16[2,2048,384]{2,1,0:T(8,128)(2,1)} %pad_maximum_fusion.3.weight_ref.refs_1_, f32[1024,128]{1,0:T(8,128)S(1)} %pad_maximum_fusion.30.cos_ref, ...), custom_call_target="tpu_custom_call" | custom-call | flops 6442450944 | bytes 7340032 | tf_op jit(solution)/shard_map/pallas_call | solution.py:632
  150.4 15.9 %shard_map.170 = (bf16[1024,768]{1,0:T(8,128)(2,1)S(1)}, bf16[1024,256]{1,0:T(8,128)(2,1)S(1)}) custom-call(bf16[1024,2048]{1,0:T(8,128)(2,1)} %collective-permute-done.14.rows_ref.left_other_ref, bf16[2,2048,384]{2,1,0:T(8,128)(2,1)} %pad_maximum_fusion.3.weight_ref.refs_1_, f32[1024,128]{1,0:T(8,128)S(1)} %pad_maximum_fusion.30.cos_ref, ...), custom_call_target="tpu_custom_call" | custom-call | flops 6442450944 | bytes 7340032 | tf_op jit(solution)/shard_map/pallas_call | solution.py:632
  203.7 32.0 %collective-permute-done.24 = bf16[512,512]{1,0:T(8,128)(2,1)S(1)} collective-permute-done((bf16[512,512]{1,0:T(8,128)(2,1)S(1)}, bf16[512,512]{1,0:T(8,128)(2,1)S(1)}, u32[]{:S(2)}, u32[]{:S(2)}) %collective-permute-start.24) | collective-permute-done | bytes 524320 | tf_op jit(solution)/shard_map/ppermute | solution.py:465
  245.3 13.0 %collective-permute-done.27 = bf16[128,2048]{1,0:T(8,128)(2,1)S(1)} collective-permute-done((bf16[128,2048]{1,0:T(8,128)(2,1)S(1)}, bf16[128,2048]{1,0:T(8,128)(2,1)S(1)}, u32[]{:S(2)}, u32[]{:S(2)}) %collective-permute-start.27) | collective-permute-done | bytes 524320 | tf_op jit(solution)/shard_map/ppermute | solution.py:465
  273.2 30.4 %collective-permute-done.31 = bf16[256,2048]{1,0:T(8,128)(2,1)S(1)} collective-permute-done((bf16[256,2048]{1,0:T(8,128)(2,1)S(1)}, bf16[256,2048]{1,0:T(8,128)(2,1)S(1)}, u32[]{:S(2)}, u32[]{:S(2)}) %collective-permute-start.31) | collective-permute-done | bytes 1048608 | tf_op jit(solution)/shard_map/ppermute | solution.py:465
  343.4 12.7 %shard_map.173 = (bf16[1024,512]{1,0:T(8,128)(2,1)S(1)}, bf16[1024,1024]{1,0:T(8,128)(2,1)S(1)}) custom-call(bf16[1024,2048]{1,0:T(8,128)(2,1)} %constant_dynamic-update-slice_fusion.7.rows_ref.left_ref, bf16[1024,2048]{1,0:T(8,128)(2,1)} %copy-done.29, bf16[2,2048,512]{2,1,0:T(8,128)(2,1)} %pad_maximum_fusion.wide_ref.refs_2_, ...), custom_call_target="tpu_custom_call" | custom-call | flops 6442450 | bytes 14680 | tf_op jit(solution)/shard_map/pallas_call | solution.py:731
  358.2 13.4 %shard_map.174 = (bf16[1024,512]{1,0:T(8,128)(2,1)S(1)}, bf16[1024,1024]{1,0:T(8,128)(2,1)S(1)}) custom-call(bf16[1024,2048]{1,0:T(8,128)(2,1)} %collective-permute-done.41.rows_ref.left_other_ref, bf16[1024,2048]{1,0:T(8,128)(2,1)} %copy-done.30, bf16[2,2048,512]{2,1,0:T(8,128)(2,1)} %pad_maximum_fusion.wide_ref.refs_2_, ...), custom_call_target="tpu_custom_call" | custom-call | flops 6442450 | bytes 14680 | tf_op jit(solution)/shard_map/pallas_call | solution.py:731
  379.1 13.2 %shard_map.176 = bf16[2,2048,512]{2,1,0:T(8,128)(2,1)} custom-call(bf16[1024,2048]{1,0:T(8,128)(2,1)} %constant_dynamic-update-slice_fusion.7.rows_ref.left_ref, bf16[1024,2048]{1,0:T(8,128)(2,1)} %collective-permute-done.41.rows_ref.left_other_ref, bf16[1024,1024]{1,0:T(8,128)(2,1)S(1)} %get-tuple-element.200.right_ref.refs_0_, ...), custom_call_target="tpu_custom_call" | custom-call | flops 8589934 | bytes 16777 | tf_op jit(solution)/shard_map/pallas_call | solution.py:841
  402.3 12.6 %shard_map.177 = (bf16[1024,512]{1,0:T(8,128)(2,1)S(1)}, bf16[1024,1024]{1,0:T(8,128)(2,1)S(1)}) custom-call(bf16[1024,2048]{1,0:T(8,128)(2,1)} %collective-permute-done.41.rows_ref.left_other_ref, bf16[1024,2048]{1,0:T(8,128)(2,1)} %copy-done.30, bf16[2,2048,512]{2,1,0:T(8,128)(2,1)} %pad_maximum_fusion.1.wide_ref.refs_3_, ...), custom_call_target="tpu_custom_call" | custom-call | flops 6442450 | bytes 14680 | tf_op jit(solution)/shard_map/pallas_call | solution.py:731
  420.5 12.8 %shard_map.178 = bf16[1024,2048]{1,0:T(8,128)(2,1)} custom-call(bf16[1024,1024]{1,0:T(8,128)(2,1)S(1)} %get-tuple-element.204.right_other_ref.refs_0_, bf16[1024,1024]{1,0:T(8,128)(2,1)S(1)} %get-tuple-element.205.refs_1_.right_other_ref, bf16[2,2048,512]{2,1,0:T(8,128)(2,1)} %pad_maximum_fusion.wide_ref.refs_2_, ...), custom_call_target="tpu_custom_call" | custom-call | flops 8589934 | bytes 20971 | tf_op jit(solution)/shard_map/pallas_call | solution.py:777
  440.1 12.6 %shard_map.175 = (bf16[1024,512]{1,0:T(8,128)(2,1)S(1)}, bf16[1024,1024]{1,0:T(8,128)(2,1)S(1)}) custom-call(bf16[1024,2048]{1,0:T(8,128)(2,1)} %constant_dynamic-update-slice_fusion.7.rows_ref.left_ref, bf16[1024,2048]{1,0:T(8,128)(2,1)} %copy-done.29, bf16[2,2048,512]{2,1,0:T(8,128)(2,1)} %pad_maximum_fusion.1.wide_ref.refs_3_, ...), custom_call_target="tpu_custom_call" | custom-call | flops 6442450 | bytes 14680 | tf_op jit(solution)/shard_map/pallas_call | solution.py:731
  452.7 13.3 %shard_map.179 = bf16[2,2048,512]{2,1,0:T(8,128)(2,1)} custom-call(bf16[1024,2048]{1,0:T(8,128)(2,1)} %constant_dynamic-update-slice_fusion.7.rows_ref.left_ref, bf16[1024,2048]{1,0:T(8,128)(2,1)} %collective-permute-done.41.rows_ref.left_other_ref, bf16[1024,1024]{1,0:T(8,128)(2,1)S(1)} %get-tuple-element.201.right_ref.refs_1_, bf16[1024,1024]{1,0:T(8,128)(2,1)S(1)} %copy-done.7), custom_call_target="tpu_custom_call" | custom-call | flops 8589934 | bytes 16777 | tf_op jit(solution)/shard_map/pallas_call | solution.py:841
  466.1 14.1 %shard_map.180 = bf16[1024,2048]{1,0:T(8,128)(2,1)} custom-call(bf16[1024,1024]{1,0:T(8,128)(2,1)S(1)} %get-tuple-element.200.right_ref.refs_0_, bf16[1024,1024]{1,0:T(8,128)(2,1)S(1)} %get-tuple-element.201.right_ref.refs_1_, bf16[2,2048,512]{2,1,0:T(8,128)(2,1)} %pad_maximum_fusion.wide_ref.refs_2_, ...), custom_call_target="tpu_custom_call" | custom-call | flops 8589934 | bytes 20971 | tf_op jit(solution)/shard_map/pallas_call | solution.py:777
  522.4 12.0 %collective-permute-done.52 = bf16[128,2048]{1,0:T(8,128)(2,1)S(1)} collective-permute-done((bf16[128,2048]{1,0:T(8,128)(2,1)S(1)}, bf16[128,2048]{1,0:T(8,128)(2,1)S(1)}, u32[]{:S(2)}, u32[]{:S(2)}) %collective-permute-start.52) | collective-permute-done | bytes 524320 | tf_op jit(solution)/shard_map/ppermute | solution.py:465
  549.4 19.7 %collective-permute-done.57 = bf16[512,1024]{1,0:T(8,128)(2,1)S(1)} collective-permute-done((bf16[512,1024]{1,0:T(8,128)(2,1)S(1)}, bf16[512,1024]{1,0:T(8,128)(2,1)S(1)}, u32[]{:S(2)}, u32[]{:S(2)}) %collective-permute-start.57) | collective-permute-done | bytes 1048608 | tf_op jit(solution)/shard_map/ppermute | solution.py:465
  613.6 15.5 %shard_map.186.right_ref.refs_0_ = bf16[1024,768]{1,0:T(8,128)(2,1)S(1)} custom-call(bf16[1024,2048]{1,0:T(8,128)(2,1)} %constant_dynamic-update-slice_fusion.15.right_ref.grad_ref, bf16[2,256,1024]{2,1,0:T(8,128)(2,1)S(1)} %pad_maximum_fusion.18.refs_1_.weight_ref, bf16[1024,768]{1,0:T(8,128)(2,1)S(1)} %copy-done.25, f32[1024,128]{1,0:T(8,128)S(1)} %copy-done.13, ...), custom_call_target="tpu_custom_call" | custom-call | flops 6442450 | bytes 7340 | tf_op jit(solution)/shard_map/pallas_call | solution.py:691
  662.2 16.0 %shard_map.187.refs_0_.right_other_ref = bf16[1024,768]{1,0:T(8,128)(2,1)S(1)} custom-call(bf16[1024,2048]{1,0:T(8,128)(2,1)} %copy-done.44, bf16[2,256,1024]{2,1,0:T(8,128)(2,1)S(1)} %copy-done.3, bf16[1024,768]{1,0:T(8,128)(2,1)S(1)} %copy-done.23, f32[1024,128]{1,0:T(8,128)S(1)} %copy-done.13, f32[1024,128]{1,0:T(8,128)S(1)} %copy-done.9, ...), custom_call_target="tpu_custom_call" | custom-call | flops 6442450 | bytes 7340 | tf_op jit(solution)/shard_map/pallas_call | solution.py:691
  688.6 12.9 %shard_map.189 = bf16[2,2048,384]{2,1,0:T(8,128)(2,1)} custom-call(bf16[1024,2048]{1,0:T(8,128)(2,1)} %slice_dynamic-update-slice_fusion.10.rows_ref.left_ref, bf16[1024,2048]{1,0:T(8,128)(2,1)} %collective-permute-done.14.rows_ref.left_other_ref, bf16[1024,768]{1,0:T(8,128)(2,1)S(1)} %shard_map.186.right_ref.refs_0_, ...), custom_call_target="tpu_custom_call" | custom-call | flops 6442450 | bytes 14680 | tf_op jit(solution)/shard_map/pallas_call | solution.py:841
  731.2 27.1 %collective-permute-done.88 = bf16[2,128,256]{2,1,0:T(8,128)(2,1)S(1)} collective-permute-done((bf16[2,128,256]{2,1,0:T(8,128)(2,1)S(1)}, bf16[2,128,256]{2,1,0:T(8,128)(2,1)S(1)}, u32[]{:S(2)}, u32[]{:S(2)}) %collective-permute-start.88) | collective-permute-done | bytes 131104 | tf_op jit(solution)/shard_map/ppermute | solution.py:465
  765.8 17.3 %collective-permute-done.78 = bf16[128,2048]{1,0:T(8,128)(2,1)S(1)} collective-permute-done((bf16[128,2048]{1,0:T(8,128)(2,1)S(1)}, bf16[128,2048]{1,0:T(8,128)(2,1)S(1)}, u32[]{:S(2)}, u32[]{:S(2)}) %collective-permute-start.78) | collective-permute-done | bytes 524320 | tf_op jit(solution)/shard_map/ppermute | solution.py:465
  805.1 20.9 %collective-permute-done.83 = bf16[2,512,256]{2,1,0:T(8,128)(2,1)S(1)} collective-permute-done((bf16[2,512,256]{2,1,0:T(8,128)(2,1)S(1)}, bf16[2,512,256]{2,1,0:T(8,128)(2,1)S(1)}, u32[]{:S(2)}, u32[]{:S(2)}) %collective-permute-start.83) | collective-permute-done | bytes 524320 | tf_op jit(solution)/shard_map/ppermute | solution.py:465
  (684 shorter events, 411.5 us)
Async XLA Ops:
  36.9 42.4 %collective-permute-start.4 = (bf16[256,2048]{1,0:T(8,128)(2,1)S(1)}, bf16[256,2048]{1,0:T(8,128)(2,1)S(1)}, u32[]{:S(2)}, u32[]{:S(2)}) collective-permute-start(bf16[256,2048]{1,0:T(8,128)(2,1)S(1)} %fusion.5), channel_id=1, source_target_pairs={{0,2},{2,0},{1,3},{3,1},{4,6},{6,4},{5,7},{7,5},{8,10},{10,8},{9,1... | collective-permute-start | bytes 3145736 | tf_op jit(solution)/shard_map/ppermute | solution.py:465
  38.1 41.2 %collective-permute-start.6 = (bf16[256,2048]{1,0:T(8,128)(2,1)S(1)}, bf16[256,2048]{1,0:T(8,128)(2,1)S(1)}, u32[]{:S(2)}, u32[]{:S(2)}) collective-permute-start(bf16[256,2048]{1,0:T(8,128)(2,1)S(1)} %fusion.5), channel_id=1, source_target_pairs={{0,1},{1,0},{2,3},{3,2},{4,5},{5,4},{6,7},{7,6},{8,9},{9,8},{10,11... | collective-permute-start | bytes 3145736 | tf_op jit(solution)/shard_map/ppermute | solution.py:465
  39.7 38.3 %collective-permute-start.5 = (bf16[1024,384]{1,0:T(8,128)(2,1)S(1)}, bf16[1024,384]{1,0:T(8,128)(2,1)S(1)}, u32[]{:S(2)}, u32[]{:S(2)}) collective-permute-start(bf16[1024,384]{1,0:T(8,128)(2,1)S(1)} %fusion.23), channel_id=1, source_target_pairs={{0,4},{4,0},{1,5},{5,1},{2,6},{6,2},{3,7},{7,3},{8,12},{12,8},{9,1... | collective-permute-start | bytes 2359304 | tf_op jit(solution)/shard_map/ppermute | solution.py:465
  42.7 35.2 %collective-permute-start.7 = (bf16[1024,384]{1,0:T(8,128)(2,1)S(1)}, bf16[1024,384]{1,0:T(8,128)(2,1)S(1)}, u32[]{:S(2)}, u32[]{:S(2)}) collective-permute-start(bf16[1024,384]{1,0:T(8,128)(2,1)S(1)} %fusion.23), channel_id=1, source_target_pairs={{0,16},{16,0},{1,17},{17,1},{2,18},{18,2},{3,19},{19,3},{4,20},{20... | collective-permute-start | bytes 2359304 | tf_op jit(solution)/shard_map/ppermute | solution.py:465
  79.3 35.6 %collective-permute-start.11 = (bf16[1024,384]{1,0:T(8,128)(2,1)S(1)}, bf16[1024,384]{1,0:T(8,128)(2,1)S(1)}, u32[]{:S(2)}, u32[]{:S(2)}) collective-permute-start(bf16[1024,384]{1,0:T(8,128)(2,1)S(1)} %collective-permute-done.5), channel_id=1, source_target_pairs={{0,16},{16,0},{1,17},{17,1},{2,18},{18,2},{3,19},{19,3},{4,20},{20... | collective-permute-start | bytes 2359304 | tf_op jit(solution)/shard_map/ppermute | solution.py:465
  128.9 39.0 %collective-permute-start.15 = (bf16[256,2048]{1,0:T(8,128)(2,1)S(1)}, bf16[256,2048]{1,0:T(8,128)(2,1)}, u32[]{:S(2)}, u32[]{:S(2)}) collective-permute-start(bf16[256,2048]{1,0:T(8,128)(2,1)S(1)} %copy-done.66), channel_id=1, source_target_pairs={{0,2},{2,0},{1,3},{3,1},{4,6},{6,4},{5,7},{7,5},{8,10},{10,8},{9,1... | collective-permute-start | bytes 3145736 | tf_op jit(solution)/shard_map/ppermute | solution.py:465
  130.5 37.3 %collective-permute-start.16 = (bf16[256,2048]{1,0:T(8,128)(2,1)S(1)}, bf16[256,2048]{1,0:T(8,128)(2,1)S(1)}, u32[]{:S(2)}, u32[]{:S(2)}) collective-permute-start(bf16[256,2048]{1,0:T(8,128)(2,1)S(1)} %copy-done.66), channel_id=1, source_target_pairs={{0,1},{1,0},{2,3},{3,2},{4,5},{5,4},{6,7},{7,6},{8,9},{9,8},{10,11... | collective-permute-start | bytes 3145736 | tf_op jit(solution)/shard_map/ppermute | solution.py:465
  131.0 36.8 %collective-permute-start.12 = (bf16[128,1024]{1,0:T(8,128)(2,1)S(1)}, bf16[128,1024]{1,0:T(8,128)(2,1)}, u32[]{:S(2)}, u32[]{:S(2)}) collective-permute-start(bf16[128,1024]{1,0:T(8,128)(2,1)S(1)} %pad_maximum_fusion.39), channel_id=1, source_target_pairs={{0,16},{16,0},{1,17},{17,1},{2,18},{18,2},{3,19},{19,3},{4,20},{20... | collective-permute-start | bytes 786440 | tf_op jit(solution)/shard_map/ppermute | solution.py:465
  200.8 38.1 %collective-permute-start.26 = (bf16[1024,2048]{1,0:T(8,128)(2,1)S(1)}, bf16[1024,2048]{1,0:T(8,128)(2,1)S(1)}, u32[]{:S(2)}, u32[]{:S(2)}) collective-permute-start(bf16[1024,2048]{1,0:T(8,128)(2,1)S(1)} %constant_dynamic-update-slice_fusion.1.grad_ref.right_ref), channel_id=1, source_target_pairs={{0,8},{8,0},{1,9},{9,1},{2,10},{10,2},{3,11},{11,3},{4,12},{12,4},... | collective-permute-start | bytes 12582920 | tf_op jit(solution)/shard_map/ppermute | solution.py:465
  200.9 34.9 %collective-permute-start.22 = (bf16[256,2048]{1,0:T(8,128)(2,1)S(1)}, bf16[256,2048]{1,0:T(8,128)(2,1)S(1)}, u32[]{:S(2)}, u32[]{:S(2)}) collective-permute-start(bf16[256,2048]{1,0:T(8,128)(2,1)S(1)} %get-tuple-element.173), channel_id=1, source_target_pairs={{0,1},{1,0},{2,3},{3,2},{4,5},{5,4},{6,7},{7,6},{8,9},{9,8},{10,11... | collective-permute-start | bytes 3145736 | tf_op jit(solution)/shard_map/ppermute | solution.py:465
  201.4 36.5 %collective-permute-start.23 = (bf16[256,2048]{1,0:T(8,128)(2,1)S(1)}, bf16[256,2048]{1,0:T(8,128)(2,1)S(1)}, u32[]{:S(2)}, u32[]{:S(2)}) collective-permute-start(bf16[256,2048]{1,0:T(8,128)(2,1)S(1)} %get-tuple-element.174), channel_id=1, source_target_pairs={{0,2},{2,0},{1,3},{3,1},{4,6},{6,4},{5,7},{7,5},{8,10},{10,8},{9,1... | collective-permute-start | bytes 3145736 | tf_op jit(solution)/shard_map/ppermute | solution.py:465
  202.1 36.8 %collective-permute-start.25 = (bf16[1024,512]{1,0:T(8,128)(2,1)S(1)}, bf16[1024,512]{1,0:T(8,128)(2,1)S(1)}, u32[]{:S(2)}, u32[]{:S(2)}) collective-permute-start(bf16[1024,512]{1,0:T(8,128)(2,1)S(1)} %copy-done.100), channel_id=1, source_target_pairs={{0,16},{16,0},{1,17},{17,1},{2,18},{18,2},{3,19},{19,3},{4,20},{20... | collective-permute-start | bytes 3145736 | tf_op jit(solution)/shard_map/ppermute | solution.py:465
  269.2 35.4 %collective-permute-start.34 = (bf16[512,1024]{1,0:T(8,128)(2,1)S(1)}, bf16[512,1024]{1,0:T(8,128)(2,1)S(1)}, u32[]{:S(2)}, u32[]{:S(2)}) collective-permute-start(bf16[512,1024]{1,0:T(8,128)(2,1)S(1)} %fusion.20), channel_id=1, source_target_pairs={{0,16},{16,0},{1,17},{17,1},{2,18},{18,2},{3,19},{19,3},{4,20},{20... | collective-permute-start | bytes 3145736 | tf_op jit(solution)/shard_map/ppermute | solution.py:465
  269.8 36.0 %collective-permute-start.32 = (bf16[256,2048]{1,0:T(8,128)(2,1)S(1)}, bf16[256,2048]{1,0:T(8,128)(2,1)S(1)}, u32[]{:S(2)}, u32[]{:S(2)}) collective-permute-start(bf16[256,2048]{1,0:T(8,128)(2,1)S(1)} %multiply_convert_fusion), channel_id=1, source_target_pairs={{0,1},{1,0},{2,3},{3,2},{4,5},{5,4},{6,7},{7,6},{8,9},{9,8},{10,11... | collective-permute-start | bytes 3145736 | tf_op jit(solution)/shard_map/ppermute | solution.py:465
  342.0 35.8 %collective-permute-start.40 = (bf16[1024,512]{1,0:T(8,128)(2,1)S(1)}, bf16[1024,512]{1,0:T(8,128)(2,1)}, u32[]{:S(2)}, u32[]{:S(2)}) collective-permute-start(bf16[1024,512]{1,0:T(8,128)(2,1)S(1)} %copy-done.50), channel_id=1, source_target_pairs={{0,16},{16,0},{1,17},{17,1},{2,18},{18,2},{3,19},{19,3},{4,20},{20... | collective-permute-start | bytes 3145736 | tf_op jit(solution)/shard_map/ppermute | solution.py:465
  543.5 40.1 %collective-permute-start.56 = (bf16[1024,2048]{1,0:T(8,128)(2,1)S(1)}, bf16[1024,2048]{1,0:T(8,128)(2,1)S(1)}, u32[]{:S(2)}, u32[]{:S(2)}) collective-permute-start(bf16[1024,2048]{1,0:T(8,128)(2,1)S(1)} %copy-done.68), channel_id=1, source_target_pairs={{0,8},{8,0},{1,9},{9,1},{2,10},{10,2},{3,11},{11,3},{4,12},{12,4},... | collective-permute-start | bytes 12582920 | tf_op jit(solution)/shard_map/ppermute | solution.py:465
  544.0 36.5 %collective-permute-start.58 = (bf16[256,2048]{1,0:T(8,128)(2,1)S(1)}, bf16[256,2048]{1,0:T(8,128)(2,1)S(1)}, u32[]{:S(2)}, u32[]{:S(2)}) collective-permute-start(bf16[256,2048]{1,0:T(8,128)(2,1)S(1)} %fusion.17), channel_id=1, source_target_pairs={{0,2},{2,0},{1,3},{3,1},{4,6},{6,4},{5,7},{7,5},{8,10},{10,8},{9,1... | collective-permute-start | bytes 3145736 | tf_op jit(solution)/shard_map/ppermute | solution.py:465
  544.1 38.4 %collective-permute-start.59 = (bf16[256,2048]{1,0:T(8,128)(2,1)S(1)}, bf16[256,2048]{1,0:T(8,128)(2,1)S(1)}, u32[]{:S(2)}, u32[]{:S(2)}) collective-permute-start(bf16[256,2048]{1,0:T(8,128)(2,1)S(1)} %fusion.17), channel_id=1, source_target_pairs={{0,1},{1,0},{2,3},{3,2},{4,5},{5,4},{6,7},{7,6},{8,9},{9,8},{10,11... | collective-permute-start | bytes 3145736 | tf_op jit(solution)/shard_map/ppermute | solution.py:465
  545.4 38.1 %collective-permute-start.60 = (bf16[512,512]{1,0:T(8,128)(2,1)S(1)}, bf16[512,512]{1,0:T(8,128)(2,1)S(1)}, u32[]{:S(2)}, u32[]{:S(2)}) collective-permute-start(bf16[512,512]{1,0:T(8,128)(2,1)S(1)} %get-tuple-element.224), channel_id=1, source_target_pairs={{0,4},{4,0},{1,5},{5,1},{2,6},{6,2},{3,7},{7,3},{8,12},{12,8},{9,1... | collective-permute-start | bytes 1572872 | tf_op jit(solution)/shard_map/ppermute | solution.py:465
  612.1 36.7 %collective-permute-start.67 = (bf16[1024,2048]{1,0:T(8,128)(2,1)}, bf16[1024,2048]{1,0:T(8,128)(2,1)S(1)}, u32[]{:S(2)}, u32[]{:S(2)}) collective-permute-start(bf16[1024,2048]{1,0:T(8,128)(2,1)} %constant_dynamic-update-slice_fusion.15.right_ref.grad_ref), channel_id=1, source_target_pairs={{0,8},{8,0},{1,9},{9,1},{2,10},{10,2},{3,11},{11,3},{4,12},{12,4},... | collective-permute-start | bytes 12582920 | tf_op jit(solution)/shard_map/ppermute | solution.py:465
  707.5 51.0 %collective-permute-start.73 = (bf16[128,2048]{1,0:T(8,128)(2,1)}, bf16[128,2048]{1,0:T(8,128)(2,1)S(1)}, u32[]{:S(2)}, u32[]{:S(2)}) collective-permute-start(bf16[128,2048]{1,0:T(8,128)(2,1)} %slice.506), channel_id=1, source_target_pairs={{0,4},{4,0},{1,5},{5,1},{2,6},{6,2},{3,7},{7,3},{8,12},{12,8},{9,1... | collective-permute-start | bytes 1572872 | tf_op jit(solution)/shard_map/ppermute | solution.py:465
  760.9 37.8 %collective-permute-start.91 = (bf16[1024,384]{1,0:T(8,128)(2,1)S(1)}, bf16[1024,384]{1,0:T(8,128)(2,1)S(1)}, u32[]{:S(2)}, u32[]{:S(2)}) collective-permute-start(bf16[1024,384]{1,0:T(8,128)(2,1)S(1)} %fusion.16), channel_id=1, source_target_pairs={{0,4},{4,0},{1,5},{5,1},{2,6},{6,2},{3,7},{7,3},{8,12},{12,8},{9,1... | collective-permute-start | bytes 2359304 | tf_op jit(solution)/shard_map/ppermute | solution.py:465
  763.4 35.3 %collective-permute-start.90 = (bf16[1024,384]{1,0:T(8,128)(2,1)S(1)}, bf16[1024,384]{1,0:T(8,128)(2,1)S(1)}, u32[]{:S(2)}, u32[]{:S(2)}) collective-permute-start(bf16[1024,384]{1,0:T(8,128)(2,1)S(1)} %copy-done.105), channel_id=1, source_target_pairs={{0,16},{16,0},{1,17},{17,1},{2,18},{18,2},{3,19},{19,3},{4,20},{20... | collective-permute-start | bytes 2359304 | tf_op jit(solution)/shard_map/ppermute | solution.py:465
  790.5 36.0 %collective-permute-start.81 = (bf16[512,1024]{1,0:T(8,128)(2,1)S(1)}, bf16[512,1024]{1,0:T(8,128)(2,1)S(1)}, u32[]{:S(2)}, u32[]{:S(2)}) collective-permute-start(bf16[512,1024]{1,0:T(8,128)(2,1)S(1)} %dynamic-slice_convert_fusion), channel_id=1, source_target_pairs={{0,8},{8,0},{1,9},{9,1},{2,10},{10,2},{3,11},{11,3},{4,12},{12,4},... | collective-permute-start | bytes 3145736 | tf_op jit(solution)/shard_map/ppermute | solution.py:465
  (218 other events, 3648.8 us)
